TPU v7x, 128 devices: a whole 4x4x4 slice. The times are simulated.
128 devices in a mesh: lon: 16 (over y_lo, x, core), lat: 8 (over y_hi, z).
Axes of the slice: x: 4, y: 4 (y_hi: 2, y_lo: 2; y = y_hi * 2 + y_lo), z: 4, core: 2. Of those that a mesh axis runs over, the one named last changes fastest.
Arguments:
- u_wind: float32 [16, 2880, 1024], P(None, 'lon', 'lat'), may hold values from -6 to 6
- v_wind: float32 [16, 2880, 1024], P(None, 'lon', 'lat'), may hold values from -6 to 6
- height: float32 [16, 2880, 1024], P(None, 'lon', 'lat'), may hold values from -6 to 6
Outputs:
- u_next: float32 [16, 2880, 1024], P(None, 'lon', 'lat')
- v_next: float32 [16, 2880, 1024], P(None, 'lon', 'lat')
- height_next: float32 [16, 2880, 1024], P(None, 'lon', 'lat')
All inputs are finite; a program needn't handle non-finite values.
Results may differ from a plain program's by a relative error of at most 0.00013.
Values sent between devices are 32-bit elements; how exact they have to be, the bound alone decides.
No kernel may reach another device: no remote copies, remote signals or barrier semaphores. Data moves between devices by JAX's collectives and lax.ppermute only.
A program may use at most 192 MiB of HBM per device.

v0:
```python
import math

import jax
import jax.numpy as jnp
import numpy as np
from jax import lax
from jax.sharding import PartitionSpec as P

grav_zonal = 0.3
grav_merid = 0.6
coriolis = 0.8
divergence_coef = 0.3
diffusion = 0.08


def with_halo(value, sides, width, wrap):
    for axis, dim in sides:
        size, length = (lax.axis_size(axis), value.shape[dim])
        up = [(i, (i + 1) % size) for i in range(size if wrap else size - 1)]
        down = [(j, i) for i, j in up]
        last = lax.slice_in_dim(value, length - width, length, axis=dim)
        initial = lax.slice_in_dim(value, 0, width, axis=dim)
        before = lax.ppermute(last, axis, up)
        after = lax.ppermute(initial, axis, down)
        value = jnp.concatenate([before, value, after], axis=dim)
    return value


def from_behind(block, axis, distance):
    devices = range(lax.axis_size(axis))
    route = [((i - distance) % len(devices), i) for i in devices]
    return lax.ppermute(block, axis, route)


def shifted(field, row_step, col_step, row_count, col_count):
    return field[
        :, 1 + row_step : 1 + row_step + row_count, 1 + col_step : 1 + col_step + col_count
    ]


def stencil(padded, first_row, lat_total):
    row_count = padded.shape[2] - 2
    col_count = padded.shape[3] - 2
    height, u_wind, v_wind = (padded[0], padded[1], padded[2])

    def view(field, row_step, col_step):
        return shifted(field, row_step, col_step, row_count, col_count)

    def laplace(field):
        return (
            view(field, 0, 1)
            + view(field, 0, -1)
            + view(field, 1, 0)
            + view(field, -1, 0)
            - 4.0 * view(field, 0, 0)
        )

    lat_index = (first_row + jnp.arange(row_count)).astype(jnp.float32)[:, None]
    center = (lat_index + 0.5) * (math.pi / lat_total)
    cos_center = jnp.sin(center)
    sin_center = -jnp.cos(center)
    face = (lat_index + 1.0) * (math.pi / lat_total)
    sin_face = -jnp.cos(face)
    cos_face = jnp.where(lat_index + 1.0 < lat_total, jnp.sin(face), 0.0)
    cos_south = jnp.sin(lat_index * (math.pi / lat_total))
    u_next = (
        view(u_wind, 0, 0)
        - grav_zonal * (view(height, 0, 1) - view(height, 0, 0)) / cos_center
        + coriolis
        * sin_center
        * 0.25
        * (view(v_wind, 0, 0) + view(v_wind, 0, 1) + view(v_wind, -1, 0) + view(v_wind, -1, 1))
        + diffusion * laplace(u_wind)
    )
    v_next = (
        view(v_wind, 0, 0)
        - grav_merid * (view(height, 1, 0) - view(height, 0, 0))
        - coriolis
        * sin_face
        * 0.25
        * (view(u_wind, 0, 0) + view(u_wind, 0, -1) + view(u_wind, 1, 0) + view(u_wind, 1, -1))
        + diffusion * laplace(v_wind)
    )
    flux = (
        view(u_wind, 0, 0)
        - view(u_wind, 0, -1)
        + cos_face * view(v_wind, 0, 0)
        - cos_south * view(v_wind, -1, 0)
    )
    height_next = (
        view(height, 0, 0) - divergence_coef * flux / cos_center + diffusion * laplace(height)
    )
    return jnp.stack([height_next, u_next, v_next])


def fourier_tables(lon_total):
    freq_index = np.arange(lon_total)
    is_cosine = freq_index <= lon_total // 2
    wavenum = np.where(is_cosine, freq_index, freq_index - lon_total // 2)
    phase_index = wavenum[:, None] * np.arange(lon_total)[None, :] % lon_total
    angles = phase_index * (2.0 * math.pi / lon_total)
    basis_rows = np.where(is_cosine[:, None], np.cos(angles), np.sin(angles)).astype(np.float32)
    sine_vals = np.sin(wavenum * (math.pi / lon_total))
    sine_sq = (sine_vals * sine_vals).astype(np.float32)
    weight = (
        np.where((freq_index == 0) | (freq_index == lon_total // 2), 1.0, 2.0) / lon_total
    ).astype(np.float32)
    return (basis_rows, sine_sq, weight)


def polar_filter(circles, damp_ratio):
    lon_total = circles.shape[1]
    block_width = lon_total // 8
    basis_table, sine_table, weight_table = fourier_tables(lon_total)
    running = jnp.zeros_like(circles)
    for block_index in range(8):
        first = block_index * block_width
        basis_rows = jnp.asarray(basis_table[first : first + block_width])
        sine_sq = jnp.asarray(sine_table[first : first + block_width])
        weight = jnp.asarray(weight_table[first : first + block_width])
        spectra = jnp.dot(circles, basis_rows.T, precision=lax.Precision.HIGHEST)
        damping = damp_ratio / jnp.maximum(sine_sq[None, :], damp_ratio)
        running = running + jnp.dot(
            spectra * damping * weight[None, :], basis_rows, precision=lax.Precision.HIGHEST
        )
    return running


def shards(u_wind, v_wind, height):
    u_wind = jnp.swapaxes(u_wind, 1, 2)
    v_wind = jnp.swapaxes(v_wind, 1, 2)
    height = jnp.swapaxes(height, 1, 2)
    levels, row_count, col_count = height.shape
    n_lat = lax.axis_size("lat")
    n_lon = lax.axis_size("lon")
    lat_total = row_count * n_lat
    lat_band = lax.axis_index("lat")
    stacked = jnp.stack([height, u_wind, v_wind])
    lon_padded = with_halo(stacked, (("lon", 3),), 1, True)
    both_padded = with_halo(lon_padded, (("lat", 2),), 1, False)
    pole_rows = jnp.concatenate(
        [lon_padded[:, :, 0:1], lon_padded[:, :, row_count - 2 : row_count]], 2
    )
    across_pole = from_behind(pole_rows, "lon", n_lon // 2)
    flip_sign = jnp.array([1.0, -1.0], jnp.float32).reshape(2, 1, 1, 1)
    north_rows = jnp.concatenate(
        [across_pole[0:2, :, 2:3] * flip_sign, -across_pole[2:3, :, 1:2]], 0
    )
    south_rows = jnp.concatenate(
        [across_pole[0:2, :, 0:1] * flip_sign, jnp.zeros_like(across_pole[2:3, :, 0:1])], 0
    )
    lower_rim = jnp.where(lat_band == 0, south_rows, both_padded[:, :, 0:1])
    upper_rim = jnp.where(lat_band == n_lat - 1, north_rows, both_padded[:, :, row_count + 1 :])
    padded = jnp.concatenate([lower_rim, both_padded[:, :, 1 : row_count + 1], upper_rim], 2)
    stepped = stencil(padded, lat_band * row_count, lat_total)
    buffer = stepped.reshape(3, levels * row_count, col_count)
    is_polar = (lat_band < n_lat // 4) | (lat_band >= n_lat - n_lat // 4)
    arrived = lax.all_to_all(buffer, "lon", split_axis=1, concat_axis=2, tiled=True)
    item_count, row_span, lon_span = arrived.shape
    flat_index = 0 + lax.axis_index("lon") * row_span + jnp.arange(row_span, dtype=jnp.int32)
    lat_row = lat_band * row_count + flat_index % row_count
    cosine = jnp.sin((lat_row.astype(jnp.float32) + 0.5) * (math.pi / lat_total))
    damp_ratio = (2.0 * cosine * cosine)[:, None]
    smoothed = polar_filter(
        arrived.reshape(item_count * row_span, lon_span), jnp.tile(damp_ratio, (item_count, 1))
    )
    smoothed = lax.all_to_all(
        smoothed.reshape(item_count, row_span, lon_span),
        "lon",
        split_axis=2,
        concat_axis=1,
        tiled=True,
    )
    result = jnp.where(is_polar, smoothed, buffer)
    result = result.reshape(3, levels, row_count, col_count)
    return (
        jnp.swapaxes(result[1], 1, 2),
        jnp.swapaxes(result[2], 1, 2),
        jnp.swapaxes(result[0], 1, 2),
    )


def solution(mesh):
    placed = (P(None, "lon", "lat"), P(None, "lon", "lat"), P(None, "lon", "lat"))
    return jax.shard_map(
        shards,
        mesh=mesh,
        in_specs=placed,
        out_specs=(P(None, "lon", "lat"), P(None, "lon", "lat"), P(None, "lon", "lat")),
        check_vma=False,
    )
```

profile of v0, /device:TPU:19, one launch (start us, length us, event | category | flops | bytes accessed | tf_op | source)
XLA Modules:
  0.0 506.7 jit_solution(7954118842381399572)
XLA Ops:
  54.8 8.3 %pad_maximum_fusion = f32[3,16,130,182]{2,1,3,0:T(8,128)S(1)} fusion(f32[3,16,1,182]{2,1,3,0:T(8,128)S(1)} %broadcast_select_fusion.1, f32[3,16,128,1]{2,1,3,0:T(8,128)S(1)} %collective-permute-done.1, f32[1,16,128,180]{2,1,3,0:T(8,128)S(1)} %bitcast.160, f32[1,16,128,180]{2,1,3,0:T(8,128)S(1)} %bitcast.163, f32[1,16,128,180]{2,1,3,0:T(8,128)S(1)} %bitcast.166, ...), kind=kLoop, calls=%fused_computation | loop fusion | flops 6814080 | bytes 9085440 | tf_op jit(solution)/shard_map/concatenate | solution.py:154
  74.0 8.3 %fusion.24 = f32[16,128,180]{1,0,2:T(8,128)} fusion(f32[16,130,182]{1,0,2:T(8,128)S(1)} %get-tuple-element.3, f32[16,130,182]{1,0,2:T(8,128)} %copy-done, f32[16,130,182]{1,0,2:T(8,128)} %copy-done.1, f32[128]{0:T(128)S(1)} %copy-done.17, f32[128]{0:T(128)S(1)} %get-tuple-element.22), kind=kLoop, calls=%fused_computation.46 | loop fusion | flops 5898240 | bytes 17695744 | tf_op jit(solution)/shard_map/add | solution.py:67
  84.8 9.0 %fusion.30 = f32[16,128,180]{1,0,2:T(8,128)} fusion(f32[16,130,182]{1,0,2:T(8,128)} %copy-done.1, f32[16,130,182]{1,0,2:T(8,128)} %copy-done, f32[16,130,182]{1,0,2:T(8,128)S(1)} %get-tuple-element.3, f32[128]{0:T(128)S(1)} %get-tuple-element.22, f32[128]{0:T(128)S(1)} %get-tuple-element.21, f32[128]{0:T(128)S(1)} %get-tuple-element.17), kind=kLoop, calls=%fused_computation.55 | loop fusion | flops 5529600 | bytes 14747136 | tf_op jit(solution)/shard_map/add | solution.py:91
  101.7 8.4 %copy.73 = f32[3,2048,180]{2,0,1:T(4,128)} copy(f32[3,2048,180]{1,2,0:T(8,128)} %constant_dynamic-update-slice_fusion) | data formatting | bytes 8847360 | tf_op jit(solution)/shard_map/stack | solution.py:93
  116.8 113.2 %all-to-all-done = f32[3,2048,180]{2,0,1:T(4,128)} async-done(((f32[3,2048,180]{2,0,1:T(4,128)}), f32[3,2048,180]{2,0,1:T(4,128)}, u32[]{:S(2)}, u32[]{:S(2)}) %all-to-all-start) | async-done | bytes 4423712 | tf_op jit(solution)/shard_map/all_to_all | solution.py:158
  230.0 11.6 %copy.74 = f32[3,16,128,180]{2,0,3,1:T(4,128)} copy(f32[3,16,128,180]{3,0,2,1:T(4,128)} %bitcast.9) | data formatting | bytes 8847360 | tf_op jit(solution)/shard_map/all_to_all | solution.py:158
  245.1 10.2 %fusion.35 = f32[384,360]{0,1:T(8,128)S(1)} fusion(f32[360,2880]{1,0:T(8,128)} %constant.92.clone, f32[360,8,3,128]{3,1,2,0:T(8,128)S(1)} %copy.81, f32[360]{0:T(512)S(1)} %copy-done.10, f32[360]{0:T(512)S(1)} %copy-done.15, f32[384]{0:T(512)S(1)} %broadcast_bitcast_fusion), kind=kOutput, calls=%fused_computation.59 | convolution fusion | flops 4778127360 | bytes 9128256 | tf_op jit(solution)/shard_map/dot_general | solution.py:121
  255.3 9.8 %fusion.90 = f32[384,2880]{0,1:T(8,128)S(1)} fusion(f32[384,360]{0,1:T(8,128)S(1)} %fusion.35, f32[360,2880]{1,0:T(8,128)S(1)} %bitcast.157), kind=kOutput, calls=%fused_computation.111 | convolution fusion | flops 4777574400 | bytes 9123840 | tf_op jit(solution)/shard_map/dot_general | solution.py:123
  265.1 7.4 %fusion.41 = f32[384,360]{0,1:T(8,128)S(1)} fusion(f32[360,2880]{1,0:T(8,128)S(1)} %bitcast.150, f32[360,8,3,128]{3,1,2,0:T(8,128)S(1)} %copy.81, f32[360]{0:T(512)S(1)} %copy-done.11, f32[384]{0:T(512)S(1)} %broadcast_bitcast_fusion), kind=kOutput, calls=%fused_computation.61 | convolution fusion | flops 4778127360 | bytes 9126816 | tf_op jit(solution)/shard_map/dot_general | solution.py:121
  272.6 8.1 %fusion.65 = f32[384,360]{0,1:T(8,128)} fusion(f32[360,2880]{1,0:T(8,128)S(1)} %bitcast.144, f32[360,8,3,128]{3,1,2,0:T(8,128)S(1)} %copy.81, f32[360]{0:T(512)S(1)} %copy-done.11, f32[384]{0:T(512)S(1)} %broadcast_bitcast_fusion), kind=kOutput, calls=%fused_computation.69 | convolution fusion | flops 4778127360 | bytes 9126816 | tf_op jit(solution)/shard_map/dot_general | solution.py:121
  280.8 8.6 %fusion.47 = f32[384,360]{0,1:T(8,128)} fusion(f32[360,2880]{1,0:T(8,128)S(1)} %bitcast.148, f32[360,8,3,128]{3,1,2,0:T(8,128)S(1)} %copy.81, f32[360]{0:T(512)S(1)} %copy-done.12, f32[384]{0:T(512)S(1)} %broadcast_bitcast_fusion), kind=kOutput, calls=%fused_computation.63 | convolution fusion | flops 4778127360 | bytes 9126816 | tf_op jit(solution)/shard_map/dot_general | solution.py:121
  289.4 7.3 %fusion.71 = f32[384,360]{0,1:T(8,128)S(1)} fusion(f32[360,2880]{1,0:T(8,128)S(1)} %bitcast.142, f32[360,8,3,128]{3,1,2,0:T(8,128)S(1)} %copy.81, f32[360]{0:T(512)S(1)} %copy-done.12, f32[384]{0:T(512)S(1)} %broadcast_bitcast_fusion), kind=kOutput, calls=%fused_computation.71 | convolution fusion | flops 4778127360 | bytes 9126816 | tf_op jit(solution)/shard_map/dot_general | solution.py:121
  296.8 7.5 %fusion.53 = f32[384,360]{0,1:T(8,128)S(1)} fusion(f32[360,2880]{1,0:T(8,128)S(1)} %bitcast.146, f32[360,8,3,128]{3,1,2,0:T(8,128)S(1)} %copy.81, f32[360]{0:T(512)S(1)} %copy-done.13, f32[384]{0:T(512)S(1)} %broadcast_bitcast_fusion), kind=kOutput, calls=%fused_computation.65 | convolution fusion | flops 4778127360 | bytes 9126816 | tf_op jit(solution)/shard_map/dot_general | solution.py:121
  304.3 7.6 %fusion.77 = f32[384,360]{0,1:T(8,128)S(1)} fusion(f32[360,2880]{1,0:T(8,128)S(1)} %bitcast.140, f32[360,8,3,128]{3,1,2,0:T(8,128)S(1)} %copy.81, f32[360]{0:T(512)S(1)} %copy-done.13, f32[384]{0:T(512)S(1)} %broadcast_bitcast_fusion), kind=kOutput, calls=%fused_computation.73 | convolution fusion | flops 4778127360 | bytes 9126816 | tf_op jit(solution)/shard_map/dot_general | solution.py:121
  311.9 9.6 %convolution_add_fusion.6 = f32[384,2880]{0,1:T(8,128)S(1)} fusion(f32[384,2880]{0,1:T(8,128)S(1)} %fusion.90, f32[384,360]{0,1:T(8,128)S(1)} %fusion.41, f32[360,2880]{1,0:T(8,128)S(1)} %bitcast.150), kind=kOutput, calls=%fused_computation.7 | convolution fusion | flops 4778680320 | bytes 13547520 | tf_op jit(solution)/shard_map/dot_general | solution.py:123
  321.5 10.2 %convolution_add_fusion.5 = f32[384,2880]{0,1:T(8,128)S(1)} fusion(f32[384,2880]{0,1:T(8,128)S(1)} %convolution_add_fusion.6, f32[384,360]{0,1:T(8,128)S(1)} %copy-done.9, f32[360,2880]{1,0:T(8,128)S(1)} %bitcast.148), kind=kOutput, calls=%fused_computation.6 | convolution fusion | flops 4778680320 | bytes 13547520 | tf_op jit(solution)/shard_map/dot_general | solution.py:123
  331.7 9.9 %convolution_add_fusion.4 = f32[384,2880]{0,1:T(8,128)S(1)} fusion(f32[384,2880]{0,1:T(8,128)S(1)} %convolution_add_fusion.5, f32[384,360]{0,1:T(8,128)S(1)} %fusion.53, f32[360,2880]{1,0:T(8,128)S(1)} %bitcast.146), kind=kOutput, calls=%fused_computation.5 | convolution fusion | flops 4778680320 | bytes 13547520 | tf_op jit(solution)/shard_map/dot_general | solution.py:123
  341.6 7.4 %fusion.59 = f32[384,360]{0,1:T(8,128)S(1)} fusion(f32[360,2880]{1,0:T(8,128)S(1)} %bitcast.152, f32[360,8,3,128]{3,1,2,0:T(8,128)S(1)} %copy.81, f32[360]{0:T(512)S(1)} %copy-done.14, f32[360]{0:T(512)S(1)} %copy-done.10, f32[384]{0:T(512)S(1)} %broadcast_bitcast_fusion), kind=kOutput, calls=%fused_computation.67 | convolution fusion | flops 4778127360 | bytes 9128256 | tf_op jit(solution)/shard_map/dot_general | solution.py:121
  349.1 9.6 %convolution_add_fusion.3 = f32[384,2880]{0,1:T(8,128)S(1)} fusion(f32[384,2880]{0,1:T(8,128)S(1)} %convolution_add_fusion.4, f32[384,360]{0,1:T(8,128)S(1)} %fusion.59, f32[360,2880]{1,0:T(8,128)S(1)} %bitcast.152), kind=kOutput, calls=%fused_computation.4 | convolution fusion | flops 4778680320 | bytes 13547520 | tf_op jit(solution)/shard_map/dot_general | solution.py:123
  358.7 10.2 %convolution_add_fusion.2 = f32[384,2880]{0,1:T(8,128)S(1)} fusion(f32[384,2880]{0,1:T(8,128)S(1)} %convolution_add_fusion.3, f32[384,360]{0,1:T(8,128)S(1)} %copy-done.8, f32[360,2880]{1,0:T(8,128)S(1)} %bitcast.144), kind=kOutput, calls=%fused_computation.3 | convolution fusion | flops 4778680320 | bytes 13547520 | tf_op jit(solution)/shard_map/dot_general | solution.py:123
  368.8 9.5 %convolution_add_fusion.1 = f32[384,2880]{0,1:T(8,128)S(1)} fusion(f32[384,2880]{0,1:T(8,128)S(1)} %convolution_add_fusion.2, f32[384,360]{0,1:T(8,128)S(1)} %fusion.71, f32[360,2880]{1,0:T(8,128)S(1)} %bitcast.142), kind=kOutput, calls=%fused_computation.2 | convolution fusion | flops 4778680320 | bytes 13547520 | tf_op jit(solution)/shard_map/dot_general | solution.py:123
  378.4 11.7 %convolution_add_fusion = f32[384,2880]{0,1:T(8,128)} fusion(f32[384,2880]{0,1:T(8,128)S(1)} %convolution_add_fusion.1, f32[384,360]{0,1:T(8,128)S(1)} %fusion.77, f32[360,2880]{1,0:T(8,128)S(1)} %bitcast.140), kind=kOutput, calls=%fused_computation.1 | convolution fusion | flops 4778680320 | bytes 13547520 | tf_op jit(solution)/shard_map/dot_general | solution.py:123
  396.0 6.8 %copy.76 = f32[3,128,2880]{1,0,2:T(4,128)} copy(f32[3,128,2880]{2,1,0:T(8,128)} %bitcast.154) | data formatting | bytes 8847360 | tf_op jit(solution)/shard_map/reshape | solution.py:168
  407.3 79.5 %all-to-all-done.1 = f32[3,128,2880]{1,0,2:T(4,128)} async-done(((f32[3,128,2880]{1,0,2:T(4,128)}), f32[3,128,2880]{1,0,2:T(4,128)}, u32[]{:S(2)}, u32[]{:S(2)}) %all-to-all-start.1) | async-done | bytes 4423712 | tf_op jit(solution)/shard_map/all_to_all | solution.py:167
  (129 shorter events, 115.6 us)
Async XLA Ops:
  1.6 2.7 collective-permute-start
  3.4 3.3 collective-permute-start.1
  23.8 13.2 %collective-permute-start.4 = (f32[3,16,1,182]{3,1,2,0:T(8,128)S(1)}, f32[3,16,1,182]{3,1,2,0:T(8,128)S(1)}, u32[]{:S(2)}, u32[]{:S(2)}) collective-permute-start(f32[3,16,1,182]{3,1,2,0:T(8,128)S(1)} %copy.66), channel_id=1, source_target_pairs={{1,0},{2,1},{3,2},{4,3},{5,4},{6,5},{7,6},{9,8},{10,9},{11,10},{12... | collective-permute-start | bytes 104840 | tf_op jit(solution)/shard_map/ppermute | solution.py:24
  29.3 11.1 %collective-permute-start.2 = (f32[3,16,3,182]{3,1,2,0:T(8,128)S(1)}, f32[3,16,3,182]{3,1,2,0:T(8,128)S(1)}, u32[]{:S(2)}, u32[]{:S(2)}) collective-permute-start(f32[3,16,3,182]{3,1,2,0:T(8,128)S(1)} %pad_maximum_fusion.2), channel_id=1, source_target_pairs={{64,0},{72,8},{80,16},{88,24},{96,32},{104,40},{112,48},{120,56},{... | collective-permute-start | bytes 314504 | tf_op jit(solution)/shard_map/ppermute | solution.py:32
  34.9 9.1 %collective-permute-start.3 = (f32[3,16,1,182]{3,1,2,0:T(8,128)S(1)}, f32[3,16,1,182]{3,1,2,0:T(8,128)S(1)}, u32[]{:S(2)}, u32[]{:S(2)}) collective-permute-start(f32[3,16,1,182]{3,1,2,0:T(8,128)S(1)} %copy.68), channel_id=1, source_target_pairs={{0,1},{1,2},{2,3},{3,4},{4,5},{5,6},{6,7},{8,9},{9,10},{10,11},{11... | collective-permute-start | bytes 104840 | tf_op jit(solution)/shard_map/ppermute | solution.py:23
  110.1 119.9 %all-to-all-start = ((f32[3,2048,180]{2,0,1:T(4,128)}), f32[3,2048,180]{2,0,1:T(4,128)}, u32[]{:S(2)}, u32[]{:S(2)}) async-start(f32[3,2048,180]{2,0,1:T(4,128)} %copy.73), calls=%async_computation | async-start | bytes 16777216 | tf_op jit(solution)/shard_map/all_to_all | solution.py:158
  241.6 13.6 %slice-start.14 = ((s8[4239360]{0:T(1024)(128)(4,1)}), s8[4194304]{0:T(1024)(128)(4,1)S(1)}, s32[]{:S(2)}) async-start(s8[4239360]{0:T(1024)(128)(4,1)} %bitcast.156), calls=%async_computation.16 | async-start | bytes 8388608
  241.6 23.4 %slice-start.10 = ((s8[4239360]{0:T(1024)(128)(4,1)}), s8[4194304]{0:T(1024)(128)(4,1)S(1)}, s32[]{:S(2)}) async-start(s8[4239360]{0:T(1024)(128)(4,1)} %bitcast.149), calls=%async_computation.12 | async-start | bytes 8388608
  245.0 10.2 %slice-start.15 = ((s8[4239360]{0:T(1024)(128)(4,1)}), s8[45056]{0:T(1024)(128)(4,1)S(1)}, s32[]{:S(2)}) async-start(s8[4239360]{0:T(1024)(128)(4,1)} %bitcast.156), calls=%async_computation.17 | async-start | bytes 90112
  245.0 20.0 %slice-start.11 = ((s8[4239360]{0:T(1024)(128)(4,1)}), s8[45056]{0:T(1024)(128)(4,1)S(1)}, s32[]{:S(2)}) async-start(s8[4239360]{0:T(1024)(128)(4,1)} %bitcast.149), calls=%async_computation.13 | async-start | bytes 90112
  255.3 9.8 %copy-start.11 = (f32[360]{0:T(512)S(1)}, f32[360]{0:T(512)}, u32[]{:S(2)}) copy-start(f32[360]{0:T(512)} %constant.96.clone) | copy-start | bytes 4324
  255.3 17.3 %slice-start.4 = ((s8[4239360]{0:T(1024)(128)(4,1)}), s8[4194304]{0:T(1024)(128)(4,1)S(1)}, s32[]{:S(2)}) async-start(s8[4239360]{0:T(1024)(128)(4,1)} %bitcast.143), calls=%async_computation.6 | async-start | bytes 8388608
  255.3 25.5 %slice-start.8 = ((s8[4239360]{0:T(1024)(128)(4,1)}), s8[4194304]{0:T(1024)(128)(4,1)S(1)}, s32[]{:S(2)}) async-start(s8[4239360]{0:T(1024)(128)(4,1)} %bitcast.147), calls=%async_computation.10 | async-start | bytes 8388608
  265.1 15.6 %slice-start.9 = ((s8[4239360]{0:T(1024)(128)(4,1)}), s8[45056]{0:T(1024)(128)(4,1)S(1)}, s32[]{:S(2)}) async-start(s8[4239360]{0:T(1024)(128)(4,1)} %bitcast.147), calls=%async_computation.11 | async-start | bytes 90112
  272.6 16.7 %slice-start.2 = ((s8[4239360]{0:T(1024)(128)(4,1)}), s8[4194304]{0:T(1024)(128)(4,1)S(1)}, s32[]{:S(2)}) async-start(s8[4239360]{0:T(1024)(128)(4,1)} %bitcast.141), calls=%async_computation.4 | async-start | bytes 8388608
  272.6 24.1 %slice-start.6 = ((s8[4239360]{0:T(1024)(128)(4,1)}), s8[4194304]{0:T(1024)(128)(4,1)S(1)}, s32[]{:S(2)}) async-start(s8[4239360]{0:T(1024)(128)(4,1)} %bitcast.145), calls=%async_computation.8 | async-start | bytes 8388608
  280.8 16.0 %slice-start.7 = ((s8[4239360]{0:T(1024)(128)(4,1)}), s8[45056]{0:T(1024)(128)(4,1)S(1)}, s32[]{:S(2)}) async-start(s8[4239360]{0:T(1024)(128)(4,1)} %bitcast.145), calls=%async_computation.9 | async-start | bytes 90112
  289.4 14.9 %slice-start = ((s8[4239360]{0:T(1024)(128)(4,1)}), s8[4194304]{0:T(1024)(128)(4,1)S(1)}, s32[]{:S(2)}) async-start(s8[4239360]{0:T(1024)(128)(4,1)} %bitcast.139), calls=%async_computation.2 | async-start | bytes 8388608
  311.9 9.6 %copy-start.9 = (f32[384,360]{0,1:T(8,128)S(1)}, f32[384,360]{0,1:T(8,128)}, u32[]{:S(2)}) copy-start(f32[384,360]{0,1:T(8,128)} %fusion.47) | copy-start | bytes 1658884
  321.4 20.2 %slice-start.12 = ((s8[4239360]{0:T(1024)(128)(4,1)}), s8[45056]{0:T(1024)(128)(4,1)S(1)}, s32[]{:S(2)}) async-start(s8[4239360]{0:T(1024)(128)(4,1)} %bitcast.151), calls=%async_computation.14 | async-start | bytes 90112
  331.6 10.0 %slice-start.13 = ((s8[4239360]{0:T(1024)(128)(4,1)}), s8[4194304]{0:T(1024)(128)(4,1)S(1)}, s32[]{:S(2)}) async-start(s8[4239360]{0:T(1024)(128)(4,1)} %bitcast.151), calls=%async_computation.15 | async-start | bytes 8388608
  331.6 10.0 %copy-start.14 = (f32[360]{0:T(512)S(1)}, f32[360]{0:T(512)}, u32[]{:S(2)}) copy-start(f32[360]{0:T(512)} %constant.103.clone) | copy-start | bytes 4324
  349.1 9.6 %copy-start.8 = (f32[384,360]{0,1:T(8,128)S(1)}, f32[384,360]{0,1:T(8,128)}, u32[]{:S(2)}) copy-start(f32[384,360]{0,1:T(8,128)} %fusion.65) | copy-start | bytes 1658884
  402.8 84.1 %all-to-all-start.1 = ((f32[3,128,2880]{1,0,2:T(4,128)}), f32[3,128,2880]{1,0,2:T(4,128)}, u32[]{:S(2)}, u32[]{:S(2)}) async-start(f32[3,128,2880]{1,0,2:T(4,128)} %copy.76), calls=%async_computation.1 | async-start | bytes 11796480 | tf_op jit(solution)/shard_map/all_to_all | solution.py:167
  (18 other events, 101.8 us)
where the time goes:
time: 513 us; the launch traced here: 507 us
  waiting for transfers between devices  199 us (39%)
  matrix products  144 us (28%)
  local copies, waits for them, and re-layouts  99.2 us (19%)
  other arithmetic  39.9 us (8%)
  starting transfers between devices  22.5 us (4%)
    all_to_all x1, waiting for transfers between devices, shards(): lax.all_to_all(buffer, 'lon', split_axis=1, concat_axis=2, tiled=True)  113 us
    dot_general x8, matrix products, polar_filter(): jnp.dot(spectra * damping * weight[None, :], basis_rows, precision=lax.Pr...  80.4 us
    all_to_all x1, waiting for transfers between devices, shards(): lax.all_to_all(smoothed.reshape(item_count, row_span, lon_span), 'lon', s...  79.5 us
    dot_general x8, matrix products, polar_filter(): spectra = jnp.dot(circles, basis_rows.T, precision=lax.Precision.HIGHEST)  64.1 us
    another operation x5, local copies, waits for them, and re-layouts, stencil(): return jnp.stack([height_next, u_next, v_next])  17.5 us
    unnamed x76, local copies, waits for them, and re-layouts  11.8 us
    all_to_all x2, local copies, waits for them, and re-layouts, shards(): lax.all_to_all(smoothed.reshape(item_count, row_span, lon_span), 'lon', s...  11.7 us
    all_to_all x1, local copies, waits for them, and re-layouts, shards(): lax.all_to_all(buffer, 'lon', split_axis=1, concat_axis=2, tiled=True)  11.6 us
  transfers between devices with their start and end apart: 7, of which 5 were waited for; matrix products, arithmetic and copies ran while one was open for 2% of the time, Pallas kernels for 0%

commit v1 on v0

v1 whole, which is shorter than its diff:
```python
import functools
import math

import jax
import jax.numpy as jnp
import numpy as np
from jax import lax
from jax.experimental import pallas as pl
from jax.experimental.pallas import tpu as pltpu
from jax.sharding import PartitionSpec as P

N_LON = 16
N_LAT = 8
LEV = 16
COLS = 180
ROWS = 128
NLON = N_LON * COLS
NLAT = N_LAT * ROWS
HALF = 192
TOP = 8
TALL = 200
STEP = 4
AXES = ("lon", "lat")

GRAV_ZONAL = 0.3
GRAV_MERID = 0.6
CORIOLIS = 0.8
DIVERGENCE = 0.3
DIFFUSION = 0.08


def latitude_tables():
    f32 = np.float32
    index = np.arange(NLAT).astype(f32)
    step = f32(math.pi / NLAT)

    def sine(angle):
        return np.sin(angle.astype(np.float64)).astype(f32)

    def cosine(angle):
        return np.cos(angle.astype(np.float64)).astype(f32)

    center = (index + f32(0.5)) * step
    face = (index + f32(1.0)) * step
    cos_center = sine(center)
    sin_center = -cosine(center)
    sin_face = -cosine(face)
    cos_face = np.where(index + 1 < NLAT, sine(face), f32(0.0))
    cos_south = sine(index * step)
    ratio = f32(2.0) * cos_center * cos_center
    table = np.stack(
        [
            GRAV_ZONAL / cos_center.astype(np.float64),
            CORIOLIS * 0.25 * sin_center.astype(np.float64),
            CORIOLIS * 0.25 * sin_face.astype(np.float64),
            cos_face,
            cos_south,
            ratio,
            DIVERGENCE / cos_center.astype(np.float64),
            np.zeros(NLAT),
        ]
    ).astype(f32)
    return np.ascontiguousarray(table.reshape(8, N_LAT, ROWS).transpose(1, 0, 2))


def split(value):
    high = value.astype(jnp.bfloat16)
    return high, (value - high.astype(value.dtype)).astype(jnp.bfloat16)


@functools.cache
def fourier_tables():
    forward = np.zeros((8, 2 * HALF, 2 * HALF))
    inverse = np.zeros((8, 2 * HALF, 2 * HALF))
    wave = np.zeros((8, 2 * HALF), np.int64)
    m = np.arange(COLS)
    first = slice(0, COLS)
    second = slice(HALF, HALF + COLS)

    def angle(k):
        return (k[:, None] * m[None, :] % NLON) * (2.0 * math.pi / NLON)

    for q in range(1, 8):
        k = q + 16 * np.arange(COLS)
        cos, sin = np.cos(angle(k)), np.sin(angle(k))
        forward[q, first, first] = cos
        forward[q, first, second] = sin
        forward[q, second, first] = -sin
        forward[q, second, second] = cos
        wave[q, first] = wave[q, second] = k
        inverse[q] = forward[q].T * (2.0 / NLON)
    k_cos, k_sin = 16 * np.arange(91), 16 * np.arange(1, 90)
    forward[0, first, first] = np.concatenate([np.cos(angle(k_cos)), np.sin(angle(k_sin))])
    wave[0, first] = np.concatenate([k_cos, k_sin])
    k_both = 8 + 16 * np.arange(90)
    forward[0, second, second] = np.concatenate([np.cos(angle(k_both)), np.sin(angle(k_both))])
    wave[0, second] = np.concatenate([k_both, k_both])
    weight = np.where((wave[0] == 0) | (wave[0] == NLON // 2), 1.0, 2.0) / NLON
    inverse[0] = (forward[0] * weight[:, None]).T
    wave = np.minimum(wave, NLON - wave)
    sine = np.sin((wave.astype(np.float32) * np.float32(math.pi / NLON)).astype(np.float64))
    sine_sq = (sine.astype(np.float32) * sine.astype(np.float32)).astype(np.float64)
    over = np.where(wave == 0, 1e30, 1.0 / np.where(wave == 0, 1.0, sine_sq)).astype(np.float32)

    def halves(matrix):
        matrix = matrix.astype(np.float32)
        high = matrix.astype(jnp.bfloat16)
        low = (matrix - high.astype(np.float32)).astype(jnp.bfloat16)
        return np.concatenate([high, low], axis=1)

    over = np.ascontiguousarray(np.broadcast_to(over[:, :, None], (8, 2 * HALF, ROWS)))
    return halves(forward), halves(inverse), over


SIN = [math.sin(math.pi * t / 8) for t in range(5)]


def times(value, c, s):
    re, im = value
    return (c * re - s * im, c * im + s * re)


def forward16(x):
    e = [x[p] + x[p + 8] for p in range(8)]
    o = [x[p] - x[p + 8] for p in range(8)]
    e2 = [e[p] + e[p + 4] for p in range(4)]
    o2 = [e[p] - e[p + 4] for p in range(4)]
    a, b = e2[0] + e2[2], e2[1] + e2[3]
    pairs = [None] * 8
    pairs[0] = (a + b, a - b)
    pairs[4] = (e2[0] - e2[2], e2[3] - e2[1])
    root = SIN[2]
    u = (o2[0], -o2[2])
    w = times((o2[1], -o2[3]), root, -root)
    pairs[2] = (u[0] + w[0], u[1] + w[1])
    pairs[6] = (u[0] - w[0], w[1] - u[1])
    d = [times((o[p], -o[p + 4]), SIN[4 - p], -SIN[p]) if p else (o[p], -o[p + 4]) for p in range(4)]
    s02 = (d[0][0] + d[2][0], d[0][1] + d[2][1])
    t02 = (d[0][0] - d[2][0], d[0][1] - d[2][1])
    s13 = (d[1][0] + d[3][0], d[1][1] + d[3][1])
    t13 = (d[1][0] - d[3][0], d[1][1] - d[3][1])
    pairs[1] = (s02[0] + s13[0], s02[1] + s13[1])
    pairs[7] = (s02[0] - s13[0], s13[1] - s02[1])
    pairs[5] = (t02[0] + t13[1], t02[1] - t13[0])
    pairs[3] = (t02[0] - t13[1], -(t02[1] + t13[0]))
    return pairs


def inverse16(pairs):
    z0, z8 = pairs[0]
    a, b = z0 + z8, z0 - z8
    e2 = [a + pairs[4][0], b - pairs[4][1], a - pairs[4][0], b + pairs[4][1]]
    u, v = pairs[2], (pairs[6][0], -pairs[6][1])
    d0 = (u[0] + v[0], u[1] + v[1])
    root = SIN[2]
    d1 = times((u[0] - v[0], u[1] - v[1]), root, root)
    o2 = [d0[0], d1[0], -d0[1], -d1[1]]
    e = [e2[p] + o2[p] for p in range(4)] + [e2[p] - o2[p] for p in range(4)]
    a1, a5 = pairs[1], pairs[5]
    a9, a13 = (pairs[7][0], -pairs[7][1]), (pairs[3][0], -pairs[3][1])
    s19 = (a1[0] + a9[0], a1[1] + a9[1])
    t19 = (a1[0] - a9[0], a1[1] - a9[1])
    s5 = (a5[0] + a13[0], a5[1] + a13[1])
    t5 = (a5[0] - a13[0], a5[1] - a13[1])
    d = [
        (s19[0] + s5[0], s19[1] + s5[1]),
        (t19[0] - t5[1], t19[1] + t5[0]),
        (s19[0] - s5[0], s19[1] - s5[1]),
        (t19[0] + t5[1], t19[1] - t5[0]),
    ]
    d = [times(d[p], SIN[4 - p], SIN[p]) if p else d[p] for p in range(4)]
    o = [d[p][0] for p in range(4)] + [-d[p][1] for p in range(4)]
    return [e[p] + o[p] for p in range(8)] + [e[p] - o[p] for p in range(8)]


def pack_kernel(h, u, v, west, east, low, high):
    step = pl.program_id(0)

    @pl.when(step == 0)
    def _():
        low[...] = jnp.zeros_like(low)
        high[...] = jnp.zeros_like(high)

    parts = (
        (pl.ds(TOP, COLS), lambda field, f, i, level: field[i]),
        (pl.ds(TOP - 1, 1), lambda field, f, i, level: west[f, pl.ds(level, 1), :]),
        (pl.ds(TOP + COLS, 1), lambda field, f, i, level: east[f, pl.ds(level, 1), :]),
    )
    for rows, read in parts:
        south, north = low[rows, :], high[rows, :]
        lane = lax.broadcasted_iota(jnp.int32, south.shape, 1)
        for i in range(STEP):
            level = step * STEP + i
            for f, field in enumerate((h, u, v)):
                block = read(field, f, i, level)
                spot = 16 * f + level
                south = jnp.where(lane == spot, pltpu.roll(block, spot, 1), south)
                north = jnp.where(lane == spot, pltpu.roll(block, spot + 1, 1), north)
                if f == 2:
                    north = jnp.where(
                        lane == spot + 16, pltpu.roll(block, spot + 18, 1), north
                    )
        low[rows, :] = south
        high[rows, :] = north


def pack(height, u_wind, v_wind, west, east):
    field = pl.BlockSpec((STEP, COLS, ROWS), lambda i: (i, 0, 0))
    side = pl.BlockSpec((3, LEV, ROWS), lambda i: (0, 0, 0))
    edge = pl.BlockSpec((TALL, ROWS), lambda i: (0, 0))
    shape = jax.ShapeDtypeStruct((TALL, ROWS), jnp.float32)
    return pl.pallas_call(
        pack_kernel,
        grid=(LEV // STEP,),
        in_specs=[field, field, field, side, side],
        out_specs=[edge, edge],
        out_shape=[shape, shape],
        cost_estimate=pl.CostEstimate(flops=0, bytes_accessed=4_700_000, transcendentals=0),
    )(height, u_wind, v_wind, west, east)


def stencil_kernel(
    place, h, u, v, west, east, above, below, across, table, uv_out, h_out, e, rim, t_sum, w_sum
):
    step = pl.program_id(0)
    at_north, at_south = place[1] == 1, place[2] == 1
    lane = lax.broadcasted_iota(jnp.int32, (TALL, ROWS), 1)

    @pl.when(step == 0)
    def _():
        turned = across[...]
        rim[0] = jnp.where(at_north, jnp.where(lane < 16, turned, -turned), above[...])
        south = jnp.where(lane < 16, turned, jnp.where(lane < 32, -turned, 0.0))
        rim[1] = jnp.where(at_south, south, below[...])

    zonal, turn_u, turn_v, cos_face, cos_south, _, diverge = (
        table[0, i : i + 1, :] for i in range(7)
    )
    here, to_west, to_east = (pl.ds(TOP + i, 184) for i in (0, -1, 1))
    inner = slice(TOP, TOP + 184)

    def diffuse(f, middle, north, south):
        around = e[f, to_east, :] + e[f, to_west, :] + north[inner] + south[inner]
        return DIFFUSION * (around - 4.0 * middle)

    for i in range(h.shape[0]):
        level = step * h.shape[0] + i
        north, south = [], []
        for f, field in enumerate((h, u, v)):
            e[f, pl.ds(TOP, COLS), :] = field[i]
            e[f, pl.ds(TOP - 1, 1), :] = west[f, pl.ds(level, 1), :]
            e[f, pl.ds(TOP + COLS, 1), :] = east[f, pl.ds(level, 1), :]
            block = e[f]
            spot = 16 * f + level
            spot_north = jnp.where(at_north, spot + 16, spot) if f == 2 else spot
            edge = pltpu.roll(rim[0], ROWS - 1 - spot_north, 1)
            north.append(jnp.where(lane == ROWS - 1, edge, pltpu.roll(block, ROWS - 1, 1)))
            edge = pltpu.roll(rim[1], lax.rem(ROWS - spot, ROWS), 1)
            south.append(jnp.where(lane == 0, edge, pltpu.roll(block, 1, 1)))
        t_sum[...] = e[1] + north[1]
        w_sum[...] = e[2] + south[2]
        mid_h, mid_u, mid_v = (e[f, here, :] for f in range(3))
        new_u = (
            mid_u
            - zonal * (e[0, to_east, :] - mid_h)
            + turn_u * (w_sum[here, :] + w_sum[to_east, :])
            + diffuse(1, mid_u, north[1], south[1])
        )
        new_v = (
            mid_v
            - GRAV_MERID * (north[0][inner] - mid_h)
            - turn_v * (t_sum[here, :] + t_sum[to_west, :])
            + diffuse(2, mid_v, north[2], south[2])
        )
        flux = mid_u - e[1, to_west, :] + cos_face * mid_v - cos_south * south[2][inner]
        new_h = mid_h - diverge * flux + diffuse(0, mid_h, north[0], south[0])
        uv_out[i, 0] = new_u[:COLS]
        uv_out[i, 1] = new_v[:COLS]
        h_out[i] = new_h[:COLS]


def stencil(place, height, u_wind, v_wind, west, east, above, below, across, tables):
    some = 2
    field = pl.BlockSpec((some, COLS, ROWS), lambda i, s: (i, 0, 0))
    side = pl.BlockSpec((3, LEV, ROWS), lambda i, s: (0, 0, 0))
    edge = pl.BlockSpec((TALL, ROWS), lambda i, s: (0, 0))
    table = pl.BlockSpec((1, 8, ROWS), lambda i, s: (s[0], 0, 0))
    pair = pl.BlockSpec((some, 2, COLS, ROWS), lambda i, s: (i, 0, 0, 0))
    tall = pltpu.VMEM((TALL, ROWS), jnp.float32)
    return pl.pallas_call(
        stencil_kernel,
        grid_spec=pltpu.PrefetchScalarGridSpec(
            num_scalar_prefetch=1,
            grid=(LEV // some,),
            in_specs=[field, field, field, side, side, edge, edge, edge, table],
            out_specs=[pair, field],
            scratch_shapes=[
                pltpu.VMEM((3, TALL, ROWS), jnp.float32),
                pltpu.VMEM((2, TALL, ROWS), jnp.float32),
                tall,
                tall,
            ],
        ),
        out_shape=[
            jax.ShapeDtypeStruct((LEV, 2, COLS, ROWS), jnp.float32),
            jax.ShapeDtypeStruct((LEV, COLS, ROWS), jnp.float32),
        ],
        cost_estimate=pl.CostEstimate(
            flops=50_000_000, bytes_accessed=9_000_000, transcendentals=0
        ),
    )(place, height, u_wind, v_wind, west, east, above, below, across, tables)


def filter_kernel(items, place, x, forward, inverse, over, table, out, spectra, waves):
    q = pl.program_id(0)
    full = COLS // 16
    rest = COLS - 16 * full

    @pl.when(q == 0)
    def _():
        def gather(start, item, read):
            lanes = slice(item * ROWS, (item + 1) * ROWS)
            pairs = forward16([read(p) for p in range(16)])
            for part in range(8):
                for side in range(2):
                    rows = pl.ds(pl.multiple_of(side * HALF + start, 16), 16)
                    high, low = split(pairs[part][side])
                    spectra[part, 0, rows, lanes] = high
                    spectra[part, 1, rows, lanes] = low

        for item in range(items):

            def chunk(c, carry, item=item):
                start = pl.multiple_of(c * 16, 16)
                gather(start, item, lambda p: x[p, item, pl.ds(start, 16), :])
                return carry

            lax.fori_loop(0, full, chunk, 0)
            empty = jnp.zeros((16 - rest, ROWS), jnp.float32)
            gather(
                16 * full,
                item,
                lambda p, item=item: jnp.concatenate(
                    [x[p, item, pl.ds(16 * full, rest), :], empty], 0
                ),
            )

    def product(matrix, high, low):
        both = jnp.dot(matrix[0], high, preferred_element_type=jnp.float32)
        small = jnp.dot(matrix[0, : 2 * HALF], low, preferred_element_type=jnp.float32)
        return both[: 2 * HALF] + (both[2 * HALF :] + small)

    found = product(forward, spectra[q, 0], spectra[q, 1])
    damping = jnp.minimum(table[0, 5:6, :] * over[0], 1.0)
    damped = jnp.concatenate(
        [found[:, i * ROWS : (i + 1) * ROWS] * damping for i in range(items)], 1
    )
    waves[q] = product(inverse, *split(damped))

    @pl.when(q == 7)
    def _():
        def scatter(start, item, count):
            lanes = slice(item * ROWS, (item + 1) * ROWS)
            pairs = [
                tuple(
                    waves[part, pl.ds(pl.multiple_of(side * HALF + start, 8), 8), lanes]
                    for side in range(2)
                )
                for part in range(8)
            ]
            for p, value in enumerate(inverse16(pairs)):
                out[p, item, pl.ds(start, count), :] = value[:count]

        for item in range(items):

            def chunk(c, carry, item=item):
                scatter(pl.multiple_of(c * 8, 8), item, 8)
                return carry

            lax.fori_loop(0, COLS // 8, chunk, 0)
            scatter(8 * (COLS // 8), item, COLS % 8)


def polar_filter(place, x, tables):
    items = x.shape[1]
    forward, inverse, over = fourier_tables()
    wide = items * ROWS
    whole = pl.BlockSpec(x.shape, lambda q, s: (0, 0, 0, 0), pipeline_mode=pl.Buffered(1))
    matrix = pl.BlockSpec((1, 4 * HALF, 2 * HALF), lambda q, s: (q, 0, 0))
    return pl.pallas_call(
        functools.partial(filter_kernel, items),
        grid_spec=pltpu.PrefetchScalarGridSpec(
            num_scalar_prefetch=1,
            grid=(8,),
            in_specs=[
                whole,
                matrix,
                matrix,
                pl.BlockSpec((1, 2 * HALF, ROWS), lambda q, s: (q, 0, 0)),
                pl.BlockSpec((1, 8, ROWS), lambda q, s: (s[0], 0, 0)),
            ],
            out_specs=pl.BlockSpec(x.shape, lambda q, s: (0, 0, 0, 0)),
            scratch_shapes=[
                pltpu.VMEM((8, 2, 2 * HALF, wide), jnp.bfloat16),
                pltpu.VMEM((8, 2 * HALF, wide), jnp.float32),
            ],
        ),
        out_shape=jax.ShapeDtypeStruct(x.shape, jnp.float32),
        compiler_params=pltpu.CompilerParams(vmem_limit_bytes=56 * 1024 * 1024),
        cost_estimate=pl.CostEstimate(
            flops=96 * (2 * HALF) ** 2 * wide, bytes_accessed=15_000_000, transcendentals=0
        ),
    )(place, x, jnp.asarray(forward), jnp.asarray(inverse), jnp.asarray(over), tables)


def around(lat, shift, distance):
    return [
        (lon * N_LAT + lat, (lon + distance) % N_LON * N_LAT + (lat + shift))
        for lon in range(N_LON)
    ]


def shards(u_wind, v_wind, height):
    band = lax.axis_index("lat")
    at_north, at_south = band == N_LAT - 1, band == 0
    place = jnp.stack([band, at_north, at_south]).astype(jnp.int32)
    tables = jnp.asarray(latitude_tables())
    fields = (height, u_wind, v_wind)
    last = jnp.stack([field[:, COLS - 1, :] for field in fields])
    initial = jnp.stack([field[:, 0, :] for field in fields])
    east_to = [(i, (i + 1) % N_LON) for i in range(N_LON)]
    west = lax.ppermute(last, "lon", east_to)
    east = lax.ppermute(initial, "lon", [(j, i) for i, j in east_to])
    low, high = pack(height, u_wind, v_wind, west, east)
    below = lax.ppermute(high, "lat", [(i, i + 1) for i in range(N_LAT - 1)])
    above = lax.ppermute(low, "lat", [(i + 1, i) for i in range(N_LAT - 1)])
    across = lax.ppermute(
        jnp.where(at_north, high, low),
        AXES,
        around(0, 0, N_LON // 2) + around(N_LAT - 1, 0, N_LON // 2),
    )
    uv, h = stencil(place, height, u_wind, v_wind, west, east, above, below, across, tables)

    def exchange(value):
        return lax.all_to_all(value, "lon", split_axis=0, concat_axis=0, tiled=True)

    def smooth(value):
        return exchange(polar_filter(place, exchange(value), tables))

    def filtered(uv, h):
        whole = jnp.concatenate([uv, h[:, None]], 1)
        result = smooth(whole)
        return result[:, 0], result[:, 1], result[:, 2]

    is_polar = (band < N_LAT // 4) | (band >= N_LAT - N_LAT // 4)
    return lax.cond(is_polar, filtered, lambda uv, h: (uv[:, 0], uv[:, 1], h), uv, h)


def solution(mesh):
    placed = (P(None, "lon", "lat"),) * 3
    return jax.shard_map(shards, mesh=mesh, in_specs=placed, out_specs=placed, check_vma=False)
```

time: 513 us -> 188 us (0.37)
  the two profiles are of different devices: /device:TPU:19 before, /device:TPU:1 now
where the time goes in v1:
time: 188 us; the launch traced here: 187 us
  blocking collectives  117 us (62%)
  Pallas kernels  37.2 us (20%)
  local copies, waits for them, and re-layouts  16.1 us (9%)
  starting transfers between devices  11.3 us (6%)
  other arithmetic  2.68 us (1%)
  waiting for transfers between devices  2.12 us (1%)
    all_to_all x2, blocking collectives, exchange(): return lax.all_to_all(value, 'lon', split_axis=0, concat_axis=0, tiled=True)  117 us
    pallas_call x1, Pallas kernels, polar_filter(): pl.pallas_call(functools.partial(filter_kernel, items), grid_spec=pltpu.P...  20.8 us
    unnamed x24, local copies, waits for them, and re-layouts  12.6 us
    pallas_call x1, Pallas kernels, stencil(): pl.pallas_call(stencil_kernel, grid_spec=pltpu.PrefetchScalarGridSpec(num...  10.5 us
    pallas_call x1, Pallas kernels, pack(): pl.pallas_call(pack_kernel, grid=(LEV // STEP,), in_specs=[field, field,...  5.85 us
    ppermute x1, starting transfers between devices, shards(): below = lax.ppermute(high, 'lat', [(i, i + 1) for i in range(N_LAT - 1)])  4.21 us
  transfers between devices with their start and end apart: 5, of which 1 were waited for; matrix products, arithmetic and copies ran while one was open for 4% of the time, Pallas kernels for 0%

profile of v1, /device:TPU:1, one launch (start us, length us, event | category | flops | bytes accessed | tf_op | source)
XLA Modules:
  0.0 187.3 jit_solution(18138253641635743758)
XLA Ops:
  0.6 0.7 slice_bitcast_fusion.7
  1.3 0.7 slice_bitcast_fusion.5
  2.1 2.6 %collective-permute-start = (f32[3,16,128]{2,1,0:T(8,128)S(1)}, f32[3,16,128]{2,1,0:T(8,128)S(1)}, u32[]{:S(2)}, u32[]{:S(2)}) collective-permute-start(f32[3,16,128]{2,1,0:T(8,128)S(1)} %pad_maximum_fusion.1), channel_id=1, source_target_pairs={{0,8},{8,16},{16,24},{24,32},{32,40},{40,48},{48,56},{56,64},{64,7... | collective-permute-start | bytes 73736 | tf_op jit(solution)/shard_map/ppermute | solution.py:432
  4.8 3.1 %copy.23.u = f32[16,180,128]{2,1,0:T(8,128)} copy(f32[16,180,128]{2,0,1:T(8,128)} %param.9) | data formatting | bytes 2949120 | tf_op args[0]
  7.9 1.6 copy.24.v
  9.4 1.6 copy.22.h
  11.1 0.6 copy-done.7
  11.7 0.6 copy-done.8
  12.3 5.9 %shard_map.101 = (f32[200,128]{1,0:T(8,128)}, f32[200,128]{1,0:T(8,128)}) custom-call(f32[16,180,128]{2,1,0:T(8,128)} %copy.22.h, f32[16,180,128]{2,1,0:T(8,128)} %copy.23.u, f32[16,180,128]{2,1,0:T(8,128)} %copy.24.v, f32[3,16,128]{2,1,0:T(8,128)} %copy-done.7, f32[3,16,128]{2,1,0:T(8,128)} %copy-done.8), custom_call_target="tpu_custom_call" | custom-call | bytes 4700000 | tf_op jit(solution)/shard_map/pallas_call | solution.py:212
  18.1 1.3 collective-permute-start.2
  19.4 0.9 broadcast_select_fusion
  20.3 4.2 %collective-permute-start.3 = (f32[200,128]{1,0:T(8,128)}, f32[200,128]{1,0:T(8,128)S(1)}, u32[]{:S(2)}, u32[]{:S(2)}) collective-permute-start(f32[200,128]{1,0:T(8,128)} %get-tuple-element.35), channel_id=1, source_target_pairs={{0,1},{1,2},{2,3},{3,4},{4,5},{5,6},{6,7},{8,9},{9,10},{10,11},{11... | collective-permute-start | bytes 307208 | tf_op jit(solution)/shard_map/ppermute | solution.py:435
  24.5 3.2 %collective-permute-start.4 = (f32[200,128]{1,0:T(8,128)S(1)}, f32[200,128]{1,0:T(8,128)S(1)}, u32[]{:S(2)}, u32[]{:S(2)}) collective-permute-start(f32[200,128]{1,0:T(8,128)S(1)} %broadcast_select_fusion), channel_id=1, source_target_pairs={{0,64},{8,72},{16,80},{24,88},{32,96},{40,104},{48,112},{56,120},{... | collective-permute-start | bytes 307208 | tf_op jit(solution)/shard_map/ppermute | solution.py:437
  27.8 2.1 %collective-permute-done.4.across = f32[200,128]{1,0:T(8,128)S(1)} collective-permute-done((f32[200,128]{1,0:T(8,128)S(1)}, f32[200,128]{1,0:T(8,128)S(1)}, u32[]{:S(2)}, u32[]{:S(2)}) %collective-permute-start.4) | collective-permute-done | bytes 102432 | tf_op jit(solution)/shard_map/ppermute | solution.py:437
  30.0 0.6 copy-done.6
  30.6 0.6 copy-done.5
  31.3 10.5 %shard_map.102 = (f32[16,2,180,128]{3,2,1,0:T(8,128)S(1)}, f32[16,180,128]{2,1,0:T(8,128)}) custom-call(s32[3]{0:T(128)S(1)} %pad_add_fusion.place, f32[16,180,128]{2,1,0:T(8,128)} %copy.22.h, f32[16,180,128]{2,1,0:T(8,128)} %copy.23.u, f32[16,180,128]{2,1,0:T(8,128)} %copy.24.v, f32[3,16,128]{2,1,0:T(8,128)} %copy-done.7, f32[3,16,128]{2,1,0:T(8,128)} %copy-done.8, ...), custom_call_target="tpu_custom_call" | custom-call | flops 50000000 | bytes 9000000 | tf_op jit(solution)/shard_map/pallas_call | solution.py:290
  41.8 141.6 %conditional.1 = (f32[16,180,128]{2,1,0:T(8,128)}, f32[16,180,128]{2,0,1:T(8,128)S(1)}, f32[16,180,128]{2,0,1:T(8,128)S(1)}) conditional(s32[]{:T(128)} %convert_element_type.2, (f32[16,2,180,128]{3,2,1,0:T(8,128)S(1)}, f32[16,180,128]{2,1,0:T(8,128)}) %shard_map.102, (f32[16,180,128]{2,1,0:T(8,128)}, f32[16,2,180,128]{3,2,1,0:T(8,128)S(1)}, ...), branch_computations={%region_0.1_spmd, %region_1.2_spmd} | conditional | flops 5436923904 | bytes 56287704 | solution.py:456
  41.8 1.7 pad_maximum_fusion
  43.5 59.9 %all_to_all.8.x = f32[16,3,180,128]{3,2,1,0:T(8,128)} all-to-all(f32[16,3,180,128]{3,2,1,0:T(8,128)S(1)} %pad_maximum_fusion), channel_id=1, replica_groups=mesh['lon'=16,'lat'=8] {'lon'}, dimensions={0} | all-to-all | bytes 8847360 | tf_op jit(solution)/shard_map/cond/branch_1_fun/all_to_all | solution.py:445
  103.4 20.8 %branch_1_fun.1 = f32[16,3,180,128]{3,2,1,0:T(8,128)} custom-call(s32[3]{0:T(128)S(1)} %get-tuple-element.20.place, f32[16,3,180,128]{3,2,1,0:T(8,128)} %all_to_all.8.x, bf16[8,768,384]{2,1,0:T(8,128)(2,1)} %constant.21.clone.1.forward, bf16[8,768,384]{2,1,0:T(8,128)(2,1)} %constant.22.clone.1.inverse, f32[8,384,128]{2,1,0:T(8,128)} %constant.23.clone.1.over, ...), custom_call_target="tpu_custom_call" | custom-call | flops 5435817984 | bytes 15000000 | tf_op jit(solution)/shard_map/cond/branch_1_fun/pallas_call | solution.py:390
  124.2 57.2 %all_to_all.9 = f32[16,3,180,128]{3,2,1,0:T(8,128)S(1)} all-to-all(f32[16,3,180,128]{3,2,1,0:T(8,128)} %branch_1_fun.1), channel_id=1, replica_groups=mesh['lon'=16,'lat'=8] {'lon'}, dimensions={0} | all-to-all | bytes 8847360 | tf_op jit(solution)/shard_map/cond/branch_1_fun/all_to_all | solution.py:445
  181.4 1.4 slice_bitcast_fusion.2
  183.4 3.8 %copy.27 = f32[16,180,128]{2,0,1:T(8,128)} copy(f32[16,180,128]{2,1,0:T(8,128)} %get-tuple-element.48) | data formatting | bytes 2949120
  (26 shorter events, 0.7 us)
Async XLA Ops:
  2.1 8.9 %collective-permute-start = (f32[3,16,128]{2,1,0:T(8,128)S(1)}, f32[3,16,128]{2,1,0:T(8,128)S(1)}, u32[]{:S(2)}, u32[]{:S(2)}) collective-permute-start(f32[3,16,128]{2,1,0:T(8,128)S(1)} %pad_maximum_fusion.1), channel_id=1, source_target_pairs={{0,8},{8,16},{16,24},{24,32},{32,40},{40,48},{48,56},{56,64},{64,7... | collective-permute-start | bytes 73736 | tf_op jit(solution)/shard_map/ppermute | solution.py:432
  4.8 3.1 %copy-start = (f32[16,180,128]{2,0,1:T(8,128)S(1)}, f32[16,180,128]{2,0,1:T(8,128)}, u32[]{:S(2)}) copy-start(f32[16,180,128]{2,0,1:T(8,128)} %param.10) | copy-start | bytes 4423684
  4.8 6.3 %collective-permute-start.1 = (f32[3,16,128]{2,1,0:T(8,128)S(1)}, f32[3,16,128]{2,1,0:T(8,128)S(1)}, u32[]{:S(2)}, u32[]{:S(2)}) collective-permute-start(f32[3,16,128]{2,1,0:T(8,128)S(1)} %pad_maximum_fusion.2), channel_id=1, source_target_pairs={{8,0},{16,8},{24,16},{32,24},{40,32},{48,40},{56,48},{64,56},{72,6... | collective-permute-start | bytes 73736 | tf_op jit(solution)/shard_map/ppermute | solution.py:433
  7.9 1.6 copy-start.1
  11.0 20.2 %copy-start.9 = (f32[8,8,128]{2,1,0:T(8,128)S(1)}, f32[8,8,128]{2,1,0:T(8,128)}, u32[]{:S(2)}) copy-start(f32[8,8,128]{2,1,0:T(8,128)} %constant.20.clone.table) | copy-start | bytes 98308
  11.0 0.6 copy-start.7
  11.7 0.6 copy-start.8
  18.1 11.8 %collective-permute-start.2 = (f32[200,128]{1,0:T(8,128)}, f32[200,128]{1,0:T(8,128)S(1)}, u32[]{:S(2)}, u32[]{:S(2)}) collective-permute-start(f32[200,128]{1,0:T(8,128)} %get-tuple-element.34), channel_id=1, source_target_pairs={{1,0},{2,1},{3,2},{4,3},{5,4},{6,5},{7,6},{9,8},{10,9},{11,10},{12... | collective-permute-start | bytes 307208 | tf_op jit(solution)/shard_map/ppermute | solution.py:436
  20.3 9.6 %collective-permute-start.3 = (f32[200,128]{1,0:T(8,128)}, f32[200,128]{1,0:T(8,128)S(1)}, u32[]{:S(2)}, u32[]{:S(2)}) collective-permute-start(f32[200,128]{1,0:T(8,128)} %get-tuple-element.35), channel_id=1, source_target_pairs={{0,1},{1,2},{2,3},{3,4},{4,5},{5,6},{6,7},{8,9},{9,10},{10,11},{11... | collective-permute-start | bytes 307208 | tf_op jit(solution)/shard_map/ppermute | solution.py:435
  24.5 5.4 %collective-permute-start.4 = (f32[200,128]{1,0:T(8,128)S(1)}, f32[200,128]{1,0:T(8,128)S(1)}, u32[]{:S(2)}, u32[]{:S(2)}) collective-permute-start(f32[200,128]{1,0:T(8,128)S(1)} %broadcast_select_fusion), channel_id=1, source_target_pairs={{0,64},{8,72},{16,80},{24,88},{32,96},{40,104},{48,112},{56,120},{... | collective-permute-start | bytes 307208 | tf_op jit(solution)/shard_map/ppermute | solution.py:437
  29.9 0.6 copy-start.6
  30.0 0.7 copy-start.4
  30.6 0.6 copy-start.5
  183.4 3.9 %copy-start.2 = (f32[16,180,128]{2,0,1:T(8,128)}, f32[16,180,128]{2,0,1:T(8,128)S(1)}, u32[]{:S(2)}) copy-start(f32[16,180,128]{2,0,1:T(8,128)S(1)} %get-tuple-element.50) | copy-start | bytes 4423684
  183.4 3.9 %copy-start.3 = (f32[16,180,128]{2,0,1:T(8,128)}, f32[16,180,128]{2,0,1:T(8,128)S(1)}, u32[]{:S(2)}) copy-start(f32[16,180,128]{2,0,1:T(8,128)S(1)} %get-tuple-element.49) | copy-start | bytes 4423684

commit v2 on v1

v2 whole, which is shorter than its diff:
```python
import functools
import math

import jax
import jax.numpy as jnp
import numpy as np
from jax import lax
from jax.experimental import pallas as pl
from jax.experimental.pallas import tpu as pltpu
from jax.sharding import PartitionSpec as P

N_LON = 16
N_LAT = 8
LEV = 16
COLS = 180
ROWS = 128
NLON = N_LON * COLS
NLAT = N_LAT * ROWS
HALF = 192
TALL = 184
PACK = 90
CHUNK = 48
SOME = 96
AHEAD = 16
AXES = ("lon", "lat")

GRAV_ZONAL = 0.3
GRAV_MERID = 0.6
CORIOLIS = 0.8
DIVERGENCE = 0.3
DIFFUSION = 0.08


def latitude_tables():
    f32 = np.float32
    index = np.arange(NLAT).astype(f32)
    step = f32(math.pi / NLAT)

    def sine(angle):
        return np.sin(angle.astype(np.float64)).astype(f32)

    def cosine(angle):
        return np.cos(angle.astype(np.float64)).astype(f32)

    center = (index + f32(0.5)) * step
    face = (index + f32(1.0)) * step
    cos_center = sine(center)
    sin_center = -cosine(center)
    sin_face = -cosine(face)
    cos_face = np.where(index + 1 < NLAT, sine(face), f32(0.0))
    cos_south = sine(index * step)
    ratio = f32(2.0) * cos_center * cos_center
    table = np.stack(
        [
            GRAV_ZONAL / cos_center.astype(np.float64),
            CORIOLIS * 0.25 * sin_center.astype(np.float64),
            CORIOLIS * 0.25 * sin_face.astype(np.float64),
            cos_face,
            cos_south,
            ratio,
            DIVERGENCE / cos_center.astype(np.float64),
            np.zeros(NLAT),
        ]
    ).astype(f32)
    return np.ascontiguousarray(table.reshape(8, N_LAT, ROWS).transpose(1, 0, 2))


def split(value):
    high = value.astype(jnp.bfloat16)
    return high, (value - high.astype(value.dtype)).astype(jnp.bfloat16)


@functools.cache
def fourier_tables():
    at = np.arange(COLS)
    angles = (at[:, None] * at[None, :] % COLS) * (2.0 * math.pi / COLS)
    matrix = np.zeros((2, HALF, HALF), np.float32)
    matrix[0, :COLS, :COLS] = np.cos(angles)
    matrix[1, :COLS, :COLS] = np.sin(angles)
    matrix = matrix.reshape(2 * HALF, HALF)
    high = matrix.astype(jnp.bfloat16)
    low = (matrix - high.astype(np.float32)).astype(jnp.bfloat16)
    columns = np.zeros((HALF, ROWS), np.float32)
    for q in range(9):
        turn = q * at * (2.0 * math.pi / NLON)
        columns[:COLS, q] = np.cos(turn)
        columns[:COLS, 16 + q] = -np.sin(turn)
        wave = q + 16 * at
        wave = np.minimum(wave, NLON - wave)
        sine = np.sin((wave.astype(np.float32) * np.float32(math.pi / NLON)).astype(np.float64))
        sine_sq = (sine.astype(np.float32) * sine.astype(np.float32)).astype(np.float64)
        over = np.where(wave == 0, 1e30, 1.0 / np.where(wave == 0, 1.0, sine_sq))
        columns[:COLS, 32 + q] = over * scale_of(q)
    return np.concatenate([high, low], axis=0), columns


def scale_of(q):
    return (1.0 if q in (0, 8) else 2.0) / NLON


SIN = [math.sin(math.pi * t / 8) for t in range(5)]


def times(value, c, s):
    re, im = value
    return (c * re - s * im, c * im + s * re)


def forward16(x):
    e = [x[p] + x[p + 8] for p in range(8)]
    o = [x[p] - x[p + 8] for p in range(8)]
    e2 = [e[p] + e[p + 4] for p in range(4)]
    o2 = [e[p] - e[p + 4] for p in range(4)]
    a, b = e2[0] + e2[2], e2[1] + e2[3]
    pairs = [None] * 8
    pairs[0] = (a + b, a - b)
    pairs[4] = (e2[0] - e2[2], e2[3] - e2[1])
    root = SIN[2]
    u = (o2[0], -o2[2])
    w = times((o2[1], -o2[3]), root, -root)
    pairs[2] = (u[0] + w[0], u[1] + w[1])
    pairs[6] = (u[0] - w[0], w[1] - u[1])
    d = [times((o[p], -o[p + 4]), SIN[4 - p], -SIN[p]) if p else (o[p], -o[p + 4]) for p in range(4)]
    s02 = (d[0][0] + d[2][0], d[0][1] + d[2][1])
    t02 = (d[0][0] - d[2][0], d[0][1] - d[2][1])
    s13 = (d[1][0] + d[3][0], d[1][1] + d[3][1])
    t13 = (d[1][0] - d[3][0], d[1][1] - d[3][1])
    pairs[1] = (s02[0] + s13[0], s02[1] + s13[1])
    pairs[7] = (s02[0] - s13[0], s13[1] - s02[1])
    pairs[5] = (t02[0] + t13[1], t02[1] - t13[0])
    pairs[3] = (t02[0] - t13[1], -(t02[1] + t13[0]))
    return pairs


def inverse16(pairs):
    z0, z8 = pairs[0]
    a, b = z0 + z8, z0 - z8
    e2 = [a + pairs[4][0], b - pairs[4][1], a - pairs[4][0], b + pairs[4][1]]
    u, v = pairs[2], (pairs[6][0], -pairs[6][1])
    d0 = (u[0] + v[0], u[1] + v[1])
    root = SIN[2]
    d1 = times((u[0] - v[0], u[1] - v[1]), root, root)
    o2 = [d0[0], d1[0], -d0[1], -d1[1]]
    e = [e2[p] + o2[p] for p in range(4)] + [e2[p] - o2[p] for p in range(4)]
    a1, a5 = pairs[1], pairs[5]
    a9, a13 = (pairs[7][0], -pairs[7][1]), (pairs[3][0], -pairs[3][1])
    s19 = (a1[0] + a9[0], a1[1] + a9[1])
    t19 = (a1[0] - a9[0], a1[1] - a9[1])
    s5 = (a5[0] + a13[0], a5[1] + a13[1])
    t5 = (a5[0] - a13[0], a5[1] - a13[1])
    d = [
        (s19[0] + s5[0], s19[1] + s5[1]),
        (t19[0] - t5[1], t19[1] + t5[0]),
        (s19[0] - s5[0], s19[1] - s5[1]),
        (t19[0] + t5[1], t19[1] - t5[0]),
    ]
    d = [times(d[p], SIN[4 - p], SIN[p]) if p else d[p] for p in range(4)]
    o = [d[p][0] for p in range(4)] + [-d[p][1] for p in range(4)]
    return [e[p] + o[p] for p in range(8)] + [e[p] - o[p] for p in range(8)]


def row(i):
    return pl.ds(pl.multiple_of(i * LEV, LEV), LEV)


def lanes_of(shape):
    return lax.broadcasted_iota(jnp.int32, shape, len(shape) - 1)


def pack_kernel(place, h, u, v, first, second, low, high):
    step = pl.program_id(0)

    @pl.when(step == 0)
    def _():
        low[...] = jnp.zeros_like(low)
        high[...] = jnp.zeros_like(high)

    spots = [lanes_of((LEV, ROWS)) + ROWS * part for part in range(2)]
    kept_low = [[low[f, part] for part in range(2)] for f in range(3)]
    kept_high = [[high[f, part] for part in range(2)] for f in range(4)]
    for i in range(PACK):
        spot = step * PACK + i + 1
        masks = [[s == spot + k for s in spots] for k in (-1, 0, 1)]
        for f, field in enumerate((h, u, v)):
            turned = pltpu.roll(field[i * LEV : (i + 1) * LEV, :], lax.rem(spot + 1, ROWS), 1)
            for part in range(2):
                kept_high[f][part] = jnp.where(masks[1][part], turned, kept_high[f][part])
                kept_low[f][part] = jnp.where(masks[2][part], turned, kept_low[f][part])
                if f == 2:
                    kept_high[3][part] = jnp.where(masks[0][part], turned, kept_high[3][part])
    for part in range(2):
        for f in range(3):
            low[f, part] = kept_low[f][part]
        for f in range(4):
            high[f, part] = kept_high[f][part]

    @pl.when(step == pl.num_programs(0) - 1)
    def _():
        even = place[4] == 1
        for f in range(4):
            if f < 3:
                south = shift_lanes([low[f, 0], low[f, 1]], -1)
                north = [high[f, 0], high[f, 1]]
            else:
                south = [jnp.zeros((LEV, ROWS), jnp.float32)] * 2
                north = shift_lanes([high[f, 0], high[f, 1]], 1)
            for part in range(2):
                first[f, part] = jnp.where(even, north[part], south[part])
                second[f, part] = jnp.where(even, south[part], north[part])


def shift_lanes(parts, by):
    turned = [pltpu.roll(part, by % ROWS, 1) for part in parts]
    lane = lanes_of(parts[0].shape)
    fresh = lane == (0 if by > 0 else ROWS - 1)
    return [jnp.where(fresh, turned[1 - i], turned[i]) for i in range(2)]


def pack(place, height, u_wind, v_wind):
    field = pl.BlockSpec((PACK * LEV, ROWS), lambda i, s: (i, 0))
    shape = (4, 2, LEV, ROWS)
    edge = pl.BlockSpec(shape, lambda i, s: (0, 0, 0, 0))
    return pl.pallas_call(
        pack_kernel,
        grid_spec=pltpu.PrefetchScalarGridSpec(
            num_scalar_prefetch=1,
            grid=(COLS // PACK,),
            in_specs=[field, field, field],
            out_specs=[edge, edge],
            scratch_shapes=[pltpu.VMEM(shape, jnp.float32)] * 2,
        ),
        out_shape=[jax.ShapeDtypeStruct(shape, jnp.float32)] * 2,
        cost_estimate=pl.CostEstimate(flops=0, bytes_accessed=4_700_000, transcendentals=0),
    )(place, height, u_wind, v_wind)


def rim_terms(place, first, second, table, terms):
    even, at_north, at_south = place[4] == 1, place[1] == 1, place[2] == 1
    lane = lanes_of((LEV, ROWS))

    def rim(f, part):
        above = jnp.where(even, first[f, part], second[f, part])
        below = jnp.where(even, second[f, part], first[f, part])
        if f == 0:
            return above, below
        turned = -second[3 if f == 2 else f, part]
        across = -second[f, part] if f == 1 else jnp.zeros_like(below)
        return jnp.where(at_north, turned, above), jnp.where(at_south, across, below)

    (h_n, h_s), (u_n, u_s), (v_n, v_s) = (
        zip(*(rim(f, part) for part in range(2))) for f in range(3)
    )
    turn_u, cos_south, diverge = (table[0, i : i + 1, 0:1] for i in (1, 4, 6))
    turn_v = table[0, 2:3, ROWS - 1 : ROWS]
    u_nw, v_se = shift_lanes(u_n, 1), shift_lanes(v_s, -1)
    for part in range(2):
        north = (
            DIFFUSION * h_n[part],
            DIFFUSION * u_n[part],
            DIFFUSION * v_n[part] - GRAV_MERID * h_n[part] - turn_v * (u_n[part] + u_nw[part]),
        )
        south = (
            DIFFUSION * h_s[part] + diverge * cos_south * v_s[part],
            DIFFUSION * u_s[part] + turn_u * (v_s[part] + v_se[part]),
            DIFFUSION * v_s[part],
        )
        for f in range(3):
            after = pltpu.roll(south[f], 1, 1)
            for odd in range(2):
                terms[f, odd, part] = jnp.where(lane % 2 == odd, north[f], after)


def stencil_kernel(
    place, h, u, v, h_west, u_west, v_west, h_east, u_east, v_east, west, east, first, second, table,
    u_out, v_out, h_first, h_second, own_h, own_u, own_v, terms, whole,
):
    step = pl.program_id(0)
    lane = lanes_of((LEV, ROWS))
    edges = (lane == 0) | (lane == ROWS - 1)

    @pl.when(step == 0)
    def _():
        rim_terms(place, first, second, table, terms)

    zonal, turn_u, turn_v, cos_face, cos_south, _, diverge = (
        jnp.broadcast_to(table[0, i : i + 1, :], (LEV, ROWS)) for i in range(7)
    )

    def north(block):
        return jnp.where(lane == ROWS - 1, 0.0, pltpu.roll(block, ROWS - 1, 1))

    def south(block):
        return jnp.where(lane == 0, 0.0, pltpu.roll(block, 1, 1))

    def update(k, odd, carry, blocks_east):
        (t_west, v_south, w_here), (west_h, west_u, west_v) = carry
        mid_h, mid_u, mid_v = middle = [field[row(k), :] for field in (h, u, v)]
        east_h, east_u, east_v = blocks_east
        h_north, h_south = north(mid_h), south(mid_h)
        u_north, u_south = north(mid_u), south(mid_u)
        v_north, v_south_east = north(mid_v), south(east_v)
        t_here = mid_u + u_north
        w_east = east_v + v_south_east
        new_u = (
            mid_u
            - zonal * (east_h - mid_h)
            + turn_u * (w_here + w_east)
            + DIFFUSION * (east_u + west_u + (u_north + u_south) - 4.0 * mid_u)
        )
        new_v = (
            mid_v
            - GRAV_MERID * (h_north - mid_h)
            - turn_v * (t_here + t_west)
            + DIFFUSION * (east_v + west_v + (v_north + v_south) - 4.0 * mid_v)
        )
        new_h = (
            mid_h
            - diverge * (mid_u - west_u + cos_face * mid_v - cos_south * v_south)
            + DIFFUSION * (east_h + west_h + (h_north + h_south) - 4.0 * mid_h)
        )
        spot = step * CHUNK + k + 1
        turn = lax.rem(2 * ROWS - 1 - spot, ROWS)
        results = []
        for f, new in enumerate((new_h, new_u, new_v)):
            term = pltpu.roll(terms[f, odd, spot // ROWS], turn, 1)
            results.append(new + jnp.where(edges, term, 0.0))
        return ((t_here, v_south_east, w_east), middle), results

    def several(base, carry, beyond):
        found = []
        for n in range(AHEAD):
            k = base + n
            if n == AHEAD - 1 and beyond is not None:
                blocks = beyond
            else:
                blocks = [field[row(k + 1), :] for field in (h, u, v)]
            if n == (COLS - 1) % AHEAD:
                is_last = step * CHUNK + k == COLS - 1
                blocks = [jnp.where(is_last, east[f], blocks[f]) for f in range(3)]
            carry, results = update(k, (n + 1) % 2, carry, blocks)
            found.append(results)
        for n, results in enumerate(found):
            for f in range(3):
                whole[f, row(base + n), :] = results[f]
        return carry

    before = [
        jnp.where(step == 0, west[f], field[...]) for f, field in enumerate((h_west, u_west, v_west))
    ]
    here_v = v[row(0), :]
    v_south = south(here_v)
    carry = ((before[1] + north(before[1]), v_south, here_v + v_south), before)
    groups = CHUNK // AHEAD
    carry = lax.fori_loop(
        0, groups - 1, lambda c, carry: several(c * AHEAD, carry, None), carry
    )
    several((groups - 1) * AHEAD, carry, [field[...] for field in (h_east, u_east, v_east)])

    @pl.when(place[3] == 0)
    def _():
        for f, out in enumerate((own_h, own_u, own_v)):
            out[...] = whole[f]

    @pl.when(place[3] == 1)
    def _():
        def turned(f):
            return jnp.transpose(whole[f].reshape(CHUNK, LEV, ROWS), (1, 0, 2))

        height = turned(0)
        h_first[...] = height[: LEV // 2]
        h_second[...] = height[LEV // 2 :]
        u_out[...] = turned(1)
        v_out[...] = turned(2)


def stencil(place, height, u_wind, v_wind, west, east, first, second, tables):
    block = pl.BlockSpec((CHUNK * LEV, ROWS), lambda i, s: (i, 0))
    one_west = pl.BlockSpec((LEV, ROWS), lambda i, s: (jnp.maximum(i * CHUNK - 1, 0), 0))
    one_east = pl.BlockSpec(
        (LEV, ROWS), lambda i, s: (jnp.minimum((i + 1) * CHUNK, COLS - 1), 0)
    )
    side = pl.BlockSpec((3, LEV, ROWS), lambda i, s: (0, 0, 0))
    edge = pl.BlockSpec((4, 2, LEV, ROWS), lambda i, s: (0, 0, 0, 0))
    kept = pl.BlockSpec((CHUNK * LEV, ROWS), lambda i, s: (jnp.where(s[3] == 0, i, 0), 0))

    def sent(levels):
        return pl.BlockSpec(
            (levels, CHUNK, ROWS), lambda i, s: (0, jnp.where(s[3] == 1, i, 0), 0)
        )

    own = jax.ShapeDtypeStruct((COLS * LEV, ROWS), jnp.float32)
    full = jax.ShapeDtypeStruct((LEV, TALL, ROWS), jnp.float32)
    half = jax.ShapeDtypeStruct((LEV // 2, TALL, ROWS), jnp.float32)
    fields = (height, u_wind, v_wind)
    return pl.pallas_call(
        stencil_kernel,
        grid_spec=pltpu.PrefetchScalarGridSpec(
            num_scalar_prefetch=1,
            grid=(pl.cdiv(COLS, CHUNK),),
            in_specs=[block] * 3
            + [one_west] * 3
            + [one_east] * 3
            + [side] * 2
            + [edge] * 2
            + [pl.BlockSpec((1, 8, ROWS), lambda i, s: (s[0], 0, 0))],
            out_specs=[sent(LEV), sent(LEV), sent(LEV // 2), sent(LEV // 2)] + [kept] * 3,
            scratch_shapes=[
                pltpu.VMEM((3, 2, 2, LEV, ROWS), jnp.float32),
                pltpu.VMEM((3, CHUNK * LEV, ROWS), jnp.float32),
            ],
        ),
        out_shape=[full, full, half, half, own, own, own],
        compiler_params=pltpu.CompilerParams(vmem_limit_bytes=58 * 1024 * 1024),
        cost_estimate=pl.CostEstimate(
            flops=60_000_000, bytes_accessed=9_000_000, transcendentals=0
        ),
    )(place, *fields, *fields, *fields, west, east, first, second, tables)


def unpack_kernel(place, own, *refs):
    parts, out = refs[:-1], refs[-1]

    @pl.when(place[3] == 1)
    def _():
        whole = jnp.concatenate([x[...] for x in parts], 0)
        out[...] = jnp.transpose(whole, (1, 0, 2)).reshape(SOME * LEV, ROWS)

    @pl.when(place[3] == 0)
    def _():
        out[...] = own[...]


def unpack(place, own, *parts):
    def pick(polar):
        return lambda i, s: jnp.where(s[3] == polar, i, 0)

    kept, used = pick(0), pick(1)
    return pl.pallas_call(
        unpack_kernel,
        grid_spec=pltpu.PrefetchScalarGridSpec(
            num_scalar_prefetch=1,
            grid=(pl.cdiv(COLS, SOME),),
            in_specs=[pl.BlockSpec((SOME * LEV, ROWS), lambda i, s: (kept(i, s), 0))]
            + [
                pl.BlockSpec((x.shape[0], SOME, ROWS), lambda i, s: (0, used(i, s), 0))
                for x in parts
            ],
            out_specs=pl.BlockSpec((SOME * LEV, ROWS), lambda i, s: (i, 0)),
        ),
        out_shape=jax.ShapeDtypeStruct((COLS * LEV, ROWS), jnp.float32),
        compiler_params=pltpu.CompilerParams(vmem_limit_bytes=58 * 1024 * 1024),
        cost_estimate=pl.CostEstimate(
            flops=0, bytes_accessed=8 * COLS * LEV * ROWS, transcendentals=0
        ),
    )(place, own, *parts)


def filter_kernel(place, x, matrix, columns, table, out, spectra, waves):
    def column(rows, q):
        return columns[rows, q : q + 1]

    def gather(start, blocks):
        rows = pl.ds(pl.multiple_of(start, 16), 16)
        pairs = forward16(blocks)
        parts = [(pairs[0][0], None)] + pairs[1:] + [(pairs[0][1], None)]
        for q, (re, im) in enumerate(parts):
            if q == 0:
                im = jnp.zeros_like(re)
            else:
                c, s = column(rows, q), column(rows, 16 + q)
                re, im = (c * re, s * re) if im is None else times((re, im), c, s)
            for side, value in enumerate((re, im)):
                high, low = split(value)
                spectra[q, 0, rows, side * ROWS : (side + 1) * ROWS] = high
                spectra[q, 1, rows, side * ROWS : (side + 1) * ROWS] = low

    def fill(c, carry):
        start = pl.multiple_of(c * 16, 16)
        gather(start, [x[p, pl.ds(start, 16), :] for p in range(16)])
        return carry

    full = COLS // 16
    lax.fori_loop(0, full, fill, 0)
    empty = jnp.zeros((HALF - COLS, ROWS), jnp.float32)
    tail = pl.ds(16 * full, COLS % 16)
    gather(16 * full, [jnp.concatenate([x[p, tail, :], empty], 0) for p in range(16)])

    def product(high, low):
        found = jnp.dot(matrix[: 2 * HALF], high, preferred_element_type=jnp.float32)
        found += jnp.dot(matrix[2 * HALF :], high, preferred_element_type=jnp.float32)
        found += jnp.dot(matrix[: 2 * HALF], low, preferred_element_type=jnp.float32)
        cos, sin = found[:HALF], found[HALF:]
        return cos[:, :ROWS], cos[:, ROWS:], sin[:, :ROWS], sin[:, ROWS:]

    ratio = table[0, 5:6, :]
    rows = slice(0, HALF)
    for q in range(9):
        cos_re, cos_im, sin_re, sin_im = product(spectra[q, 0], spectra[q, 1])
        damping = jnp.minimum(ratio * column(rows, 32 + q), scale_of(q))
        re, im = damping * (cos_re + sin_im), damping * (cos_im - sin_re)
        cos_re, cos_im, sin_re, sin_im = product(*split(jnp.concatenate([re, im], 1)))
        re = cos_re - sin_im
        if q:
            im = cos_im + sin_re
            c, s = column(rows, q), column(rows, 16 + q)
            if q < 8:
                waves[q, 1] = c * im - s * re
            re = c * re + s * im
        waves[q, 0] = re

    def give(c, carry):
        rows = pl.ds(pl.multiple_of(c * 8, 8), 8)
        pairs = [(waves[0, 0, rows, :], waves[8, 0, rows, :])]
        pairs += [(waves[q, 0, rows, :], waves[q, 1, rows, :]) for q in range(1, 8)]
        for p, value in enumerate(inverse16(pairs)):
            out[p, rows, :] = value
        return carry

    lax.fori_loop(0, TALL // 8, give, 0)


def polar_filter(place, x, tables):
    matrix, columns = fourier_tables()
    whole = pl.BlockSpec(x.shape, lambda i, s: (0, 0, 0))
    return pl.pallas_call(
        filter_kernel,
        grid_spec=pltpu.PrefetchScalarGridSpec(
            num_scalar_prefetch=1,
            grid=(1,),
            in_specs=[
                whole,
                pl.BlockSpec(matrix.shape, lambda i, s: (0, 0)),
                pl.BlockSpec(columns.shape, lambda i, s: (0, 0)),
                pl.BlockSpec((1, 8, ROWS), lambda i, s: (s[0], 0, 0)),
            ],
            out_specs=whole,
            scratch_shapes=[
                pltpu.VMEM((9, 2, HALF, 2 * ROWS), jnp.bfloat16),
                pltpu.VMEM((9, 2, HALF, ROWS), jnp.float32),
            ],
        ),
        out_shape=jax.ShapeDtypeStruct(x.shape, jnp.float32),
        compiler_params=pltpu.CompilerParams(vmem_limit_bytes=58 * 1024 * 1024),
        cost_estimate=pl.CostEstimate(
            flops=216 * HALF * HALF * ROWS, bytes_accessed=3_500_000, transcendentals=0
        ),
    )(place, x, jnp.asarray(matrix), jnp.asarray(columns), tables)


BESIDE = ((0, 3), (1, 2), (6, 5), (7, 4))
BEYOND = ((0, 4), (1, 5), (6, 2), (7, 3))


def lent(pairs, turn):
    return [
        (lon * N_LAT + polar, (lon ^ turn) * N_LAT + other)
        for lon in range(N_LON)
        for polar, other in pairs
    ]


def returned(pairs, turn):
    return [(j, i) for i, j in lent(pairs, turn)]


def partner(band, pairs):
    return sum(jnp.where(band == other, polar, 0) for polar, other in pairs).astype(jnp.int32)


def shards(u_wind, v_wind, height):
    band = lax.axis_index("lat")
    is_polar = (band < N_LAT // 4) | (band >= N_LAT - N_LAT // 4)
    even = band % 2 == 0
    place = jnp.stack([band, band == N_LAT - 1, band == 0, is_polar, even]).astype(jnp.int32)
    tables = jnp.asarray(latitude_tables())
    fields = [jnp.swapaxes(x, 0, 1) for x in (height, u_wind, v_wind)]
    flat = [x.reshape(COLS * LEV, ROWS) for x in fields]
    east_to = [(i, (i + 1) % N_LON) for i in range(N_LON)]
    west = lax.ppermute(jnp.stack([x[COLS - 1] for x in fields]), "lon", east_to)
    east = lax.ppermute(jnp.stack([x[0] for x in fields]), "lon", [(j, i) for i, j in east_to])
    first, second = pack(place, *flat)
    spot = lax.broadcasted_iota(jnp.int32, first.shape, 1) * ROWS + lax.broadcasted_iota(
        jnp.int32, first.shape, 3
    )

    def widened(value, is_north):
        def edge(side):
            north = [side[f, :, ROWS - 1 - (f == 3) :][:, :1] for f in range(3)]
            north.append(side[2, :, ROWS - 2 : ROWS - 1])
            south = [side[min(f, 2), :, :1] for f in range(4)]
            return jnp.where(is_north, jnp.stack(north), jnp.stack(south))[:, None]

        value = jnp.where(spot == 0, edge(west), value)
        return jnp.where(spot == COLS + 1, edge(east), value)

    swap = [(i, i ^ 1) for i in range(N_LAT)]
    first = lax.ppermute(widened(first, even), "lat", swap)
    routes = [(lon, i, lon, i + 1) for lon in range(N_LON) for i in range(1, N_LAT - 1, 2)]
    routes += [(lon, i + 1, lon, i) for lon, i, _, _ in routes]
    routes += [
        (lon, i, (lon + N_LON // 2) % N_LON, i) for lon in range(N_LON) for i in (0, N_LAT - 1)
    ]
    second = lax.ppermute(
        widened(second, jnp.logical_not(even)),
        AXES,
        [(a * N_LAT + b, c * N_LAT + d) for a, b, c, d in routes],
    )
    u, v, h_first, h_second, own_h, own_u, own_v = stencil(
        place, *flat, west, east, first, second, tables
    )

    def exchange(value):
        return lax.all_to_all(value, "lon", split_axis=0, concat_axis=0, tiled=True)

    def keep(u, v_circles, h_first, h_second):
        u_circles = exchange(u)
        v = exchange(polar_filter(place, v_circles, tables))
        return v, polar_filter(place, u_circles, tables)

    def help_out(u, v_circles, h_first, h_second):
        circles = exchange(jnp.concatenate([h_first, h_second], 0))
        lender = jnp.where(
            lax.axis_index("lon") < N_LON // 2, partner(band, BESIDE), partner(band, BEYOND)
        )
        smooth = polar_filter(lender.reshape(1), circles, tables)
        return exchange(smooth), smooth

    h_first = lax.ppermute(h_first, AXES, lent(BESIDE, 0))
    h_second = lax.ppermute(h_second, AXES, lent(BEYOND, N_LON // 2))
    v_circles = exchange(v)
    v_or_h, u = lax.cond(is_polar, keep, help_out, u, v_circles, h_first, h_second)
    h_first = lax.ppermute(v_or_h[: LEV // 2], AXES, returned(BESIDE, 0))
    h_second = lax.ppermute(v_or_h[LEV // 2 :], AXES, returned(BEYOND, N_LON // 2))
    u = exchange(u)
    result = (
        unpack(place, own_u, u),
        unpack(place, own_v, v_or_h),
        unpack(place, own_h, h_first, h_second),
    )
    return tuple(jnp.swapaxes(x.reshape(COLS, LEV, ROWS), 0, 1) for x in result)


def solution(mesh):
    placed = (P(None, "lon", "lat"),) * 3
    return jax.shard_map(shards, mesh=mesh, in_specs=placed, out_specs=placed, check_vma=False)
```

time: 188 us -> 160 us (0.85)
  blocking collectives: 117 us -> 0 us
  waiting for transfers between devices: 2.12 us -> 69.6 us
  starting transfers between devices: 11.3 us -> 40.4 us
  local copies, waits for them, and re-layouts: 16.1 us -> 8.1 us
  Pallas kernels: 37.2 us -> 39.1 us
    all_to_all x2 -> x0, blocking collectives: 117 us -> none  [exchange(): return lax.all_to_all(value, 'lon', split_axis=0, concat_axis=0, tiled=True)]
    ppermute x5 -> x8, waiting for transfers between devices: 2.12 us -> 43.1 us  [the longest x1 24.8 us: shards(): lax.ppermute(v_or_h[LEV // 2:], AXES, returned(BEYOND, N_LON // 2))]
    all_to_all x0 -> x4, waiting for transfers between devices: none -> 26.5 us  [exchange(): return lax.all_to_all(value, 'lon', split_axis=0, concat_axis=0, tiled=True)]
    all_to_all x0 -> x4, starting transfers between devices: none -> 23.1 us  [exchange(): return lax.all_to_all(value, 'lon', split_axis=0, concat_axis=0, tiled=True)]
    unnamed x24 -> x20, local copies, waits for them, and re-layouts: 12.6 us -> 2.65 us
    ppermute x5 -> x8, starting transfers between devices: 11.3 us -> 17.4 us  [the longest x1 7.48 us: shards(): h_first = lax.ppermute(h_first, AXES, lent(BESIDE, 0))]
    slice x0 -> x8, local copies, waits for them, and re-layouts: none -> 4.22 us  [the longest x3 2.15 us: shards(): x[0]]
    pallas_call x2 -> x6, Pallas kernels: 26.6 us -> 29 us  [the longest x2 15.2 us: polar_filter(): pl.pallas_call(filter_kernel, grid_spec=pltpu.PrefetchScalarGridSpec(num_...]
  transfers between devices with their start and end apart: 5 -> 12, of which waited for: 1 -> 7; matrix products, arithmetic and copies ran while one was open for 4% -> 1% of each run, Pallas kernels for 0% -> 16%
where the time goes in v2:
time: 160 us; the launch traced here: 159 us
  waiting for transfers between devices  69.6 us (43%)
  starting transfers between devices  40.4 us (25%)
  Pallas kernels  39.1 us (24%)
  local copies, waits for them, and re-layouts  8.1 us (5%)
    all_to_all x4, waiting for transfers between devices, exchange(): return lax.all_to_all(value, 'lon', split_axis=0, concat_axis=0, tiled=True)  26.5 us
    ppermute x1, waiting for transfers between devices, shards(): lax.ppermute(v_or_h[LEV // 2:], AXES, returned(BEYOND, N_LON // 2))  24.8 us
    all_to_all x4, starting transfers between devices, exchange(): return lax.all_to_all(value, 'lon', split_axis=0, concat_axis=0, tiled=True)  23.1 us
    pallas_call x2, Pallas kernels, polar_filter(): pl.pallas_call(filter_kernel, grid_spec=pltpu.PrefetchScalarGridSpec(num_...  15.2 us
    ppermute x1, waiting for transfers between devices, shards(): h_first = lax.ppermute(h_first, AXES, lent(BESIDE, 0))  14.9 us
    pallas_call x1, Pallas kernels, stencil(): pl.pallas_call(stencil_kernel, grid_spec=pltpu.PrefetchScalarGridSpec(num...  10.1 us
    pallas_call x3, Pallas kernels, unpack(): pl.pallas_call(unpack_kernel, grid_spec=pltpu.PrefetchScalarGridSpec(num_...  9.61 us
    ppermute x1, starting transfers between devices, shards(): h_first = lax.ppermute(h_first, AXES, lent(BESIDE, 0))  7.48 us
  transfers between devices with their start and end apart: 12, of which 7 were waited for; matrix products, arithmetic and copies ran while one was open for 1% of the time, Pallas kernels for 16%

profile of v2, /device:TPU:1, one launch (start us, length us, event | category | flops | bytes accessed | tf_op | source)
XLA Modules:
  0.0 159.1 jit_solution(14210763667359020909)
XLA Ops:
  2.8 2.6 %collective-permute-start = (f32[3,16,128]{2,1,0:T(8,128)S(1)}, f32[3,16,128]{2,1,0:T(8,128)S(1)}, u32[]{:S(2)}, u32[]{:S(2)}) collective-permute-start(f32[3,16,128]{2,1,0:T(8,128)S(1)} %pad_maximum_fusion.1), channel_id=1, source_target_pairs={{0,8},{8,16},{16,24},{24,32},{32,40},{40,48},{48,56},{56,64},{64,7... | collective-permute-start | bytes 73736 | tf_op jit(solution)/shard_map/ppermute | solution.py:579
  5.5 4.2 %shard_map.85 = (f32[4,2,16,128]{3,2,1,0:T(8,128)}, f32[4,2,16,128]{3,2,1,0:T(8,128)}) custom-call(s32[5]{0:T(128)S(1)} %stack.77.place, f32[2880,128]{1,0:T(8,128)} %bitcast.29, f32[2880,128]{1,0:T(8,128)} %bitcast.34, f32[2880,128]{1,0:T(8,128)} %bitcast.39), custom_call_target="tpu_custom_call" | custom-call | bytes 4700000 | tf_op jit(solution)/shard_map/pallas_call | solution.py:223
  11.4 1.4 collective-permute-start.3
  12.8 2.0 %collective-permute-start.2 = (f32[4,2,16,128]{3,2,1,0:T(8,128)S(1)}, f32[4,2,16,128]{3,2,1,0:T(8,128)S(1)}, u32[]{:S(2)}, u32[]{:S(2)}) collective-permute-start(f32[4,2,16,128]{3,2,1,0:T(8,128)S(1)} %get-tuple-element.82), channel_id=1, source_target_pairs={{0,1},{1,0},{2,3},{3,2},{4,5},{5,4},{6,7},{7,6},{8,9},{9,8},{10,11... | collective-permute-start | bytes 196616 | tf_op jit(solution)/shard_map/ppermute | solution.py:597
  14.8 1.6 %collective-permute-done.2.first = f32[4,2,16,128]{3,2,1,0:T(8,128)S(1)} collective-permute-done((f32[4,2,16,128]{3,2,1,0:T(8,128)S(1)}, f32[4,2,16,128]{3,2,1,0:T(8,128)S(1)}, u32[]{:S(2)}, u32[]{:S(2)}) %collective-permute-start.2) | collective-permute-done | bytes 65568 | tf_op jit(solution)/shard_map/ppermute | solution.py:597
  17.0 10.1 %shard_map.86 = (f32[16,184,128]{2,1,0:T(8,128)}, f32[16,184,128]{2,1,0:T(8,128)}, f32[8,184,128]{2,1,0:T(8,128)}, f32[8,184,128]{2,1,0:T(8,128)}, f32[2880,128]...) custom-call(s32[5]{0:T(128)S(1)} %stack.77.place, f32[2880,128]{1,0:T(8,128)} %bitcast.30, f32[2880,128]{1,0:T(8,128)} %bitcast.35, ...), custom_call_target="tpu_custom_call" | custom-call | flops 60000000 | bytes 9000000 | tf_op jit(solution)/shard_map/pallas_call | solution.py:395
  27.2 7.5 %all-to-all-start.4 = ((f32[16,184,128]{2,1,0:T(8,128)}), f32[16,184,128]{2,1,0:T(8,128)S(1)}, u32[]{:S(2)}, u32[]{:S(2)}) async-start(f32[16,184,128]{2,1,0:T(8,128)} %get-tuple-element.55), calls=%async_computation.4 | async-start | bytes 3014656 | tf_op jit(solution)/shard_map/all_to_all | solution.py:613
  34.7 7.5 %collective-permute-start.4 = (f32[8,184,128]{2,1,0:T(8,128)}, f32[8,184,128]{2,1,0:T(8,128)S(1)}, u32[]{:S(2)}, u32[]{:S(2)}) collective-permute-start(f32[8,184,128]{2,1,0:T(8,128)} %get-tuple-element.53), channel_id=1, source_target_pairs={{0,3},{1,2},{6,5},{7,4},{8,11},{9,10},{14,13},{15,12},{16,19},{17,... | collective-permute-start | bytes 2261000 | tf_op jit(solution)/shard_map/ppermute | solution.py:628
  42.2 1.3 collective-permute-start.5
  43.5 14.9 %collective-permute-done.4 = f32[8,184,128]{2,1,0:T(8,128)S(1)} collective-permute-done((f32[8,184,128]{2,1,0:T(8,128)}, f32[8,184,128]{2,1,0:T(8,128)S(1)}, u32[]{:S(2)}, u32[]{:S(2)}) %collective-permute-start.4) | collective-permute-done | bytes 753696 | tf_op jit(solution)/shard_map/ppermute | solution.py:628
  58.4 1.3 collective-permute-done.5
  59.8 54.3 %conditional.1 = (f32[16,184,128]{2,1,0:T(8,128)}, f32[16,184,128]{2,1,0:T(8,128)}) conditional(s32[]{:T(128)} %convert_element_type.2, (s32[]{:T(128)}, f32[8,184,128]{2,1,0:T(8,128)S(1)}, f32[8,184,128]{2,1,0:T(8,128)S(1)}, bf16[768,192]{1,0:T(8,128)(2,1)S(1)}, f32[192,128]{1,0:T(8,128)S(1)}, /*index=5*/f32[8,8,128]{2,1,0:T(8,128)S(1)}) %tuple.38, ...), branch_computations={%region_0.1_spmd, %region_1.2_spmd} | conditional | flops 2038431744 | bytes 22073388 | solution.py:631
  59.8 6.5 %all-to-all-start.1 = ((f32[16,184,128]{2,1,0:T(8,128)}), f32[16,184,128]{2,1,0:T(8,128)S(1)}, u32[]{:S(2)}, u32[]{:S(2)}) async-start(f32[16,184,128]{2,1,0:T(8,128)} %get-tuple-element.35), calls=%async_computation.1 | async-start | bytes 3014656 | tf_op jit(solution)/shard_map/cond/branch_1_fun/all_to_all | solution.py:613
  66.3 6.9 %branch_1_fun.2 = f32[16,184,128]{2,1,0:T(8,128)} custom-call(s32[5]{0:T(128)S(1)} %get-tuple-element.30.place, f32[16,184,128]{2,1,0:T(8,128)S(1)} %get-tuple-element.31.x, bf16[768,192]{1,0:T(8,128)(2,1)S(1)} %get-tuple-element.32.matrix, f32[192,128]{1,0:T(8,128)S(1)} %get-tuple-element.33.columns, f32[8,8,128]{2,1,0:T(8,128)S(1)} %get-tuple-element.34.table), custom_call_target="tpu_custom_call" | custom-call | flops 1019215872 | bytes 3500000 | tf_op jit(solution)/shard_map/cond/branch_1_fun/pallas_call | solution.py:525
  73.2 13.9 %all-to-all-done.1.x = f32[16,184,128]{2,1,0:T(8,128)S(1)} async-done(((f32[16,184,128]{2,1,0:T(8,128)}), f32[16,184,128]{2,1,0:T(8,128)S(1)}, u32[]{:S(2)}, u32[]{:S(2)}) %all-to-all-start.1) | async-done | bytes 1507360 | tf_op jit(solution)/shard_map/cond/branch_1_fun/all_to_all | solution.py:613
  88.2 4.9 %all-to-all-start = ((f32[16,184,128]{2,1,0:T(8,128)}), f32[16,184,128]{2,1,0:T(8,128)}, u32[]{:S(2)}, u32[]{:S(2)}) async-start(f32[16,184,128]{2,1,0:T(8,128)} %branch_1_fun.2), calls=%async_computation | async-start | bytes 3014656 | tf_op jit(solution)/shard_map/cond/branch_1_fun/all_to_all | solution.py:613
  93.1 8.3 %branch_1_fun.3 = f32[16,184,128]{2,1,0:T(8,128)} custom-call(s32[5]{0:T(128)S(1)} %get-tuple-element.30.place, f32[16,184,128]{2,1,0:T(8,128)} %copy-done.2, bf16[768,192]{1,0:T(8,128)(2,1)S(1)} %get-tuple-element.32.matrix, f32[192,128]{1,0:T(8,128)S(1)} %get-tuple-element.33.columns, f32[8,8,128]{2,1,0:T(8,128)S(1)} %get-tuple-element.34.table), custom_call_target="tpu_custom_call" | custom-call | flops 1019215872 | bytes 3500000 | tf_op jit(solution)/shard_map/cond/branch_1_fun/pallas_call | solution.py:525
  101.4 12.7 %all-to-all-done = f32[16,184,128]{2,1,0:T(8,128)} async-done(((f32[16,184,128]{2,1,0:T(8,128)}), f32[16,184,128]{2,1,0:T(8,128)}, u32[]{:S(2)}, u32[]{:S(2)}) %all-to-all-start) | async-done | bytes 1507360 | tf_op jit(solution)/shard_map/cond/branch_1_fun/all_to_all | solution.py:613
  114.0 4.2 %all-to-all-start.5 = ((f32[16,184,128]{2,1,0:T(8,128)}), f32[16,184,128]{2,1,0:T(8,128)S(1)}, u32[]{:S(2)}, u32[]{:S(2)}) async-start(f32[16,184,128]{2,1,0:T(8,128)} %get-tuple-element.57), calls=%async_computation.5 | async-start | bytes 3014656 | tf_op jit(solution)/shard_map/all_to_all | solution.py:613
  118.2 1.4 fusion.6
  122.3 3.2 %shard_map.88 = f32[2880,128]{1,0:T(8,128)} custom-call(s32[5]{0:T(128)S(1)} %stack.77.place, f32[2880,128]{1,0:T(8,128)} %get-tuple-element.58.own, f32[16,184,128]{2,1,0:T(8,128)} %get-tuple-element.59.refs_0_), custom_call_target="tpu_custom_call" | custom-call | bytes 2949120 | tf_op jit(solution)/shard_map/pallas_call | solution.py:438
  125.5 24.8 %collective-permute-done.7.refs_1_ = f32[8,184,128]{2,1,0:T(8,128)S(1)} collective-permute-done((f32[8,184,128]{2,1,0:T(8,128)S(1)}, f32[8,184,128]{2,1,0:T(8,128)S(1)}, u32[]{:S(2)}, u32[]{:S(2)}) %collective-permute-start.7) | collective-permute-done | bytes 753696 | tf_op jit(solution)/shard_map/ppermute | solution.py:633
  151.5 3.2 %shard_map.89 = f32[2880,128]{1,0:T(8,128)} custom-call(s32[5]{0:T(128)S(1)} %stack.77.place, f32[2880,128]{1,0:T(8,128)} %get-tuple-element.60.own, f32[8,184,128]{2,1,0:T(8,128)} %copy-done.4, f32[8,184,128]{2,1,0:T(8,128)} %copy-done.3), custom_call_target="tpu_custom_call" | custom-call | bytes 2949120 | tf_op jit(solution)/shard_map/pallas_call | solution.py:438
  155.9 3.2 %shard_map.87 = f32[2880,128]{1,0:T(8,128)} custom-call(s32[5]{0:T(128)S(1)} %stack.77.place, f32[2880,128]{1,0:T(8,128)} %get-tuple-element.52.own, f32[16,184,128]{2,1,0:T(8,128)} %copy-done), custom_call_target="tpu_custom_call" | custom-call | bytes 2949120 | tf_op jit(solution)/shard_map/pallas_call | solution.py:438
  (44 shorter events, 10.6 us)
Async XLA Ops:
  2.8 6.9 %collective-permute-start = (f32[3,16,128]{2,1,0:T(8,128)S(1)}, f32[3,16,128]{2,1,0:T(8,128)S(1)}, u32[]{:S(2)}, u32[]{:S(2)}) collective-permute-start(f32[3,16,128]{2,1,0:T(8,128)S(1)} %pad_maximum_fusion.1), channel_id=1, source_target_pairs={{0,8},{8,16},{16,24},{24,32},{32,40},{40,48},{48,56},{56,64},{64,7... | collective-permute-start | bytes 73736 | tf_op jit(solution)/shard_map/ppermute | solution.py:579
  5.4 4.6 %collective-permute-start.1 = (f32[3,16,128]{2,1,0:T(8,128)S(1)}, f32[3,16,128]{2,1,0:T(8,128)S(1)}, u32[]{:S(2)}, u32[]{:S(2)}) collective-permute-start(f32[3,16,128]{2,1,0:T(8,128)S(1)} %pad_maximum_fusion.2), channel_id=1, source_target_pairs={{8,0},{16,8},{24,16},{32,24},{40,32},{48,40},{56,48},{64,56},{72,6... | collective-permute-start | bytes 73736 | tf_op jit(solution)/shard_map/ppermute | solution.py:580
  5.5 11.5 %copy-start.9 = (f32[8,8,128]{2,1,0:T(8,128)S(1)}, f32[8,8,128]{2,1,0:T(8,128)}, u32[]{:S(2)}) copy-start(f32[8,8,128]{2,1,0:T(8,128)} %constant.57.clone.table) | copy-start | bytes 98308
  9.7 6.7 %copy-start.5 = (f32[3,16,128]{2,1,0:T(8,128)}, f32[3,16,128]{2,1,0:T(8,128)S(1)}, u32[]{:S(2)}) copy-start(f32[3,16,128]{2,1,0:T(8,128)S(1)} %collective-permute-done.west) | copy-start | bytes 73732
  10.0 6.4 %copy-start.6 = (f32[3,16,128]{2,1,0:T(8,128)}, f32[3,16,128]{2,1,0:T(8,128)S(1)}, u32[]{:S(2)}) copy-start(f32[3,16,128]{2,1,0:T(8,128)S(1)} %collective-permute-done.1.east) | copy-start | bytes 73732
  11.4 3.4 %collective-permute-start.3 = (f32[4,2,16,128]{3,2,1,0:T(8,128)S(1)}, f32[4,2,16,128]{3,2,1,0:T(8,128)S(1)}, u32[]{:S(2)}, u32[]{:S(2)}) collective-permute-start(f32[4,2,16,128]{3,2,1,0:T(8,128)S(1)} %get-tuple-element.81), channel_id=1, source_target_pairs={{1,2},{3,4},{5,6},{9,10},{11,12},{13,14},{17,18},{19,20},{21,22},{... | collective-permute-start | bytes 196616 | tf_op jit(solution)/shard_map/ppermute | solution.py:603
  12.8 3.6 %collective-permute-start.2 = (f32[4,2,16,128]{3,2,1,0:T(8,128)S(1)}, f32[4,2,16,128]{3,2,1,0:T(8,128)S(1)}, u32[]{:S(2)}, u32[]{:S(2)}) collective-permute-start(f32[4,2,16,128]{3,2,1,0:T(8,128)S(1)} %get-tuple-element.82), channel_id=1, source_target_pairs={{0,1},{1,0},{2,3},{3,2},{4,5},{5,4},{6,7},{7,6},{8,9},{9,8},{10,11... | collective-permute-start | bytes 196616 | tf_op jit(solution)/shard_map/ppermute | solution.py:597
  14.8 1.7 %copy-start.7 = (f32[4,2,16,128]{3,2,1,0:T(8,128)}, f32[4,2,16,128]{3,2,1,0:T(8,128)S(1)}, u32[]{:S(2)}) copy-start(f32[4,2,16,128]{3,2,1,0:T(8,128)S(1)} %collective-permute-done.3.second) | copy-start | bytes 196612
  16.4 0.6 copy-start.8
  27.1 32.6 %copy-start.10 = (bf16[768,192]{1,0:T(8,128)(2,1)S(1)}, bf16[768,192]{1,0:T(8,128)(2,1)}, u32[]{:S(2)}) copy-start(bf16[768,192]{1,0:T(8,128)(2,1)} %constant.58.clone) | copy-start | bytes 884740
  27.2 32.6 %copy-start.11 = (f32[192,128]{1,0:T(8,128)S(1)}, f32[192,128]{1,0:T(8,128)}, u32[]{:S(2)}) copy-start(f32[192,128]{1,0:T(8,128)} %constant.59.clone) | copy-start | bytes 294916
  27.2 32.6 %all-to-all-start.4 = ((f32[16,184,128]{2,1,0:T(8,128)}), f32[16,184,128]{2,1,0:T(8,128)S(1)}, u32[]{:S(2)}, u32[]{:S(2)}) async-start(f32[16,184,128]{2,1,0:T(8,128)} %get-tuple-element.55), calls=%async_computation.4 | async-start | bytes 3014656 | tf_op jit(solution)/shard_map/all_to_all | solution.py:613
  34.7 23.7 %collective-permute-start.4 = (f32[8,184,128]{2,1,0:T(8,128)}, f32[8,184,128]{2,1,0:T(8,128)S(1)}, u32[]{:S(2)}, u32[]{:S(2)}) collective-permute-start(f32[8,184,128]{2,1,0:T(8,128)} %get-tuple-element.53), channel_id=1, source_target_pairs={{0,3},{1,2},{6,5},{7,4},{8,11},{9,10},{14,13},{15,12},{16,19},{17,... | collective-permute-start | bytes 2261000 | tf_op jit(solution)/shard_map/ppermute | solution.py:628
  42.2 17.6 %collective-permute-start.5 = (f32[8,184,128]{2,1,0:T(8,128)}, f32[8,184,128]{2,1,0:T(8,128)S(1)}, u32[]{:S(2)}, u32[]{:S(2)}) collective-permute-start(f32[8,184,128]{2,1,0:T(8,128)} %get-tuple-element.54), channel_id=1, source_target_pairs={{0,68},{1,69},{6,66},{7,67},{8,76},{9,77},{14,74},{15,75},{16,84},... | collective-permute-start | bytes 2261000 | tf_op jit(solution)/shard_map/ppermute | solution.py:629
  59.8 27.3 %all-to-all-start.1 = ((f32[16,184,128]{2,1,0:T(8,128)}), f32[16,184,128]{2,1,0:T(8,128)S(1)}, u32[]{:S(2)}, u32[]{:S(2)}) async-start(f32[16,184,128]{2,1,0:T(8,128)} %get-tuple-element.35), calls=%async_computation.1 | async-start | bytes 3014656 | tf_op jit(solution)/shard_map/cond/branch_1_fun/all_to_all | solution.py:613
  87.1 1.1 copy-start.2
  88.2 25.8 %all-to-all-start = ((f32[16,184,128]{2,1,0:T(8,128)}), f32[16,184,128]{2,1,0:T(8,128)}, u32[]{:S(2)}, u32[]{:S(2)}) async-start(f32[16,184,128]{2,1,0:T(8,128)} %branch_1_fun.2), calls=%async_computation | async-start | bytes 3014656 | tf_op jit(solution)/shard_map/cond/branch_1_fun/all_to_all | solution.py:613
  114.0 40.7 %all-to-all-start.5 = ((f32[16,184,128]{2,1,0:T(8,128)}), f32[16,184,128]{2,1,0:T(8,128)S(1)}, u32[]{:S(2)}, u32[]{:S(2)}) async-start(f32[16,184,128]{2,1,0:T(8,128)} %get-tuple-element.57), calls=%async_computation.5 | async-start | bytes 3014656 | tf_op jit(solution)/shard_map/all_to_all | solution.py:613
  119.7 30.6 %collective-permute-start.7 = (f32[8,184,128]{2,1,0:T(8,128)S(1)}, f32[8,184,128]{2,1,0:T(8,128)S(1)}, u32[]{:S(2)}, u32[]{:S(2)}) collective-permute-start(f32[8,184,128]{2,1,0:T(8,128)S(1)} %get-tuple-element.69), channel_id=1, source_target_pairs={{68,0},{69,1},{66,6},{67,7},{76,8},{77,9},{74,14},{75,15},{84,16},... | collective-permute-start | bytes 2261000 | tf_op jit(solution)/shard_map/ppermute | solution.py:633
  121.0 29.7 %collective-permute-start.6 = (f32[8,184,128]{2,1,0:T(8,128)S(1)}, f32[8,184,128]{2,1,0:T(8,128)S(1)}, u32[]{:S(2)}, u32[]{:S(2)}) collective-permute-start(f32[8,184,128]{2,1,0:T(8,128)S(1)} %get-tuple-element.70), channel_id=1, source_target_pairs={{3,0},{2,1},{5,6},{4,7},{11,8},{10,9},{13,14},{12,15},{19,16},{18,... | collective-permute-start | bytes 2261000 | tf_op jit(solution)/shard_map/ppermute | solution.py:632
  150.3 0.9 copy-start.3
  150.7 0.9 copy-start.4
  154.7 1.2 copy-start

commit v3 on v2

--- a/solution.py
+++ b/solution.py
@@ -167,6 +167,55 @@
     return lax.broadcasted_iota(jnp.int32, shape, len(shape) - 1)
 
 
+def ends_kernel(*refs):
+    for f in range(3):
+        refs[6][f] = refs[f][...]
+        refs[7][f] = refs[3 + f][...]
+
+
+def ends(fields):
+    first = pl.BlockSpec((LEV, ROWS), lambda i: (0, 0))
+    last = pl.BlockSpec((LEV, ROWS), lambda i: (COLS - 1, 0))
+    out = pl.BlockSpec((3, LEV, ROWS), lambda i: (0, 0, 0))
+    return pl.pallas_call(
+        ends_kernel,
+        grid=(1,),
+        in_specs=[first] * 3 + [last] * 3,
+        out_specs=[out] * 2,
+        out_shape=[jax.ShapeDtypeStruct((3, LEV, ROWS), jnp.float32)] * 2,
+    )(*fields, *fields)
+
+
+def widen_kernel(place, first, second, west, east, first_out, second_out):
+    even = place[4] == 1
+    lane = lanes_of((LEV, ROWS))
+    for f in range(4):
+        back = 2 if f == 3 else 1
+        side_west, side_east = west[min(f, 2)], east[min(f, 2)]
+        end = (COLS + 1) % ROWS
+        north = (pltpu.roll(side_west, back, 1), pltpu.roll(side_east, end + back, 1))
+        south = (side_west, pltpu.roll(side_east, end, 1))
+        for source, out, is_north in (
+            (first, first_out, even),
+            (second, second_out, jnp.logical_not(even)),
+        ):
+            at_west, at_east = (jnp.where(is_north, a, b) for a, b in zip(north, south))
+            out[f, 0] = jnp.where(lane == 0, at_west, source[f, 0])
+            out[f, 1] = jnp.where(lane == end, at_east, source[f, 1])
+
+
+def widen(place, first, second, west, east):
+    vmem = pl.BlockSpec(memory_space=pltpu.VMEM)
+    shape = jax.ShapeDtypeStruct(first.shape, jnp.float32)
+    return pl.pallas_call(
+        widen_kernel,
+        grid_spec=pltpu.PrefetchScalarGridSpec(
+            num_scalar_prefetch=1, grid=(1,), in_specs=[vmem] * 4, out_specs=[vmem] * 2
+        ),
+        out_shape=[shape] * 2,
+    )(place, first, second, west, east)
+
+
 def pack_kernel(place, h, u, v, first, second, low, high):
     step = pl.program_id(0)
 
@@ -271,9 +320,10 @@
 
 
 def stencil_kernel(
-    place, h, u, v, h_west, u_west, v_west, h_east, u_east, v_east, west, east, first, second, table,
-    u_out, v_out, h_first, h_second, own_h, own_u, own_v, terms, whole,
+    polar, place, h, u, v, h_west, u_west, v_west, h_east, u_east, v_east, west, east, first, second, table,
+    *refs,
 ):
+    outs, (terms, whole) = refs[:-2], refs[-2:]
     step = pl.program_id(0)
     lane = lanes_of((LEV, ROWS))
     edges = (lane == 0) | (lane == ROWS - 1)
@@ -356,24 +406,23 @@
     )
     several((groups - 1) * AHEAD, carry, [field[...] for field in (h_east, u_east, v_east)])
 
-    @pl.when(place[3] == 0)
-    def _():
-        for f, out in enumerate((own_h, own_u, own_v)):
+    if not polar:
+        for f, out in enumerate(outs):
             out[...] = whole[f]
-
-    @pl.when(place[3] == 1)
-    def _():
-        def turned(f):
-            return jnp.transpose(whole[f].reshape(CHUNK, LEV, ROWS), (1, 0, 2))
-
-        height = turned(0)
-        h_first[...] = height[: LEV // 2]
-        h_second[...] = height[LEV // 2 :]
-        u_out[...] = turned(1)
-        v_out[...] = turned(2)
-
-
-def stencil(place, height, u_wind, v_wind, west, east, first, second, tables):
+        return
+
+    def turned(f):
+        return jnp.transpose(whole[f].reshape(CHUNK, LEV, ROWS), (1, 0, 2))
+
+    uv_out, h_first, h_second = outs
+    height = turned(0)
+    h_first[...] = height[: LEV // 2]
+    h_second[...] = height[LEV // 2 :]
+    uv_out[:, 0] = turned(1)
+    uv_out[:, 1] = turned(2)
+
+
+def stencil(polar, place, height, u_wind, v_wind, west, east, first, second, tables):
     block = pl.BlockSpec((CHUNK * LEV, ROWS), lambda i, s: (i, 0))
     one_west = pl.BlockSpec((LEV, ROWS), lambda i, s: (jnp.maximum(i * CHUNK - 1, 0), 0))
     one_east = pl.BlockSpec(
@@ -381,19 +430,14 @@
     )
     side = pl.BlockSpec((3, LEV, ROWS), lambda i, s: (0, 0, 0))
     edge = pl.BlockSpec((4, 2, LEV, ROWS), lambda i, s: (0, 0, 0, 0))
-    kept = pl.BlockSpec((CHUNK * LEV, ROWS), lambda i, s: (jnp.where(s[3] == 0, i, 0), 0))
-
-    def sent(levels):
-        return pl.BlockSpec(
-            (levels, CHUNK, ROWS), lambda i, s: (0, jnp.where(s[3] == 1, i, 0), 0)
-        )
-
+    sent = pl.BlockSpec((LEV // 2, CHUNK, ROWS), lambda i, s: (0, i, 0))
+    pair = pl.BlockSpec((LEV, 2, CHUNK, ROWS), lambda i, s: (0, 0, i, 0))
     own = jax.ShapeDtypeStruct((COLS * LEV, ROWS), jnp.float32)
-    full = jax.ShapeDtypeStruct((LEV, TALL, ROWS), jnp.float32)
+    full = jax.ShapeDtypeStruct((LEV, 2, TALL, ROWS), jnp.float32)
     half = jax.ShapeDtypeStruct((LEV // 2, TALL, ROWS), jnp.float32)
     fields = (height, u_wind, v_wind)
     return pl.pallas_call(
-        stencil_kernel,
+        functools.partial(stencil_kernel, polar),
         grid_spec=pltpu.PrefetchScalarGridSpec(
             num_scalar_prefetch=1,
             grid=(pl.cdiv(COLS, CHUNK),),
@@ -403,13 +447,13 @@
             + [side] * 2
             + [edge] * 2
             + [pl.BlockSpec((1, 8, ROWS), lambda i, s: (s[0], 0, 0))],
-            out_specs=[sent(LEV), sent(LEV), sent(LEV // 2), sent(LEV // 2)] + [kept] * 3,
+            out_specs=[pair, sent, sent] if polar else [block] * 3,
             scratch_shapes=[
                 pltpu.VMEM((3, 2, 2, LEV, ROWS), jnp.float32),
                 pltpu.VMEM((3, CHUNK * LEV, ROWS), jnp.float32),
             ],
         ),
-        out_shape=[full, full, half, half, own, own, own],
+        out_shape=[full, half, half] if polar else [own] * 3,
         compiler_params=pltpu.CompilerParams(vmem_limit_bytes=58 * 1024 * 1024),
         cost_estimate=pl.CostEstimate(
             flops=60_000_000, bytes_accessed=9_000_000, transcendentals=0
@@ -417,42 +461,47 @@
     )(place, *fields, *fields, *fields, west, east, first, second, tables)
 
 
-def unpack_kernel(place, own, *refs):
-    parts, out = refs[:-1], refs[-1]
+def unpack_kernel(
+    place, own_u, own_v, own_h, uv, h_first, h_second, u_out, v_out, h_out
+):
+    def turned(block):
+        return jnp.transpose(block, (1, 0, 2)).reshape(SOME * LEV, ROWS)
 
     @pl.when(place[3] == 1)
     def _():
-        whole = jnp.concatenate([x[...] for x in parts], 0)
-        out[...] = jnp.transpose(whole, (1, 0, 2)).reshape(SOME * LEV, ROWS)
+        u_out[...] = turned(uv[:, 0])
+        v_out[...] = turned(uv[:, 1])
+        h_out[...] = turned(jnp.concatenate([h_first[...], h_second[...]], 0))
 
     @pl.when(place[3] == 0)
     def _():
-        out[...] = own[...]
-
-
-def unpack(place, own, *parts):
+        u_out[...] = own_u[...]
+        v_out[...] = own_v[...]
+        h_out[...] = own_h[...]
+
+
+def unpack(place, own_u, own_v, own_h, uv, h_first, h_second):
     def pick(polar):
         return lambda i, s: jnp.where(s[3] == polar, i, 0)
 
     kept, used = pick(0), pick(1)
+    half = pl.BlockSpec((LEV // 2, SOME, ROWS), lambda i, s: (0, used(i, s), 0))
     return pl.pallas_call(
         unpack_kernel,
         grid_spec=pltpu.PrefetchScalarGridSpec(
             num_scalar_prefetch=1,
             grid=(pl.cdiv(COLS, SOME),),
-            in_specs=[pl.BlockSpec((SOME * LEV, ROWS), lambda i, s: (kept(i, s), 0))]
-            + [
-                pl.BlockSpec((x.shape[0], SOME, ROWS), lambda i, s: (0, used(i, s), 0))
-                for x in parts
-            ],
-            out_specs=pl.BlockSpec((SOME * LEV, ROWS), lambda i, s: (i, 0)),
-        ),
-        out_shape=jax.ShapeDtypeStruct((COLS * LEV, ROWS), jnp.float32),
+            in_specs=[pl.BlockSpec((SOME * LEV, ROWS), lambda i, s: (kept(i, s), 0))] * 3
+            + [pl.BlockSpec((LEV, 2, SOME, ROWS), lambda i, s: (0, 0, used(i, s), 0))]
+            + [half] * 2,
+            out_specs=[pl.BlockSpec((SOME * LEV, ROWS), lambda i, s: (i, 0))] * 3,
+        ),
+        out_shape=[jax.ShapeDtypeStruct((COLS * LEV, ROWS), jnp.float32)] * 3,
         compiler_params=pltpu.CompilerParams(vmem_limit_bytes=58 * 1024 * 1024),
         cost_estimate=pl.CostEstimate(
-            flops=0, bytes_accessed=8 * COLS * LEV * ROWS, transcendentals=0
-        ),
-    )(place, own, *parts)
+            flops=0, bytes_accessed=24 * COLS * LEV * ROWS, transcendentals=0
+        ),
+    )(place, own_u, own_v, own_h, uv, h_first, h_second)
 
 
 def filter_kernel(place, x, matrix, columns, table, out, spectra, waves):
@@ -480,7 +529,7 @@
         return carry
 
     full = COLS // 16
-    lax.fori_loop(0, full, fill, 0)
+    lax.fori_loop(0, full, fill, 0, unroll=full)
     empty = jnp.zeros((HALF - COLS, ROWS), jnp.float32)
     tail = pl.ds(16 * full, COLS % 16)
     gather(16 * full, [jnp.concatenate([x[p, tail, :], empty], 0) for p in range(16)])
@@ -516,24 +565,24 @@
             out[p, rows, :] = value
         return carry
 
-    lax.fori_loop(0, TALL // 8, give, 0)
+    lax.fori_loop(0, TALL // 8, give, 0, unroll=TALL // 8)
 
 
 def polar_filter(place, x, tables):
     matrix, columns = fourier_tables()
-    whole = pl.BlockSpec(x.shape, lambda i, s: (0, 0, 0))
+    field = pl.BlockSpec((LEV, None, TALL, ROWS), lambda i, s: (0, i, 0, 0))
     return pl.pallas_call(
         filter_kernel,
         grid_spec=pltpu.PrefetchScalarGridSpec(
             num_scalar_prefetch=1,
-            grid=(1,),
+            grid=(x.shape[1],),
             in_specs=[
-                whole,
+                field,
                 pl.BlockSpec(matrix.shape, lambda i, s: (0, 0)),
                 pl.BlockSpec(columns.shape, lambda i, s: (0, 0)),
                 pl.BlockSpec((1, 8, ROWS), lambda i, s: (s[0], 0, 0)),
             ],
-            out_specs=whole,
+            out_specs=field,
             scratch_shapes=[
                 pltpu.VMEM((9, 2, HALF, 2 * ROWS), jnp.bfloat16),
                 pltpu.VMEM((9, 2, HALF, ROWS), jnp.float32),
@@ -542,7 +591,7 @@
         out_shape=jax.ShapeDtypeStruct(x.shape, jnp.float32),
         compiler_params=pltpu.CompilerParams(vmem_limit_bytes=58 * 1024 * 1024),
         cost_estimate=pl.CostEstimate(
-            flops=216 * HALF * HALF * ROWS, bytes_accessed=3_500_000, transcendentals=0
+            flops=216 * HALF * HALF * ROWS * x.shape[1], bytes_accessed=3_500_000 * x.shape[1], transcendentals=0
         ),
     )(place, x, jnp.asarray(matrix), jnp.asarray(columns), tables)
 
@@ -565,6 +614,14 @@
 
 def partner(band, pairs):
     return sum(jnp.where(band == other, polar, 0) for polar, other in pairs).astype(jnp.int32)
+
+
+def unused(like):
+    return pl.pallas_call(
+        lambda out: None,
+        out_specs=pl.BlockSpec(memory_space=pl.ANY),
+        out_shape=jax.ShapeDtypeStruct(like.shape, like.dtype),
+    )()
 
 
 def shards(u_wind, v_wind, height):
@@ -576,67 +633,61 @@
     fields = [jnp.swapaxes(x, 0, 1) for x in (height, u_wind, v_wind)]
     flat = [x.reshape(COLS * LEV, ROWS) for x in fields]
     east_to = [(i, (i + 1) % N_LON) for i in range(N_LON)]
-    west = lax.ppermute(jnp.stack([x[COLS - 1] for x in fields]), "lon", east_to)
-    east = lax.ppermute(jnp.stack([x[0] for x in fields]), "lon", [(j, i) for i, j in east_to])
+    initial, last = ends(flat)
+    west = lax.ppermute(last, "lon", east_to)
+    east = lax.ppermute(initial, "lon", [(j, i) for i, j in east_to])
     first, second = pack(place, *flat)
-    spot = lax.broadcasted_iota(jnp.int32, first.shape, 1) * ROWS + lax.broadcasted_iota(
-        jnp.int32, first.shape, 3
-    )
-
-    def widened(value, is_north):
-        def edge(side):
-            north = [side[f, :, ROWS - 1 - (f == 3) :][:, :1] for f in range(3)]
-            north.append(side[2, :, ROWS - 2 : ROWS - 1])
-            south = [side[min(f, 2), :, :1] for f in range(4)]
-            return jnp.where(is_north, jnp.stack(north), jnp.stack(south))[:, None]
-
-        value = jnp.where(spot == 0, edge(west), value)
-        return jnp.where(spot == COLS + 1, edge(east), value)
-
+    first, second = widen(place, first, second, west, east)
     swap = [(i, i ^ 1) for i in range(N_LAT)]
-    first = lax.ppermute(widened(first, even), "lat", swap)
+    first = lax.ppermute(first, "lat", swap)
     routes = [(lon, i, lon, i + 1) for lon in range(N_LON) for i in range(1, N_LAT - 1, 2)]
     routes += [(lon, i + 1, lon, i) for lon, i, _, _ in routes]
     routes += [
         (lon, i, (lon + N_LON // 2) % N_LON, i) for lon in range(N_LON) for i in (0, N_LAT - 1)
     ]
     second = lax.ppermute(
-        widened(second, jnp.logical_not(even)),
+        second,
         AXES,
         [(a * N_LAT + b, c * N_LAT + d) for a, b, c, d in routes],
     )
-    u, v, h_first, h_second, own_h, own_u, own_v = stencil(
-        place, *flat, west, east, first, second, tables
-    )
-
     def exchange(value):
         return lax.all_to_all(value, "lon", split_axis=0, concat_axis=0, tiled=True)
 
-    def keep(u, v_circles, h_first, h_second):
-        u_circles = exchange(u)
-        v = exchange(polar_filter(place, v_circles, tables))
-        return v, polar_filter(place, u_circles, tables)
-
-    def help_out(u, v_circles, h_first, h_second):
+    def keep(circles, h_first, h_second):
+        return polar_filter(place, circles, tables), unused(h_first), unused(h_second)
+
+    def help_out(circles, h_first, h_second):
         circles = exchange(jnp.concatenate([h_first, h_second], 0))
         lender = jnp.where(
             lax.axis_index("lon") < N_LON // 2, partner(band, BESIDE), partner(band, BEYOND)
         )
-        smooth = polar_filter(lender.reshape(1), circles, tables)
-        return exchange(smooth), smooth
+        h = exchange(polar_filter(lender.reshape(1), circles[:, None], tables)[:, 0])
+        return unused(uv), h[: LEV // 2], h[LEV // 2 :]
+
+    inputs = (place, *flat, west, east, first, second, tables)
+    whole = jax.ShapeDtypeStruct((LEV, 2, TALL, ROWS), jnp.float32)
+    half = jax.ShapeDtypeStruct((LEV // 2, TALL, ROWS), jnp.float32)
+    own = jax.ShapeDtypeStruct((COLS * LEV, ROWS), jnp.float32)
+    uv, h_first, h_second = lax.cond(
+        is_polar,
+        lambda *inputs: tuple(stencil(True, *inputs)),
+        lambda *inputs: (unused(whole), unused(half), unused(half)),
+        *inputs,
+    )
 
     h_first = lax.ppermute(h_first, AXES, lent(BESIDE, 0))
     h_second = lax.ppermute(h_second, AXES, lent(BEYOND, N_LON // 2))
-    v_circles = exchange(v)
-    v_or_h, u = lax.cond(is_polar, keep, help_out, u, v_circles, h_first, h_second)
-    h_first = lax.ppermute(v_or_h[: LEV // 2], AXES, returned(BESIDE, 0))
-    h_second = lax.ppermute(v_or_h[LEV // 2 :], AXES, returned(BEYOND, N_LON // 2))
-    u = exchange(u)
-    result = (
-        unpack(place, own_u, u),
-        unpack(place, own_v, v_or_h),
-        unpack(place, own_h, h_first, h_second),
+    circles, own_h, own_u, own_v = lax.cond(
+        is_polar,
+        lambda uv, *inputs: (exchange(uv), unused(own), unused(own), unused(own)),
+        lambda uv, *inputs: (unused(uv), *stencil(False, *inputs)),
+        uv, *inputs,
     )
+    circles, h_first, h_second = lax.cond(is_polar, keep, help_out, circles, h_first, h_second)
+    h_first = lax.ppermute(h_first, AXES, returned(BESIDE, 0))
+    h_second = lax.ppermute(h_second, AXES, returned(BEYOND, N_LON // 2))
+    uv = lax.cond(is_polar, exchange, unused, circles)
+    result = unpack(place, own_u, own_v, own_h, uv, h_first, h_second)
     return tuple(jnp.swapaxes(x.reshape(COLS, LEV, ROWS), 0, 1) for x in result)
 
 

time: 160 us -> 141 us (0.88)
  blocking collectives: 0 us -> 41.4 us
  waiting for transfers between devices: 69.6 us -> 44.9 us
  starting transfers between devices: 40.4 us -> 20.3 us
  Pallas kernels: 39.1 us -> 31.1 us
  local copies, waits for them, and re-layouts: 8.1 us -> 1.69 us
    all_to_all x0 -> x1, blocking collectives: none -> 41.4 us  [exchange(): return lax.all_to_all(value, 'lon', split_axis=0, concat_axis=0, tiled=True)]
    ppermute x6, waiting for transfers between devices: 26.8 us -> 5.01 us  [the longest x1 2.27 us: shards(): h_first = lax.ppermute(h_first, AXES, returned(BESIDE, 0))]
    all_to_all x4 -> x1, starting transfers between devices: 23.1 us -> 7.84 us  [exchange(): return lax.all_to_all(value, 'lon', split_axis=0, concat_axis=0, tiled=True)]
    ppermute x1, waiting for transfers between devices: 14.9 us -> 0.01 us  [shards(): h_first = lax.ppermute(h_first, AXES, lent(BESIDE, 0))]
    all_to_all x4 -> x1, waiting for transfers between devices: 26.5 us -> 39.9 us  [exchange(): return lax.all_to_all(value, 'lon', split_axis=0, concat_axis=0, tiled=True)]
    pallas_call x2 -> x1, Pallas kernels: 15.2 us -> 9.79 us  [polar_filter(): pl.pallas_call(filter_kernel, grid_spec=pltpu.PrefetchScalarGridSpec(num_...]
    ppermute x1, starting transfers between devices: 7.48 us -> 2.18 us  [shards(): h_first = lax.ppermute(h_first, AXES, lent(BESIDE, 0))]
    slice x8 -> x0, local copies, waits for them, and re-layouts: 4.22 us -> none  [the longest x3 2.15 us: shards(): x[0]]
  transfers between devices with their start and end apart: 12 -> 9, of which waited for: 7 -> 5; matrix products, arithmetic and copies ran while one was open for 1% -> 0% of each run, Pallas kernels for 16% -> 3%
where the time goes in v3:
time: 141 us; the launch traced here: 140 us
  waiting for transfers between devices  44.9 us (32%)
  blocking collectives  41.4 us (29%)
  Pallas kernels  31.1 us (22%)
  starting transfers between devices  20.3 us (14%)
  local copies, waits for them, and re-layouts  1.69 us (1%)
    all_to_all x1, blocking collectives, exchange(): return lax.all_to_all(value, 'lon', split_axis=0, concat_axis=0, tiled=True)  41.4 us
    all_to_all x1, waiting for transfers between devices, exchange(): return lax.all_to_all(value, 'lon', split_axis=0, concat_axis=0, tiled=True)  39.9 us
    pallas_call x1, Pallas kernels, polar_filter(): pl.pallas_call(filter_kernel, grid_spec=pltpu.PrefetchScalarGridSpec(num_...  9.79 us
    pallas_call x1, Pallas kernels, stencil(): pl.pallas_call(functools.partial(stencil_kernel, polar), grid_spec=pltpu....  8.52 us
    all_to_all x1, starting transfers between devices, exchange(): return lax.all_to_all(value, 'lon', split_axis=0, concat_axis=0, tiled=True)  7.84 us
    pallas_call x1, Pallas kernels, unpack(): pl.pallas_call(unpack_kernel, grid_spec=pltpu.PrefetchScalarGridSpec(num_...  5.42 us
    pallas_call x1, Pallas kernels, pack(): pl.pallas_call(pack_kernel, grid_spec=pltpu.PrefetchScalarGridSpec(num_sc...  3.72 us
  transfers between devices with their start and end apart: 9, of which 5 were waited for; matrix products, arithmetic and copies ran while one was open for 0% of the time, Pallas kernels for 3%

profile of v3, /device:TPU:1, one launch (start us, length us, event | category | flops | bytes accessed | tf_op | source)
XLA Modules:
  0.0 140.4 jit_solution(2372759670326569988)
XLA Ops:
  0.7 1.5 %shard_map.85 = (f32[3,16,128]{2,1,0:T(8,128)}, f32[3,16,128]{2,1,0:T(8,128)}) custom-call(f32[2880,128]{1,0:T(8,128)} %bitcast.26, f32[2880,128]{1,0:T(8,128)} %bitcast.31, f32[2880,128]{1,0:T(8,128)} %bitcast.36, f32[2880,128]{1,0:T(8,128)} %bitcast.27, f32[2880,128]{1,0:T(8,128)} %bitcast.32, f32[2880,128]{1,0:T(8,128)} %bitcast.37), custom_call_target="tpu_custom_call" | custom-call | tf_op jit(solution)/shard_map/pallas_call | solution.py:180
  2.2 2.6 %collective-permute-start = (f32[3,16,128]{2,1,0:T(8,128)}, f32[3,16,128]{2,1,0:T(8,128)S(1)}, u32[]{:S(2)}, u32[]{:S(2)}) collective-permute-start(f32[3,16,128]{2,1,0:T(8,128)} %get-tuple-element.125), channel_id=1, source_target_pairs={{0,8},{8,16},{16,24},{24,32},{32,40},{40,48},{48,56},{56,64},{64,7... | collective-permute-start | bytes 73736 | tf_op jit(solution)/shard_map/ppermute | solution.py:637
  4.9 3.7 %shard_map.86 = (f32[4,2,16,128]{3,2,1,0:T(8,128)}, f32[4,2,16,128]{3,2,1,0:T(8,128)}) custom-call(s32[5]{0:T(128)S(1)} %stack.35.place, f32[2880,128]{1,0:T(8,128)S(1)} %bitcast.28, f32[2880,128]{1,0:T(8,128)S(1)} %bitcast.33, f32[2880,128]{1,0:T(8,128)} %bitcast.38), custom_call_target="tpu_custom_call" | custom-call | bytes 4700000 | tf_op jit(solution)/shard_map/pallas_call | solution.py:272
  8.6 2.1 %shard_map.87 = (f32[4,2,16,128]{3,2,1,0:T(8,128)}, f32[4,2,16,128]{3,2,1,0:T(8,128)}) custom-call(s32[5]{0:T(128)S(1)} %stack.35.place, f32[4,2,16,128]{3,2,1,0:T(8,128)} %get-tuple-element.127.first, f32[4,2,16,128]{3,2,1,0:T(8,128)} %get-tuple-element.128.second, f32[3,16,128]{2,1,0:T(8,128)S(1)} %collective-permute-done.west, ...), custom_call_target="tpu_custom_call" | custom-call | tf_op jit(solution)/shard_map/pallas_call | solution.py:210
  10.8 1.6 %collective-permute-start.2 = (f32[4,2,16,128]{3,2,1,0:T(8,128)}, f32[4,2,16,128]{3,2,1,0:T(8,128)S(1)}, u32[]{:S(2)}, u32[]{:S(2)}) collective-permute-start(f32[4,2,16,128]{3,2,1,0:T(8,128)} %get-tuple-element.129), channel_id=1, source_target_pairs={{0,1},{1,0},{2,3},{3,2},{4,5},{5,4},{6,7},{7,6},{8,9},{9,8},{10,11... | collective-permute-start | bytes 196616 | tf_op jit(solution)/shard_map/ppermute | solution.py:642
  12.4 1.3 collective-permute-start.3
  14.3 1.5 %collective-permute-done.3 = f32[4,2,16,128]{3,2,1,0:T(8,128)S(1)} collective-permute-done((f32[4,2,16,128]{3,2,1,0:T(8,128)}, f32[4,2,16,128]{3,2,1,0:T(8,128)S(1)}, u32[]{:S(2)}, u32[]{:S(2)}) %collective-permute-start.3) | collective-permute-done | bytes 65568 | tf_op jit(solution)/shard_map/ppermute | solution.py:648
  15.7 8.5 %conditional.4 = (f32[8,184,128]{2,1,0:T(8,128)}, f32[8,184,128]{2,1,0:T(8,128)}, f32[16,2,184,128]{3,2,1,0:T(8,128)}) conditional(s32[]{:T(128)} %convert_element_type.2, () %tuple.47, (s32[5]{0:T(128)S(1)}, f32[2880,128]{1,0:T(8,128)S(1)}, f32[2880,128]{1,0:T(8,128)S(1)}, f32[2880,128]{1,0:T(8,128)}, f32[3,16,128]{2,1,0:T(8,128)S(1)}, ...), branch_computations={%region_0.1_spmd, %region_1.2_spmd} | conditional | flops 60000000 | bytes 9000024 | solution.py:671
  15.7 8.5 %branch_1_fun.7 = (f32[16,2,184,128]{3,2,1,0:T(8,128)}, f32[8,184,128]{2,1,0:T(8,128)}, f32[8,184,128]{2,1,0:T(8,128)}) custom-call(s32[5]{0:T(128)S(1)} %get-tuple-element.68.place, f32[2880,128]{1,0:T(8,128)S(1)} %get-tuple-element.69.h.h_west.h_east, f32[2880,128]{1,0:T(8,128)S(1)} %get-tuple-element.70.u.u_west.u_east, ...), custom_call_target="tpu_custom_call" | custom-call | flops 60000000 | bytes 9000000 | tf_op jit(solution)/shard_map/cond/branch_1_fun/pallas_call | solution.py:439
  24.3 2.2 %collective-permute-start.4 = (f32[8,184,128]{2,1,0:T(8,128)}, f32[8,184,128]{2,1,0:T(8,128)}, u32[]{:S(2)}, u32[]{:S(2)}) collective-permute-start(f32[8,184,128]{2,1,0:T(8,128)} %get-tuple-element.135), channel_id=1, source_target_pairs={{0,3},{1,2},{6,5},{7,4},{8,11},{9,10},{14,13},{15,12},{16,19},{17,... | collective-permute-start | bytes 2261000 | tf_op jit(solution)/shard_map/ppermute | solution.py:678
  26.4 2.2 %collective-permute-start.5 = (f32[8,184,128]{2,1,0:T(8,128)}, f32[8,184,128]{2,1,0:T(8,128)}, u32[]{:S(2)}, u32[]{:S(2)}) collective-permute-start(f32[8,184,128]{2,1,0:T(8,128)} %get-tuple-element.136), channel_id=1, source_target_pairs={{0,68},{1,69},{6,66},{7,67},{8,76},{9,77},{14,74},{15,75},{16,84},... | collective-permute-start | bytes 2261000 | tf_op jit(solution)/shard_map/ppermute | solution.py:679
  28.6 49.3 %conditional.5 = (f32[16,2,184,128]{3,2,1,0:T(8,128)}, f32[2880,128]{1,0:T(8,128)}, f32[2880,128]{1,0:T(8,128)}, f32[2880,128]{1,0:T(8,128)}) conditional(s32[]{:T(128)} %convert_element_type.2, (s32[5]{0:T(128)S(1)}, f32[2880,128]{1,0:T(8,128)S(1)}, f32[2880,128]{1,0:T(8,128)S(1)}, f32[2880,128]{1,0:T(8,128)}, f32[3,16,128]{2,1,0:T(8,128)S(1)}, ...), branch_computations={%region_2.3_spmd, %region_3.4_spmd} | conditional | flops 60000000 | bytes 21102684 | solution.py:680
  28.6 7.8 %all-to-all-start = ((f32[16,2,184,128]{3,2,1,0:T(8,128)}), f32[16,2,184,128]{3,2,1,0:T(8,128)S(1)}, u32[]{:S(2)}, u32[]{:S(2)}) async-start(f32[16,2,184,128]{3,2,1,0:T(8,128)} %param.3), calls=%async_computation | async-start | bytes 6029312 | tf_op jit(solution)/shard_map/cond/branch_1_fun/all_to_all | solution.py:654
  36.5 39.9 %all-to-all-done = f32[16,2,184,128]{3,2,1,0:T(8,128)S(1)} async-done(((f32[16,2,184,128]{3,2,1,0:T(8,128)}), f32[16,2,184,128]{3,2,1,0:T(8,128)S(1)}, u32[]{:S(2)}, u32[]{:S(2)}) %all-to-all-start) | async-done | bytes 3014688 | tf_op jit(solution)/shard_map/cond/branch_1_fun/all_to_all | solution.py:654
  76.3 1.6 %copy-done.2 = f32[16,2,184,128]{3,2,1,0:T(8,128)} copy-done((f32[16,2,184,128]{3,2,1,0:T(8,128)}, f32[16,2,184,128]{3,2,1,0:T(8,128)S(1)}, u32[]{:S(2)}) %copy-start.2) | copy-done | bytes 3014680 | tf_op jit(solution)/shard_map/cond
  77.9 10.0 %conditional.6 = (f32[8,184,128]{2,1,0:T(8,128)}, f32[8,184,128]{2,1,0:T(8,128)}, f32[16,2,184,128]{3,2,1,0:T(8,128)S(1)}) conditional(s32[]{:T(128)} %convert_element_type.2, (s32[]{:T(128)}, f32[8,184,128]{2,1,0:T(8,128)}, f32[8,184,128]{2,1,0:T(8,128)}, bf16[768,192]{1,0:T(8,128)(2,1)}, f32[192,128]{1,0:T(8,128)S(1)}, ...), branch_computations={%region_4.5_spmd, %region_5.6_spmd} | conditional | flops 2038431744 | bytes 25782600 | solution.py:686
  78.1 9.8 %branch_1_fun.13 = f32[16,2,184,128]{3,2,1,0:T(8,128)S(1)} custom-call(s32[5]{0:T(128)S(1)} %get-tuple-element.98.place, f32[16,2,184,128]{3,2,1,0:T(8,128)} %get-tuple-element.99.x, bf16[768,192]{1,0:T(8,128)(2,1)} %get-tuple-element.100.matrix, f32[192,128]{1,0:T(8,128)S(1)} %get-tuple-element.101.columns, f32[8,8,128]{2,1,0:T(8,128)S(1)} %get-tuple-element.102.table), custom_call_target="tpu_custom_call" | custom-call | flops 2038431744 | bytes 7000000 | tf_op jit(solution)/shard_map/cond/branch_1_fun/pallas_call | solution.py:574
  88.0 1.3 collective-permute-start.6
  89.3 1.3 collective-permute-start.7
  90.6 41.4 %conditional.7 = (f32[16,2,184,128]{3,2,1,0:T(8,128)}) conditional(s32[]{:T(128)} %convert_element_type.2, () %tuple.48, f32[16,2,184,128]{3,2,1,0:T(8,128)S(1)} %get-tuple-element.138), branch_computations={%region_6.7_spmd, %region_7.8_spmd} | conditional | bytes 6029320 | solution.py:689
  90.6 41.4 %all_to_all.16 = f32[16,2,184,128]{3,2,1,0:T(8,128)} all-to-all(f32[16,2,184,128]{3,2,1,0:T(8,128)S(1)} %param.7), channel_id=1, replica_groups=mesh['lon'=16,'lat'=8] {'lon'}, dimensions={0} | all-to-all | bytes 6029312 | tf_op jit(solution)/shard_map/cond/branch_1_fun/all_to_all | solution.py:654
  132.0 2.3 %collective-permute-done.6.h_first = f32[8,184,128]{2,1,0:T(8,128)} collective-permute-done((f32[8,184,128]{2,1,0:T(8,128)}, f32[8,184,128]{2,1,0:T(8,128)}, u32[]{:S(2)}, u32[]{:S(2)}) %collective-permute-start.6) | collective-permute-done | bytes 753696 | tf_op jit(solution)/shard_map/ppermute | solution.py:687
  134.2 0.7 collective-permute-done.7.h_second
  134.9 5.4 %shard_map.88 = (f32[2880,128]{1,0:T(8,128)}, f32[2880,128]{1,0:T(8,128)}, f32[2880,128]{1,0:T(8,128)}) custom-call(s32[5]{0:T(128)S(1)} %stack.35.place, f32[2880,128]{1,0:T(8,128)} %get-tuple-element.132.own_u, f32[2880,128]{1,0:T(8,128)} %get-tuple-element.133.own_v, f32[2880,128]{1,0:T(8,128)} %get-tuple-element.134.own_h, ...), custom_call_target="tpu_custom_call" | custom-call | bytes 8847360 | tf_op jit(solution)/shard_map/pallas_call | solution.py:489
  (21 shorter events, 0.7 us)
Async XLA Ops:
  0.6 4.3 %copy-start = (f32[16,180,128]{2,0,1:T(8,128)S(1)}, f32[16,180,128]{2,0,1:T(8,128)}, u32[]{:S(2)}) copy-start(f32[16,180,128]{2,0,1:T(8,128)} %param.16) | copy-start | bytes 4423684
  0.6 4.3 %copy-start.1 = (f32[16,180,128]{2,0,1:T(8,128)S(1)}, f32[16,180,128]{2,0,1:T(8,128)}, u32[]{:S(2)}) copy-start(f32[16,180,128]{2,0,1:T(8,128)} %param.14) | copy-start | bytes 4423684
  2.2 6.4 %collective-permute-start = (f32[3,16,128]{2,1,0:T(8,128)}, f32[3,16,128]{2,1,0:T(8,128)S(1)}, u32[]{:S(2)}, u32[]{:S(2)}) collective-permute-start(f32[3,16,128]{2,1,0:T(8,128)} %get-tuple-element.125), channel_id=1, source_target_pairs={{0,8},{8,16},{16,24},{24,32},{32,40},{40,48},{48,56},{56,64},{64,7... | collective-permute-start | bytes 73736 | tf_op jit(solution)/shard_map/ppermute | solution.py:637
  4.8 3.8 %collective-permute-start.1 = (f32[3,16,128]{2,1,0:T(8,128)}, f32[3,16,128]{2,1,0:T(8,128)S(1)}, u32[]{:S(2)}, u32[]{:S(2)}) collective-permute-start(f32[3,16,128]{2,1,0:T(8,128)} %get-tuple-element.126), channel_id=1, source_target_pairs={{8,0},{16,8},{24,16},{32,24},{40,32},{48,40},{56,48},{64,56},{72,6... | collective-permute-start | bytes 73736 | tf_op jit(solution)/shard_map/ppermute | solution.py:638
  4.9 10.8 %copy-start.4 = (f32[8,8,128]{2,1,0:T(8,128)S(1)}, f32[8,8,128]{2,1,0:T(8,128)}, u32[]{:S(2)}) copy-start(f32[8,8,128]{2,1,0:T(8,128)} %constant.52.clone) | copy-start | bytes 98308
  10.8 3.5 %collective-permute-start.2 = (f32[4,2,16,128]{3,2,1,0:T(8,128)}, f32[4,2,16,128]{3,2,1,0:T(8,128)S(1)}, u32[]{:S(2)}, u32[]{:S(2)}) collective-permute-start(f32[4,2,16,128]{3,2,1,0:T(8,128)} %get-tuple-element.129), channel_id=1, source_target_pairs={{0,1},{1,0},{2,3},{3,2},{4,5},{5,4},{6,7},{7,6},{8,9},{9,8},{10,11... | collective-permute-start | bytes 196616 | tf_op jit(solution)/shard_map/ppermute | solution.py:642
  12.4 3.3 %collective-permute-start.3 = (f32[4,2,16,128]{3,2,1,0:T(8,128)}, f32[4,2,16,128]{3,2,1,0:T(8,128)S(1)}, u32[]{:S(2)}, u32[]{:S(2)}) collective-permute-start(f32[4,2,16,128]{3,2,1,0:T(8,128)} %get-tuple-element.130), channel_id=1, source_target_pairs={{1,2},{3,4},{5,6},{9,10},{11,12},{13,14},{17,18},{19,20},{21,22},{... | collective-permute-start | bytes 196616 | tf_op jit(solution)/shard_map/ppermute | solution.py:648
  24.3 53.7 %collective-permute-start.4 = (f32[8,184,128]{2,1,0:T(8,128)}, f32[8,184,128]{2,1,0:T(8,128)}, u32[]{:S(2)}, u32[]{:S(2)}) collective-permute-start(f32[8,184,128]{2,1,0:T(8,128)} %get-tuple-element.135), channel_id=1, source_target_pairs={{0,3},{1,2},{6,5},{7,4},{8,11},{9,10},{14,13},{15,12},{16,19},{17,... | collective-permute-start | bytes 2261000 | tf_op jit(solution)/shard_map/ppermute | solution.py:678
  26.4 51.5 %collective-permute-start.5 = (f32[8,184,128]{2,1,0:T(8,128)}, f32[8,184,128]{2,1,0:T(8,128)}, u32[]{:S(2)}, u32[]{:S(2)}) collective-permute-start(f32[8,184,128]{2,1,0:T(8,128)} %get-tuple-element.136), channel_id=1, source_target_pairs={{0,68},{1,69},{6,66},{7,67},{8,76},{9,77},{14,74},{15,75},{16,84},... | collective-permute-start | bytes 2261000 | tf_op jit(solution)/shard_map/ppermute | solution.py:679
  28.6 49.3 %copy-start.6 = (f32[192,128]{1,0:T(8,128)S(1)}, f32[192,128]{1,0:T(8,128)}, u32[]{:S(2)}) copy-start(f32[192,128]{1,0:T(8,128)} %constant.54.clone) | copy-start | bytes 294916
  28.6 47.7 %all-to-all-start = ((f32[16,2,184,128]{3,2,1,0:T(8,128)}), f32[16,2,184,128]{3,2,1,0:T(8,128)S(1)}, u32[]{:S(2)}, u32[]{:S(2)}) async-start(f32[16,2,184,128]{3,2,1,0:T(8,128)} %param.3), calls=%async_computation | async-start | bytes 6029312 | tf_op jit(solution)/shard_map/cond/branch_1_fun/all_to_all | solution.py:654
  76.3 1.6 %copy-start.2 = (f32[16,2,184,128]{3,2,1,0:T(8,128)}, f32[16,2,184,128]{3,2,1,0:T(8,128)S(1)}, u32[]{:S(2)}) copy-start(f32[16,2,184,128]{3,2,1,0:T(8,128)S(1)} %all-to-all-done) | copy-start | bytes 9043972 | tf_op jit(solution)/shard_map/cond
  88.0 46.3 %collective-permute-start.6 = (f32[8,184,128]{2,1,0:T(8,128)}, f32[8,184,128]{2,1,0:T(8,128)}, u32[]{:S(2)}, u32[]{:S(2)}) collective-permute-start(f32[8,184,128]{2,1,0:T(8,128)} %get-tuple-element.139), channel_id=1, source_target_pairs={{3,0},{2,1},{5,6},{4,7},{11,8},{10,9},{13,14},{12,15},{19,16},{18,... | collective-permute-start | bytes 2261000 | tf_op jit(solution)/shard_map/ppermute | solution.py:687
  89.3 45.7 %collective-permute-start.7 = (f32[8,184,128]{2,1,0:T(8,128)}, f32[8,184,128]{2,1,0:T(8,128)}, u32[]{:S(2)}, u32[]{:S(2)}) collective-permute-start(f32[8,184,128]{2,1,0:T(8,128)} %get-tuple-element.140), channel_id=1, source_target_pairs={{68,0},{69,1},{66,6},{67,7},{76,8},{77,9},{74,14},{75,15},{84,16},... | collective-permute-start | bytes 2261000 | tf_op jit(solution)/shard_map/ppermute | solution.py:688

commit v4 on v3

--- a/solution.py
+++ b/solution.py
@@ -19,9 +19,9 @@
 HALF = 192
 TALL = 184
 PACK = 90
-CHUNK = 48
+CHUNK = 64
 SOME = 96
-AHEAD = 16
+AHEAD = 32
 AXES = ("lon", "lat")
 
 GRAV_ZONAL = 0.3
@@ -167,55 +167,6 @@
     return lax.broadcasted_iota(jnp.int32, shape, len(shape) - 1)
 
 
-def ends_kernel(*refs):
-    for f in range(3):
-        refs[6][f] = refs[f][...]
-        refs[7][f] = refs[3 + f][...]
-
-
-def ends(fields):
-    first = pl.BlockSpec((LEV, ROWS), lambda i: (0, 0))
-    last = pl.BlockSpec((LEV, ROWS), lambda i: (COLS - 1, 0))
-    out = pl.BlockSpec((3, LEV, ROWS), lambda i: (0, 0, 0))
-    return pl.pallas_call(
-        ends_kernel,
-        grid=(1,),
-        in_specs=[first] * 3 + [last] * 3,
-        out_specs=[out] * 2,
-        out_shape=[jax.ShapeDtypeStruct((3, LEV, ROWS), jnp.float32)] * 2,
-    )(*fields, *fields)
-
-
-def widen_kernel(place, first, second, west, east, first_out, second_out):
-    even = place[4] == 1
-    lane = lanes_of((LEV, ROWS))
-    for f in range(4):
-        back = 2 if f == 3 else 1
-        side_west, side_east = west[min(f, 2)], east[min(f, 2)]
-        end = (COLS + 1) % ROWS
-        north = (pltpu.roll(side_west, back, 1), pltpu.roll(side_east, end + back, 1))
-        south = (side_west, pltpu.roll(side_east, end, 1))
-        for source, out, is_north in (
-            (first, first_out, even),
-            (second, second_out, jnp.logical_not(even)),
-        ):
-            at_west, at_east = (jnp.where(is_north, a, b) for a, b in zip(north, south))
-            out[f, 0] = jnp.where(lane == 0, at_west, source[f, 0])
-            out[f, 1] = jnp.where(lane == end, at_east, source[f, 1])
-
-
-def widen(place, first, second, west, east):
-    vmem = pl.BlockSpec(memory_space=pltpu.VMEM)
-    shape = jax.ShapeDtypeStruct(first.shape, jnp.float32)
-    return pl.pallas_call(
-        widen_kernel,
-        grid_spec=pltpu.PrefetchScalarGridSpec(
-            num_scalar_prefetch=1, grid=(1,), in_specs=[vmem] * 4, out_specs=[vmem] * 2
-        ),
-        out_shape=[shape] * 2,
-    )(place, first, second, west, east)
-
-
 def pack_kernel(place, h, u, v, first, second, low, high):
     step = pl.program_id(0)
 
@@ -283,7 +234,7 @@
     )(place, height, u_wind, v_wind)
 
 
-def rim_terms(place, first, second, table, terms):
+def rim_terms(place, first, second, table, terms, beside):
     even, at_north, at_south = place[4] == 1, place[1] == 1, place[2] == 1
     lane = lanes_of((LEV, ROWS))
 
@@ -317,20 +268,23 @@
             after = pltpu.roll(south[f], 1, 1)
             for odd in range(2):
                 terms[f, odd, part] = jnp.where(lane % 2 == odd, north[f], after)
+    last = pltpu.roll(u_n[1], (ROWS - 1 - COLS) % ROWS, 1)
+    beside[0] = jnp.where(lane == ROWS - 1, -turn_v * last, 0.0)
+    beside[1] = jnp.where(lane == 0, turn_u * pltpu.roll(v_s[0], ROWS - 1, 1), 0.0)
 
 
 def stencil_kernel(
-    polar, place, h, u, v, h_west, u_west, v_west, h_east, u_east, v_east, west, east, first, second, table,
+    polar, place, h, u, v, h_west, u_west, v_west, h_east, u_east, v_east, first, second, table,
     *refs,
 ):
-    outs, (terms, whole) = refs[:-2], refs[-2:]
+    outs, (terms, whole, beside, sides) = refs[:-4], refs[-4:]
     step = pl.program_id(0)
     lane = lanes_of((LEV, ROWS))
     edges = (lane == 0) | (lane == ROWS - 1)
 
     @pl.when(step == 0)
     def _():
-        rim_terms(place, first, second, table, terms)
+        rim_terms(place, first, second, table, terms, beside)
 
     zonal, turn_u, turn_v, cos_face, cos_south, _, diverge = (
         jnp.broadcast_to(table[0, i : i + 1, :], (LEV, ROWS)) for i in range(7)
@@ -386,7 +340,7 @@
                 blocks = [field[row(k + 1), :] for field in (h, u, v)]
             if n == (COLS - 1) % AHEAD:
                 is_last = step * CHUNK + k == COLS - 1
-                blocks = [jnp.where(is_last, east[f], blocks[f]) for f in range(3)]
+                blocks = [jnp.where(is_last, 0.0, block) for block in blocks]
             carry, results = update(k, (n + 1) % 2, carry, blocks)
             found.append(results)
         for n, results in enumerate(found):
@@ -395,7 +349,7 @@
         return carry
 
     before = [
-        jnp.where(step == 0, west[f], field[...]) for f, field in enumerate((h_west, u_west, v_west))
+        jnp.where(step == 0, 0.0, field[...]) for field in (h_west, u_west, v_west)
     ]
     here_v = v[row(0), :]
     v_south = south(here_v)
@@ -406,9 +360,30 @@
     )
     several((groups - 1) * AHEAD, carry, [field[...] for field in (h_east, u_east, v_east)])
 
+    @pl.when(step == 0)
+    def _():
+        mid_h, mid_u, mid_v = (field[row(0), :] for field in (h, u, v))
+        sides[1, 0] = DIFFUSION * mid_h
+        sides[1, 1] = turn_u * (mid_v + south(mid_v)) + beside[1] - zonal * mid_h + DIFFUSION * mid_u
+        sides[1, 2] = DIFFUSION * mid_v
+
+    @pl.when(step == pl.num_programs(0) - 1)
+    def _():
+        end = (COLS - 1) % CHUNK
+        mid_h, mid_u, mid_v = (field[row(end), :] for field in (h, u, v))
+        sides[0, 0] = diverge * mid_u + DIFFUSION * mid_h
+        sides[0, 1] = DIFFUSION * mid_u
+        sides[0, 2] = DIFFUSION * mid_v - turn_v * (mid_u + north(mid_u)) + beside[0]
+        if polar:
+            for f in range(3):
+                for side in range(2):
+                    whole[f, row(end + 1 + side), :] = sides[side, f]
+
     if not polar:
-        for f, out in enumerate(outs):
-            out[...] = whole[f]
+        for f in range(3):
+            outs[f][...] = whole[f]
+        for side in range(2):
+            outs[3 + side][...] = sides[side]
         return
 
     def turned(f):
@@ -422,7 +397,7 @@
     uv_out[:, 1] = turned(2)
 
 
-def stencil(polar, place, height, u_wind, v_wind, west, east, first, second, tables):
+def stencil(polar, place, height, u_wind, v_wind, first, second, tables):
     block = pl.BlockSpec((CHUNK * LEV, ROWS), lambda i, s: (i, 0))
     one_west = pl.BlockSpec((LEV, ROWS), lambda i, s: (jnp.maximum(i * CHUNK - 1, 0), 0))
     one_east = pl.BlockSpec(
@@ -435,6 +410,7 @@
     own = jax.ShapeDtypeStruct((COLS * LEV, ROWS), jnp.float32)
     full = jax.ShapeDtypeStruct((LEV, 2, TALL, ROWS), jnp.float32)
     half = jax.ShapeDtypeStruct((LEV // 2, TALL, ROWS), jnp.float32)
+    ends = jax.ShapeDtypeStruct((3, LEV, ROWS), jnp.float32)
     fields = (height, u_wind, v_wind)
     return pl.pallas_call(
         functools.partial(stencil_kernel, polar),
@@ -444,25 +420,26 @@
             in_specs=[block] * 3
             + [one_west] * 3
             + [one_east] * 3
-            + [side] * 2
             + [edge] * 2
             + [pl.BlockSpec((1, 8, ROWS), lambda i, s: (s[0], 0, 0))],
-            out_specs=[pair, sent, sent] if polar else [block] * 3,
+            out_specs=[pair, sent, sent] if polar else [block] * 3 + [side] * 2,
             scratch_shapes=[
                 pltpu.VMEM((3, 2, 2, LEV, ROWS), jnp.float32),
                 pltpu.VMEM((3, CHUNK * LEV, ROWS), jnp.float32),
+                pltpu.VMEM((2, LEV, ROWS), jnp.float32),
+                pltpu.VMEM((2, 3, LEV, ROWS), jnp.float32),
             ],
         ),
-        out_shape=[full, half, half] if polar else [own] * 3,
+        out_shape=[full, half, half] if polar else [own] * 3 + [ends] * 2,
         compiler_params=pltpu.CompilerParams(vmem_limit_bytes=58 * 1024 * 1024),
         cost_estimate=pl.CostEstimate(
             flops=60_000_000, bytes_accessed=9_000_000, transcendentals=0
         ),
-    )(place, *fields, *fields, *fields, west, east, first, second, tables)
+    )(place, *fields, *fields, *fields, first, second, tables)
 
 
 def unpack_kernel(
-    place, own_u, own_v, own_h, uv, h_first, h_second, u_out, v_out, h_out
+    place, own_u, own_v, own_h, west, east, uv, h_first, h_second, u_out, v_out, h_out
 ):
     def turned(block):
         return jnp.transpose(block, (1, 0, 2)).reshape(SOME * LEV, ROWS)
@@ -478,9 +455,19 @@
         u_out[...] = own_u[...]
         v_out[...] = own_v[...]
         h_out[...] = own_h[...]
-
-
-def unpack(place, own_u, own_v, own_h, uv, h_first, h_second):
+        end = row((COLS - 1) % SOME)
+        for f, out in enumerate((h_out, u_out, v_out)):
+
+            @pl.when(pl.program_id(0) == 0)
+            def _(f=f, out=out):
+                out[row(0), :] += west[f]
+
+            @pl.when(pl.program_id(0) == (COLS - 1) // SOME)
+            def _(f=f, out=out):
+                out[end, :] += east[f]
+
+
+def unpack(place, own_u, own_v, own_h, west, east, uv, h_first, h_second):
     def pick(polar):
         return lambda i, s: jnp.where(s[3] == polar, i, 0)
 
@@ -492,6 +479,7 @@
             num_scalar_prefetch=1,
             grid=(pl.cdiv(COLS, SOME),),
             in_specs=[pl.BlockSpec((SOME * LEV, ROWS), lambda i, s: (kept(i, s), 0))] * 3
+            + [pl.BlockSpec((3, LEV, ROWS), lambda i, s: (0, 0, 0))] * 2
             + [pl.BlockSpec((LEV, 2, SOME, ROWS), lambda i, s: (0, 0, used(i, s), 0))]
             + [half] * 2,
             out_specs=[pl.BlockSpec((SOME * LEV, ROWS), lambda i, s: (i, 0))] * 3,
@@ -501,7 +489,7 @@
         cost_estimate=pl.CostEstimate(
             flops=0, bytes_accessed=24 * COLS * LEV * ROWS, transcendentals=0
         ),
-    )(place, own_u, own_v, own_h, uv, h_first, h_second)
+    )(place, own_u, own_v, own_h, west, east, uv, h_first, h_second)
 
 
 def filter_kernel(place, x, matrix, columns, table, out, spectra, waves):
@@ -523,16 +511,27 @@
                 spectra[q, 0, rows, side * ROWS : (side + 1) * ROWS] = high
                 spectra[q, 1, rows, side * ROWS : (side + 1) * ROWS] = low
 
+    at = lax.broadcasted_iota(jnp.int32, (16, ROWS), 0)
+
+    def with_beside(blocks, spot, source, distance):
+        return [
+            block + jnp.where(at == spot, x[(p + distance) % 16, source : source + 1, :], 0.0)
+            for p, block in enumerate(blocks)
+        ]
+
+    gather(0, with_beside([x[p, 0:16, :] for p in range(16)], 0, COLS, -1))
+
     def fill(c, carry):
         start = pl.multiple_of(c * 16, 16)
         gather(start, [x[p, pl.ds(start, 16), :] for p in range(16)])
         return carry
 
     full = COLS // 16
-    lax.fori_loop(0, full, fill, 0, unroll=full)
+    lax.fori_loop(1, full, fill, 0, unroll=full - 1)
     empty = jnp.zeros((HALF - COLS, ROWS), jnp.float32)
     tail = pl.ds(16 * full, COLS % 16)
-    gather(16 * full, [jnp.concatenate([x[p, tail, :], empty], 0) for p in range(16)])
+    blocks = [jnp.concatenate([x[p, tail, :], empty], 0) for p in range(16)]
+    gather(16 * full, with_beside(blocks, COLS % 16 - 1, COLS + 1, 1))
 
     def product(high, low):
         found = jnp.dot(matrix[: 2 * HALF], high, preferred_element_type=jnp.float32)
@@ -589,7 +588,7 @@
             ],
         ),
         out_shape=jax.ShapeDtypeStruct(x.shape, jnp.float32),
-        compiler_params=pltpu.CompilerParams(vmem_limit_bytes=58 * 1024 * 1024),
+        compiler_params=pltpu.CompilerParams(vmem_limit_bytes=28 * 1024 * 1024),
         cost_estimate=pl.CostEstimate(
             flops=216 * HALF * HALF * ROWS * x.shape[1], bytes_accessed=3_500_000 * x.shape[1], transcendentals=0
         ),
@@ -632,12 +631,7 @@
     tables = jnp.asarray(latitude_tables())
     fields = [jnp.swapaxes(x, 0, 1) for x in (height, u_wind, v_wind)]
     flat = [x.reshape(COLS * LEV, ROWS) for x in fields]
-    east_to = [(i, (i + 1) % N_LON) for i in range(N_LON)]
-    initial, last = ends(flat)
-    west = lax.ppermute(last, "lon", east_to)
-    east = lax.ppermute(initial, "lon", [(j, i) for i, j in east_to])
     first, second = pack(place, *flat)
-    first, second = widen(place, first, second, west, east)
     swap = [(i, i ^ 1) for i in range(N_LAT)]
     first = lax.ppermute(first, "lat", swap)
     routes = [(lon, i, lon, i + 1) for lon in range(N_LON) for i in range(1, N_LAT - 1, 2)]
@@ -653,21 +647,20 @@
     def exchange(value):
         return lax.all_to_all(value, "lon", split_axis=0, concat_axis=0, tiled=True)
 
-    def keep(circles, h_first, h_second):
-        return polar_filter(place, circles, tables), unused(h_first), unused(h_second)
-
-    def help_out(circles, h_first, h_second):
+    def help_out(h_first, h_second):
         circles = exchange(jnp.concatenate([h_first, h_second], 0))
         lender = jnp.where(
             lax.axis_index("lon") < N_LON // 2, partner(band, BESIDE), partner(band, BEYOND)
         )
-        h = exchange(polar_filter(lender.reshape(1), circles[:, None], tables)[:, 0])
-        return unused(uv), h[: LEV // 2], h[LEV // 2 :]
-
-    inputs = (place, *flat, west, east, first, second, tables)
+        smooth = polar_filter(lender.reshape(1), circles[:, None], tables)[:, 0]
+        h = exchange(smooth)
+        return h[: LEV // 2], h[LEV // 2 :]
+
+    inputs = (place, *flat, first, second, tables)
     whole = jax.ShapeDtypeStruct((LEV, 2, TALL, ROWS), jnp.float32)
     half = jax.ShapeDtypeStruct((LEV // 2, TALL, ROWS), jnp.float32)
     own = jax.ShapeDtypeStruct((COLS * LEV, ROWS), jnp.float32)
+    ends = jax.ShapeDtypeStruct((3, LEV, ROWS), jnp.float32)
     uv, h_first, h_second = lax.cond(
         is_polar,
         lambda *inputs: tuple(stencil(True, *inputs)),
@@ -677,17 +670,30 @@
 
     h_first = lax.ppermute(h_first, AXES, lent(BESIDE, 0))
     h_second = lax.ppermute(h_second, AXES, lent(BEYOND, N_LON // 2))
-    circles, own_h, own_u, own_v = lax.cond(
+    circles, own_h, own_u, own_v, west, east = lax.cond(
         is_polar,
-        lambda uv, *inputs: (exchange(uv), unused(own), unused(own), unused(own)),
+        lambda uv, *inputs: (
+            polar_filter(place, exchange(uv), tables),
+            *(unused(like) for like in (own, own, own, ends, ends)),
+        ),
         lambda uv, *inputs: (unused(uv), *stencil(False, *inputs)),
         uv, *inputs,
     )
-    circles, h_first, h_second = lax.cond(is_polar, keep, help_out, circles, h_first, h_second)
+    h_first, h_second, circles = lax.optimization_barrier((h_first, h_second, circles))
+    h_first, h_second = lax.cond(
+        is_polar, lambda *parts: tuple(unused(part) for part in parts), help_out, h_first, h_second
+    )
     h_first = lax.ppermute(h_first, AXES, returned(BESIDE, 0))
     h_second = lax.ppermute(h_second, AXES, returned(BEYOND, N_LON // 2))
     uv = lax.cond(is_polar, exchange, unused, circles)
-    result = unpack(place, own_u, own_v, own_h, uv, h_first, h_second)
+    pairs = [
+        (lon * N_LAT + lat, (lon + 1) % N_LON * N_LAT + lat)
+        for lon in range(N_LON)
+        for lat in range(N_LAT // 4, N_LAT - N_LAT // 4)
+    ]
+    west = lax.ppermute(west, AXES, pairs)
+    east = lax.ppermute(east, AXES, [(j, i) for i, j in pairs])
+    result = unpack(place, own_u, own_v, own_h, west, east, uv, h_first, h_second)
     return tuple(jnp.swapaxes(x.reshape(COLS, LEV, ROWS), 0, 1) for x in result)
 
 

time: 141 us -> 133 us (0.943)
  Pallas kernels: 31.1 us -> 27.8 us
  waiting for transfers between devices: 44.9 us -> 42.1 us
    pallas_call x2 -> x0, Pallas kernels: 3.69 us -> none  [the longest x1 2.15 us: widen(): pl.pallas_call(widen_kernel, grid_spec=pltpu.PrefetchScalarGridSpec(num_s...]
    ppermute x1, waiting for transfers between devices: 2.27 us -> 0.01 us  [shards(): h_first = lax.ppermute(h_first, AXES, returned(BESIDE, 0))]
    cond x2 -> x0, local copies, waits for them, and re-layouts: 1.59 us -> none
  transfers between devices with their start and end apart: 9 -> 9, of which waited for: 5 -> 3; matrix products, arithmetic and copies ran while one was open for 0% -> 0% of each run, Pallas kernels for 3% -> 8%
where the time goes in v4:
time: 133 us; the launch traced here: 132 us
  waiting for transfers between devices  42.1 us (32%)
  blocking collectives  41.1 us (31%)
  Pallas kernels  27.8 us (21%)
  starting transfers between devices  19.4 us (15%)
    all_to_all x1, blocking collectives, exchange(): return lax.all_to_all(value, 'lon', split_axis=0, concat_axis=0, tiled=True)  41.1 us
    all_to_all x1, waiting for transfers between devices, exchange(): return lax.all_to_all(value, 'lon', split_axis=0, concat_axis=0, tiled=True)  40.1 us
    pallas_call x1, Pallas kernels, polar_filter(): pl.pallas_call(filter_kernel, grid_spec=pltpu.PrefetchScalarGridSpec(num_...  10.4 us
    pallas_call x1, Pallas kernels, stencil(): pl.pallas_call(functools.partial(stencil_kernel, polar), grid_spec=pltpu....  7.93 us
    all_to_all x1, starting transfers between devices, exchange(): return lax.all_to_all(value, 'lon', split_axis=0, concat_axis=0, tiled=True)  7.43 us
    pallas_call x1, Pallas kernels, unpack(): pl.pallas_call(unpack_kernel, grid_spec=pltpu.PrefetchScalarGridSpec(num_...  4.98 us
    pallas_call x1, Pallas kernels, pack(): pl.pallas_call(pack_kernel, grid_spec=pltpu.PrefetchScalarGridSpec(num_sc...  4.44 us
  transfers between devices with their start and end apart: 9, of which 3 were waited for; matrix products, arithmetic and copies ran while one was open for 0% of the time, Pallas kernels for 8%

profile of v4, /device:TPU:1, one launch (start us, length us, event | category | flops | bytes accessed | tf_op | source)
XLA Modules:
  0.0 132.2 jit_solution(6754493941918035551)
XLA Ops:
  0.7 0.1 stack.35.place
  0.7 4.4 %shard_map.85 = (f32[4,2,16,128]{3,2,1,0:T(8,128)}, f32[4,2,16,128]{3,2,1,0:T(8,128)}) custom-call(s32[5]{0:T(128)S(1)} %stack.35.place, f32[2880,128]{1,0:T(8,128)} %bitcast.28, f32[2880,128]{1,0:T(8,128)} %bitcast.31, f32[2880,128]{1,0:T(8,128)} %bitcast.34), custom_call_target="tpu_custom_call" | custom-call | bytes 4700000 | tf_op jit(solution)/shard_map/pallas_call | solution.py:223
  5.2 2.5 %collective-permute-start = (f32[4,2,16,128]{3,2,1,0:T(8,128)}, f32[4,2,16,128]{3,2,1,0:T(8,128)S(1)}, u32[]{:S(2)}, u32[]{:S(2)}) collective-permute-start(f32[4,2,16,128]{3,2,1,0:T(8,128)} %get-tuple-element.106), channel_id=1, source_target_pairs={{0,1},{1,0},{2,3},{3,2},{4,5},{5,4},{6,7},{7,6},{8,9},{9,8},{10,11... | collective-permute-start | bytes 196616 | tf_op jit(solution)/shard_map/ppermute | solution.py:636
  7.7 1.3 collective-permute-start.1
  8.9 0.6 collective-permute-done
  9.5 1.5 %collective-permute-done.1 = f32[4,2,16,128]{3,2,1,0:T(8,128)S(1)} collective-permute-done((f32[4,2,16,128]{3,2,1,0:T(8,128)}, f32[4,2,16,128]{3,2,1,0:T(8,128)S(1)}, u32[]{:S(2)}, u32[]{:S(2)}) %collective-permute-start.1) | collective-permute-done | bytes 65568 | tf_op jit(solution)/shard_map/ppermute | solution.py:642
  11.0 8.0 %conditional.4 = ((f32[16,2,184,128]{3,2,1,0:T(8,128)}, f32[8,184,128]{2,1,0:T(8,128)}, f32[8,184,128]{2,1,0:T(8,128)})) conditional(s32[]{:T(128)} %convert_element_type.2, () %tuple.39, (s32[5]{0:T(128)S(1)}, f32[2880,128]{1,0:T(8,128)S(1)}, f32[2880,128]{1,0:T(8,128)S(1)}, f32[2880,128]{1,0:T(8,128)}, f32[4,2,16,128]{3,2,1,0:T(8,128)S(1)}, ...), branch_computations={%region_0.1_spmd, %region_1.2_spmd} | conditional | flops 60000000 | bytes 9000008 | solution.py:664
  11.0 7.9 %branch_1_fun.9 = (f32[16,2,184,128]{3,2,1,0:T(8,128)}, f32[8,184,128]{2,1,0:T(8,128)}, f32[8,184,128]{2,1,0:T(8,128)}) custom-call(s32[5]{0:T(128)S(1)} %get-tuple-element.54.place, f32[2880,128]{1,0:T(8,128)S(1)} %get-tuple-element.55.h.h_west.h_east, f32[2880,128]{1,0:T(8,128)S(1)} %get-tuple-element.56.u.u_west.u_east, ...), custom_call_target="tpu_custom_call" | custom-call | flops 60000000 | bytes 9000000 | tf_op jit(solution)/shard_map/cond/branch_1_fun/pallas_call | solution.py:415
  19.0 2.2 %collective-permute-start.4 = (f32[8,184,128]{2,1,0:T(8,128)}, f32[8,184,128]{2,1,0:T(8,128)}, u32[]{:S(2)}, u32[]{:S(2)}) collective-permute-start(f32[8,184,128]{2,1,0:T(8,128)} %get-tuple-element.114), channel_id=1, source_target_pairs={{0,3},{1,2},{6,5},{7,4},{8,11},{9,10},{14,13},{15,12},{16,19},{17,... | collective-permute-start | bytes 2261000 | tf_op jit(solution)/shard_map/ppermute | solution.py:671
  21.1 2.2 %collective-permute-start.5 = (f32[8,184,128]{2,1,0:T(8,128)}, f32[8,184,128]{2,1,0:T(8,128)}, u32[]{:S(2)}, u32[]{:S(2)}) collective-permute-start(f32[8,184,128]{2,1,0:T(8,128)} %get-tuple-element.115), channel_id=1, source_target_pairs={{0,68},{1,69},{6,66},{7,67},{8,76},{9,77},{14,74},{15,75},{16,84},... | collective-permute-start | bytes 2261000 | tf_op jit(solution)/shard_map/ppermute | solution.py:672
  23.3 58.0 %conditional.5 = (f32[16,2,184,128]{3,2,1,0:T(8,128)}, f32[2880,128]{1,0:T(8,128)}, f32[2880,128]{1,0:T(8,128)}, f32[2880,128]{1,0:T(8,128)}, f32[3,16,128]{2,1,0:T(8,128)S(1)}, /*index=5*/f32[3,16,128]{2,1,0:T(8,128)S(1)}) conditional(s32[]{:T(128)} %convert_element_type.2, (s32[5]{0:T(128)S(1)}, f32[2880,128]{1,0:T(8,128)S(1)}, ...), branch_computations={%region_2.3_spmd, %region_3.4_spmd} | conditional | flops 2038431744 | bytes 16044048 | solution.py:673
  23.3 7.4 %all-to-all-start = ((f32[16,2,184,128]{3,2,1,0:T(8,128)}), f32[16,2,184,128]{3,2,1,0:T(8,128)S(1)}, u32[]{:S(2)}, u32[]{:S(2)}) async-start(f32[16,2,184,128]{3,2,1,0:T(8,128)} %get-tuple-element.74), calls=%async_computation | async-start | bytes 6029312 | tf_op jit(solution)/shard_map/cond/branch_1_fun/all_to_all | solution.py:648
  30.7 40.1 %all-to-all-done.x = f32[16,2,184,128]{3,2,1,0:T(8,128)S(1)} async-done(((f32[16,2,184,128]{3,2,1,0:T(8,128)}), f32[16,2,184,128]{3,2,1,0:T(8,128)S(1)}, u32[]{:S(2)}, u32[]{:S(2)}) %all-to-all-start) | async-done | bytes 3014688 | tf_op jit(solution)/shard_map/cond/branch_1_fun/all_to_all | solution.py:648
  70.9 10.4 %branch_1_fun.10 = f32[16,2,184,128]{3,2,1,0:T(8,128)} custom-call(s32[5]{0:T(128)S(1)} %get-tuple-element.73.place, f32[16,2,184,128]{3,2,1,0:T(8,128)S(1)} %all-to-all-done.x, bf16[768,192]{1,0:T(8,128)(2,1)} %get-tuple-element.75.matrix, f32[192,128]{1,0:T(8,128)S(1)} %get-tuple-element.76.columns, f32[8,8,128]{2,1,0:T(8,128)S(1)} %get-tuple-element.77.table), custom_call_target="tpu_custom_call" | custom-call | flops 2038431744 | bytes 7000000 | tf_op jit(solution)/shard_map/cond/branch_1_fun/pallas_call | solution.py:573
  81.3 0.2 conditional.7
  81.5 1.3 collective-permute-start.6
  82.8 1.3 collective-permute-start.7
  84.1 0.7 collective-permute-start.2
  84.8 0.7 collective-permute-start.3
  85.5 41.1 %conditional.6 = (f32[16,2,184,128]{3,2,1,0:T(8,128)S(1)}) conditional(s32[]{:T(128)} %convert_element_type.2, () %tuple.41, f32[16,2,184,128]{3,2,1,0:T(8,128)} %get-tuple-element.117), branch_computations={%region_4.5_spmd, %region_5.6_spmd} | conditional | bytes 6029320 | solution.py:688
  85.5 41.1 %all_to_all.16 = f32[16,2,184,128]{3,2,1,0:T(8,128)S(1)} all-to-all(f32[16,2,184,128]{3,2,1,0:T(8,128)} %param.5), channel_id=1, replica_groups=mesh['lon'=16,'lat'=8] {'lon'}, dimensions={0} | all-to-all | bytes 6029312 | tf_op jit(solution)/shard_map/cond/branch_1_fun/all_to_all | solution.py:648
  126.6 0.6 copy-done.3
  127.2 0.0 copy-done.4
  127.2 5.0 %shard_map.86 = (f32[2880,128]{1,0:T(8,128)}, f32[2880,128]{1,0:T(8,128)}, f32[2880,128]{1,0:T(8,128)}) custom-call(s32[5]{0:T(128)S(1)} %stack.35.place, f32[2880,128]{1,0:T(8,128)} %get-tuple-element.109.own_u, f32[2880,128]{1,0:T(8,128)} %get-tuple-element.110.own_v, f32[2880,128]{1,0:T(8,128)} %get-tuple-element.111.own_h, f32[3,16,128]{2,1,0:T(8,128)} %copy-done.3, ...), custom_call_target="tpu_custom_call" | custom-call | bytes 8847360 | tf_op jit(solution)/shard_map/pallas_call | solution.py:476
  (23 shorter events, 0.0 us)
Async XLA Ops:
  0.7 10.2 %copy-start = (f32[16,180,128]{2,0,1:T(8,128)S(1)}, f32[16,180,128]{2,0,1:T(8,128)}, u32[]{:S(2)}) copy-start(f32[16,180,128]{2,0,1:T(8,128)} %param.16) | copy-start | bytes 4423684
  0.7 10.2 %copy-start.1 = (f32[16,180,128]{2,0,1:T(8,128)S(1)}, f32[16,180,128]{2,0,1:T(8,128)}, u32[]{:S(2)}) copy-start(f32[16,180,128]{2,0,1:T(8,128)} %param.14) | copy-start | bytes 4423684
  0.7 10.2 %copy-start.2 = (f32[8,8,128]{2,1,0:T(8,128)S(1)}, f32[8,8,128]{2,1,0:T(8,128)}, u32[]{:S(2)}) copy-start(f32[8,8,128]{2,1,0:T(8,128)} %constant.52.clone) | copy-start | bytes 98308
  5.2 4.3 %collective-permute-start = (f32[4,2,16,128]{3,2,1,0:T(8,128)}, f32[4,2,16,128]{3,2,1,0:T(8,128)S(1)}, u32[]{:S(2)}, u32[]{:S(2)}) collective-permute-start(f32[4,2,16,128]{3,2,1,0:T(8,128)} %get-tuple-element.106), channel_id=1, source_target_pairs={{0,1},{1,0},{2,3},{3,2},{4,5},{5,4},{6,7},{7,6},{8,9},{9,8},{10,11... | collective-permute-start | bytes 196616 | tf_op jit(solution)/shard_map/ppermute | solution.py:636
  7.7 3.3 %collective-permute-start.1 = (f32[4,2,16,128]{3,2,1,0:T(8,128)}, f32[4,2,16,128]{3,2,1,0:T(8,128)S(1)}, u32[]{:S(2)}, u32[]{:S(2)}) collective-permute-start(f32[4,2,16,128]{3,2,1,0:T(8,128)} %get-tuple-element.107), channel_id=1, source_target_pairs={{1,2},{3,4},{5,6},{9,10},{11,12},{13,14},{17,18},{19,20},{21,22},{... | collective-permute-start | bytes 196616 | tf_op jit(solution)/shard_map/ppermute | solution.py:642
  11.0 12.3 %copy-start.6 = (f32[192,128]{1,0:T(8,128)S(1)}, f32[192,128]{1,0:T(8,128)}, u32[]{:S(2)}) copy-start(f32[192,128]{1,0:T(8,128)} %constant.54.clone) | copy-start | bytes 294916
  19.0 62.3 %collective-permute-start.4 = (f32[8,184,128]{2,1,0:T(8,128)}, f32[8,184,128]{2,1,0:T(8,128)}, u32[]{:S(2)}, u32[]{:S(2)}) collective-permute-start(f32[8,184,128]{2,1,0:T(8,128)} %get-tuple-element.114), channel_id=1, source_target_pairs={{0,3},{1,2},{6,5},{7,4},{8,11},{9,10},{14,13},{15,12},{16,19},{17,... | collective-permute-start | bytes 2261000 | tf_op jit(solution)/shard_map/ppermute | solution.py:671
  21.1 60.1 %collective-permute-start.5 = (f32[8,184,128]{2,1,0:T(8,128)}, f32[8,184,128]{2,1,0:T(8,128)}, u32[]{:S(2)}, u32[]{:S(2)}) collective-permute-start(f32[8,184,128]{2,1,0:T(8,128)} %get-tuple-element.115), channel_id=1, source_target_pairs={{0,68},{1,69},{6,66},{7,67},{8,76},{9,77},{14,74},{15,75},{16,84},... | collective-permute-start | bytes 2261000 | tf_op jit(solution)/shard_map/ppermute | solution.py:672
  23.3 47.6 %all-to-all-start = ((f32[16,2,184,128]{3,2,1,0:T(8,128)}), f32[16,2,184,128]{3,2,1,0:T(8,128)S(1)}, u32[]{:S(2)}, u32[]{:S(2)}) async-start(f32[16,2,184,128]{3,2,1,0:T(8,128)} %get-tuple-element.74), calls=%async_computation | async-start | bytes 6029312 | tf_op jit(solution)/shard_map/cond/branch_1_fun/all_to_all | solution.py:648
  81.5 45.1 %collective-permute-start.6 = (f32[8,184,128]{2,1,0:T(8,128)}, f32[8,184,128]{2,1,0:T(8,128)}, u32[]{:S(2)}, u32[]{:S(2)}) collective-permute-start(f32[8,184,128]{2,1,0:T(8,128)} %get-tuple-element.120), channel_id=1, source_target_pairs={{3,0},{2,1},{5,6},{4,7},{11,8},{10,9},{13,14},{12,15},{19,16},{18,... | collective-permute-start | bytes 2261000 | tf_op jit(solution)/shard_map/ppermute | solution.py:686
  82.8 43.8 %collective-permute-start.7 = (f32[8,184,128]{2,1,0:T(8,128)}, f32[8,184,128]{2,1,0:T(8,128)}, u32[]{:S(2)}, u32[]{:S(2)}) collective-permute-start(f32[8,184,128]{2,1,0:T(8,128)} %get-tuple-element.121), channel_id=1, source_target_pairs={{68,0},{69,1},{66,6},{67,7},{76,8},{77,9},{74,14},{75,15},{84,16},... | collective-permute-start | bytes 2261000 | tf_op jit(solution)/shard_map/ppermute | solution.py:687
  84.1 42.5 %collective-permute-start.2 = (f32[3,16,128]{2,1,0:T(8,128)S(1)}, f32[3,16,128]{2,1,0:T(8,128)S(1)}, u32[]{:S(2)}, u32[]{:S(2)}) collective-permute-start(f32[3,16,128]{2,1,0:T(8,128)S(1)} %get-tuple-element.112), channel_id=1, source_target_pairs={{2,10},{3,11},{4,12},{5,13},{10,18},{11,19},{12,20},{13,21},{18,26... | collective-permute-start | bytes 73736 | tf_op jit(solution)/shard_map/ppermute | solution.py:694
  84.8 41.8 %collective-permute-start.3 = (f32[3,16,128]{2,1,0:T(8,128)S(1)}, f32[3,16,128]{2,1,0:T(8,128)S(1)}, u32[]{:S(2)}, u32[]{:S(2)}) collective-permute-start(f32[3,16,128]{2,1,0:T(8,128)S(1)} %get-tuple-element.113), channel_id=1, source_target_pairs={{10,2},{11,3},{12,4},{13,5},{18,10},{19,11},{20,12},{21,13},{26,18... | collective-permute-start | bytes 73736 | tf_op jit(solution)/shard_map/ppermute | solution.py:695
  126.6 0.6 copy-start.3
  126.6 0.6 copy-start.4

commit v5 on v4

--- a/solution.py
+++ b/solution.py
@@ -615,11 +615,11 @@
     return sum(jnp.where(band == other, polar, 0) for polar, other in pairs).astype(jnp.int32)
 
 
-def unused(like):
+def unused(*likes):
     return pl.pallas_call(
-        lambda out: None,
-        out_specs=pl.BlockSpec(memory_space=pl.ANY),
-        out_shape=jax.ShapeDtypeStruct(like.shape, like.dtype),
+        lambda *outs: None,
+        out_specs=[pl.BlockSpec(memory_space=pl.ANY)] * len(likes),
+        out_shape=[jax.ShapeDtypeStruct(like.shape, like.dtype) for like in likes],
     )()
 
 
@@ -664,35 +664,39 @@
     uv, h_first, h_second = lax.cond(
         is_polar,
         lambda *inputs: tuple(stencil(True, *inputs)),
-        lambda *inputs: (unused(whole), unused(half), unused(half)),
+        lambda *inputs: tuple(unused(whole, half, half)),
         *inputs,
     )
 
     h_first = lax.ppermute(h_first, AXES, lent(BESIDE, 0))
     h_second = lax.ppermute(h_second, AXES, lent(BEYOND, N_LON // 2))
+    def beside(own_h, own_u, own_v, onward, back):
+        me = lax.axis_index("lon")
+        to = jnp.arange(N_LON).reshape(N_LON, 1, 1, 1)
+        sent = jnp.where(to == (me + 1) % N_LON, onward, 0.0)
+        got = exchange(jnp.where(to == (me - 1) % N_LON, back, sent))
+
+        def of(source):
+            return lax.dynamic_index_in_dim(got, source % N_LON, 0, keepdims=False)
+
+        return own_h, own_u, own_v, of(me - 1), of(me + 1)
+
     circles, own_h, own_u, own_v, west, east = lax.cond(
         is_polar,
         lambda uv, *inputs: (
             polar_filter(place, exchange(uv), tables),
-            *(unused(like) for like in (own, own, own, ends, ends)),
+            *unused(own, own, own, ends, ends),
         ),
-        lambda uv, *inputs: (unused(uv), *stencil(False, *inputs)),
+        lambda uv, *inputs: (*unused(uv), *beside(*stencil(False, *inputs))),
         uv, *inputs,
     )
     h_first, h_second, circles = lax.optimization_barrier((h_first, h_second, circles))
     h_first, h_second = lax.cond(
-        is_polar, lambda *parts: tuple(unused(part) for part in parts), help_out, h_first, h_second
+        is_polar, lambda *parts: tuple(unused(*parts)), help_out, h_first, h_second
     )
     h_first = lax.ppermute(h_first, AXES, returned(BESIDE, 0))
     h_second = lax.ppermute(h_second, AXES, returned(BEYOND, N_LON // 2))
-    uv = lax.cond(is_polar, exchange, unused, circles)
-    pairs = [
-        (lon * N_LAT + lat, (lon + 1) % N_LON * N_LAT + lat)
-        for lon in range(N_LON)
-        for lat in range(N_LAT // 4, N_LAT - N_LAT // 4)
-    ]
-    west = lax.ppermute(west, AXES, pairs)
-    east = lax.ppermute(east, AXES, [(j, i) for i, j in pairs])
+    uv = lax.cond(is_polar, exchange, lambda like: unused(like)[0], circles)
     result = unpack(place, own_u, own_v, own_h, west, east, uv, h_first, h_second)
     return tuple(jnp.swapaxes(x.reshape(COLS, LEV, ROWS), 0, 1) for x in result)
 

time: 133 us -> 131 us (0.985)
  transfers between devices with their start and end apart: 9 -> 7, of which waited for: 3 -> 3; matrix products, arithmetic and copies ran while one was open for 0% -> 0% of each run, Pallas kernels for 8% -> 8%
where the time goes in v5:
time: 131 us; the launch traced here: 130 us
  waiting for transfers between devices  42.2 us (32%)
  blocking collectives  41.1 us (31%)
  Pallas kernels  27.8 us (21%)
  starting transfers between devices  18.1 us (14%)
    all_to_all x1, blocking collectives, exchange(): return lax.all_to_all(value, 'lon', split_axis=0, concat_axis=0, tiled=True)  41.1 us
    all_to_all x1, waiting for transfers between devices, exchange(): return lax.all_to_all(value, 'lon', split_axis=0, concat_axis=0, tiled=True)  40.1 us
    pallas_call x1, Pallas kernels, polar_filter(): pl.pallas_call(filter_kernel, grid_spec=pltpu.PrefetchScalarGridSpec(num_...  10.5 us
    pallas_call x1, Pallas kernels, stencil(): pl.pallas_call(functools.partial(stencil_kernel, polar), grid_spec=pltpu....  7.95 us
    all_to_all x1, starting transfers between devices, exchange(): return lax.all_to_all(value, 'lon', split_axis=0, concat_axis=0, tiled=True)  7.43 us
    pallas_call x1, Pallas kernels, unpack(): pl.pallas_call(unpack_kernel, grid_spec=pltpu.PrefetchScalarGridSpec(num_...  4.97 us
    pallas_call x1, Pallas kernels, pack(): pl.pallas_call(pack_kernel, grid_spec=pltpu.PrefetchScalarGridSpec(num_sc...  4.44 us
  transfers between devices with their start and end apart: 7, of which 3 were waited for; matrix products, arithmetic and copies ran while one was open for 0% of the time, Pallas kernels for 8%

profile of v5, /device:TPU:1, one launch (start us, length us, event | category | flops | bytes accessed | tf_op | source)
XLA Modules:
  0.0 130.3 jit_solution(2319756556686812192)
XLA Ops:
  0.7 0.1 stack.35.place
  0.7 4.4 %shard_map.85 = (f32[4,2,16,128]{3,2,1,0:T(8,128)}, f32[4,2,16,128]{3,2,1,0:T(8,128)}) custom-call(s32[5]{0:T(128)S(1)} %stack.35.place, f32[2880,128]{1,0:T(8,128)} %bitcast.32, f32[2880,128]{1,0:T(8,128)} %bitcast.35, f32[2880,128]{1,0:T(8,128)} %bitcast.38), custom_call_target="tpu_custom_call" | custom-call | bytes 4700000 | tf_op jit(solution)/shard_map/pallas_call | solution.py:223
  5.2 2.5 %collective-permute-start = (f32[4,2,16,128]{3,2,1,0:T(8,128)}, f32[4,2,16,128]{3,2,1,0:T(8,128)S(1)}, u32[]{:S(2)}, u32[]{:S(2)}) collective-permute-start(f32[4,2,16,128]{3,2,1,0:T(8,128)} %get-tuple-element.111), channel_id=1, source_target_pairs={{0,1},{1,0},{2,3},{3,2},{4,5},{5,4},{6,7},{7,6},{8,9},{9,8},{10,11... | collective-permute-start | bytes 196616 | tf_op jit(solution)/shard_map/ppermute | solution.py:636
  7.7 1.3 collective-permute-start.1
  8.9 0.6 collective-permute-done
  9.5 1.5 %collective-permute-done.1 = f32[4,2,16,128]{3,2,1,0:T(8,128)S(1)} collective-permute-done((f32[4,2,16,128]{3,2,1,0:T(8,128)}, f32[4,2,16,128]{3,2,1,0:T(8,128)S(1)}, u32[]{:S(2)}, u32[]{:S(2)}) %collective-permute-start.1) | collective-permute-done | bytes 65568 | tf_op jit(solution)/shard_map/ppermute | solution.py:642
  11.0 0.0 copy-start.3
  11.0 8.0 %conditional.4 = ((f32[16,2,184,128]{3,2,1,0:T(8,128)}, f32[8,184,128]{2,1,0:T(8,128)}, f32[8,184,128]{2,1,0:T(8,128)})) conditional(s32[]{:T(128)} %convert_element_type.2, () %tuple.37, (s32[5]{0:T(128)S(1)}, f32[2880,128]{1,0:T(8,128)S(1)}, f32[2880,128]{1,0:T(8,128)S(1)}, f32[2880,128]{1,0:T(8,128)}, f32[4,2,16,128]{3,2,1,0:T(8,128)S(1)}, ...), branch_computations={%region_0.1_spmd, %region_1.2_spmd} | conditional | flops 60000000 | bytes 9000008 | solution.py:664
  11.0 8.0 %branch_1_fun.4 = (f32[16,2,184,128]{3,2,1,0:T(8,128)}, f32[8,184,128]{2,1,0:T(8,128)}, f32[8,184,128]{2,1,0:T(8,128)}) custom-call(s32[5]{0:T(128)S(1)} %get-tuple-element.54.place, f32[2880,128]{1,0:T(8,128)S(1)} %get-tuple-element.55.h.h_west.h_east, f32[2880,128]{1,0:T(8,128)S(1)} %get-tuple-element.56.u.u_west.u_east, ...), custom_call_target="tpu_custom_call" | custom-call | flops 60000000 | bytes 9000000 | tf_op jit(solution)/shard_map/cond/branch_1_fun/pallas_call | solution.py:415
  19.0 2.2 %collective-permute-start.2 = (f32[8,184,128]{2,1,0:T(8,128)}, f32[8,184,128]{2,1,0:T(8,128)}, u32[]{:S(2)}, u32[]{:S(2)}) collective-permute-start(f32[8,184,128]{2,1,0:T(8,128)} %get-tuple-element.119), channel_id=1, source_target_pairs={{0,3},{1,2},{6,5},{7,4},{8,11},{9,10},{14,13},{15,12},{16,19},{17,... | collective-permute-start | bytes 2261000 | tf_op jit(solution)/shard_map/ppermute | solution.py:671
  21.1 2.2 %collective-permute-start.3 = (f32[8,184,128]{2,1,0:T(8,128)}, f32[8,184,128]{2,1,0:T(8,128)}, u32[]{:S(2)}, u32[]{:S(2)}) collective-permute-start(f32[8,184,128]{2,1,0:T(8,128)} %get-tuple-element.120), channel_id=1, source_target_pairs={{0,68},{1,69},{6,66},{7,67},{8,76},{9,77},{14,74},{15,75},{16,84},... | collective-permute-start | bytes 2261000 | tf_op jit(solution)/shard_map/ppermute | solution.py:672
  23.3 58.0 %conditional.5 = (f32[16,2,184,128]{3,2,1,0:T(8,128)}, f32[2880,128]{1,0:T(8,128)}, f32[2880,128]{1,0:T(8,128)}, f32[2880,128]{1,0:T(8,128)}, f32[3,16,128]{2,1,0:T(8,128)S(1)}, /*index=5*/f32[3,16,128]{2,1,0:T(8,128)S(1)}) conditional(s32[]{:T(128)} %convert_element_type.2, (s32[5]{0:T(128)S(1)}, f32[2880,128]{1,0:T(8,128)S(1)}, ...), branch_computations={%region_2.3_spmd, %region_3.4_spmd} | conditional | flops 2038431744 | bytes 16044048 | solution.py:684
  23.3 7.4 %all-to-all-start = ((f32[16,2,184,128]{3,2,1,0:T(8,128)}), f32[16,2,184,128]{3,2,1,0:T(8,128)S(1)}, u32[]{:S(2)}, u32[]{:S(2)}) async-start(f32[16,2,184,128]{3,2,1,0:T(8,128)} %get-tuple-element.74), calls=%async_computation | async-start | bytes 6029312 | tf_op jit(solution)/shard_map/cond/branch_1_fun/all_to_all | solution.py:648
  30.8 40.1 %all-to-all-done.x = f32[16,2,184,128]{3,2,1,0:T(8,128)S(1)} async-done(((f32[16,2,184,128]{3,2,1,0:T(8,128)}), f32[16,2,184,128]{3,2,1,0:T(8,128)S(1)}, u32[]{:S(2)}, u32[]{:S(2)}) %all-to-all-start) | async-done | bytes 3014688 | tf_op jit(solution)/shard_map/cond/branch_1_fun/all_to_all | solution.py:648
  70.9 10.5 %branch_1_fun.5 = f32[16,2,184,128]{3,2,1,0:T(8,128)} custom-call(s32[5]{0:T(128)S(1)} %get-tuple-element.73.place, f32[16,2,184,128]{3,2,1,0:T(8,128)S(1)} %all-to-all-done.x, bf16[768,192]{1,0:T(8,128)(2,1)S(1)} %get-tuple-element.75.matrix, f32[192,128]{1,0:T(8,128)} %get-tuple-element.76.columns, f32[8,8,128]{2,1,0:T(8,128)S(1)} %get-tuple-element.77.table), custom_call_target="tpu_custom_call" | custom-call | flops 2038431744 | bytes 7000000 | tf_op jit(solution)/shard_map/cond/branch_1_fun/pallas_call | solution.py:573
  81.4 0.0 collective-permute-done.2
  81.4 0.0 collective-permute-done.3
  81.4 0.2 conditional.7
  81.6 1.3 collective-permute-start.4
  82.9 1.3 collective-permute-start.5
  84.2 41.1 %conditional.6 = (f32[16,2,184,128]{3,2,1,0:T(8,128)S(1)}) conditional(s32[]{:T(128)} %convert_element_type.2, () %tuple.39, f32[16,2,184,128]{3,2,1,0:T(8,128)} %get-tuple-element.122), branch_computations={%region_4.5_spmd, %region_5.6_spmd} | conditional | bytes 6029320 | solution.py:699
  84.2 41.1 %all_to_all.20 = f32[16,2,184,128]{3,2,1,0:T(8,128)S(1)} all-to-all(f32[16,2,184,128]{3,2,1,0:T(8,128)} %param.5), channel_id=1, replica_groups=mesh['lon'=16,'lat'=8] {'lon'}, dimensions={0} | all-to-all | bytes 6029312 | tf_op jit(solution)/shard_map/cond/branch_1_fun/all_to_all | solution.py:648
  125.3 0.0 collective-permute-done.4.h_first
  125.4 5.0 %shard_map.86 = (f32[2880,128]{1,0:T(8,128)}, f32[2880,128]{1,0:T(8,128)}, f32[2880,128]{1,0:T(8,128)}) custom-call(s32[5]{0:T(128)S(1)} %stack.35.place, f32[2880,128]{1,0:T(8,128)} %get-tuple-element.114.own_u, f32[2880,128]{1,0:T(8,128)} %get-tuple-element.115.own_v, f32[2880,128]{1,0:T(8,128)} %get-tuple-element.116.own_h, ...), custom_call_target="tpu_custom_call" | custom-call | bytes 8847360 | tf_op jit(solution)/shard_map/pallas_call | solution.py:476
  (10 shorter events, 0.0 us)
Async XLA Ops:
  0.7 10.2 %copy-start = (f32[16,180,128]{2,0,1:T(8,128)S(1)}, f32[16,180,128]{2,0,1:T(8,128)}, u32[]{:S(2)}) copy-start(f32[16,180,128]{2,0,1:T(8,128)} %param.16) | copy-start | bytes 4423684
  0.7 10.2 %copy-start.1 = (f32[16,180,128]{2,0,1:T(8,128)S(1)}, f32[16,180,128]{2,0,1:T(8,128)}, u32[]{:S(2)}) copy-start(f32[16,180,128]{2,0,1:T(8,128)} %param.14) | copy-start | bytes 4423684
  0.7 10.2 %copy-start.2 = (f32[8,8,128]{2,1,0:T(8,128)S(1)}, f32[8,8,128]{2,1,0:T(8,128)}, u32[]{:S(2)}) copy-start(f32[8,8,128]{2,1,0:T(8,128)} %constant.89.clone) | copy-start | bytes 98308
  5.2 4.3 %collective-permute-start = (f32[4,2,16,128]{3,2,1,0:T(8,128)}, f32[4,2,16,128]{3,2,1,0:T(8,128)S(1)}, u32[]{:S(2)}, u32[]{:S(2)}) collective-permute-start(f32[4,2,16,128]{3,2,1,0:T(8,128)} %get-tuple-element.111), channel_id=1, source_target_pairs={{0,1},{1,0},{2,3},{3,2},{4,5},{5,4},{6,7},{7,6},{8,9},{9,8},{10,11... | collective-permute-start | bytes 196616 | tf_op jit(solution)/shard_map/ppermute | solution.py:636
  7.7 3.3 %collective-permute-start.1 = (f32[4,2,16,128]{3,2,1,0:T(8,128)}, f32[4,2,16,128]{3,2,1,0:T(8,128)S(1)}, u32[]{:S(2)}, u32[]{:S(2)}) collective-permute-start(f32[4,2,16,128]{3,2,1,0:T(8,128)} %get-tuple-element.112), channel_id=1, source_target_pairs={{1,2},{3,4},{5,6},{9,10},{11,12},{13,14},{17,18},{19,20},{21,22},{... | collective-permute-start | bytes 196616 | tf_op jit(solution)/shard_map/ppermute | solution.py:642
  11.0 12.3 %copy-start.3 = (bf16[768,192]{1,0:T(8,128)(2,1)S(1)}, bf16[768,192]{1,0:T(8,128)(2,1)}, u32[]{:S(2)}) copy-start(bf16[768,192]{1,0:T(8,128)(2,1)} %constant.90.clone) | copy-start | bytes 884740
  19.0 62.4 %collective-permute-start.2 = (f32[8,184,128]{2,1,0:T(8,128)}, f32[8,184,128]{2,1,0:T(8,128)}, u32[]{:S(2)}, u32[]{:S(2)}) collective-permute-start(f32[8,184,128]{2,1,0:T(8,128)} %get-tuple-element.119), channel_id=1, source_target_pairs={{0,3},{1,2},{6,5},{7,4},{8,11},{9,10},{14,13},{15,12},{16,19},{17,... | collective-permute-start | bytes 2261000 | tf_op jit(solution)/shard_map/ppermute | solution.py:671
  21.1 60.2 %collective-permute-start.3 = (f32[8,184,128]{2,1,0:T(8,128)}, f32[8,184,128]{2,1,0:T(8,128)}, u32[]{:S(2)}, u32[]{:S(2)}) collective-permute-start(f32[8,184,128]{2,1,0:T(8,128)} %get-tuple-element.120), channel_id=1, source_target_pairs={{0,68},{1,69},{6,66},{7,67},{8,76},{9,77},{14,74},{15,75},{16,84},... | collective-permute-start | bytes 2261000 | tf_op jit(solution)/shard_map/ppermute | solution.py:672
  23.3 47.6 %all-to-all-start = ((f32[16,2,184,128]{3,2,1,0:T(8,128)}), f32[16,2,184,128]{3,2,1,0:T(8,128)S(1)}, u32[]{:S(2)}, u32[]{:S(2)}) async-start(f32[16,2,184,128]{3,2,1,0:T(8,128)} %get-tuple-element.74), calls=%async_computation | async-start | bytes 6029312 | tf_op jit(solution)/shard_map/cond/branch_1_fun/all_to_all | solution.py:648
  81.6 43.7 %collective-permute-start.4 = (f32[8,184,128]{2,1,0:T(8,128)}, f32[8,184,128]{2,1,0:T(8,128)}, u32[]{:S(2)}, u32[]{:S(2)}) collective-permute-start(f32[8,184,128]{2,1,0:T(8,128)} %get-tuple-element.125), channel_id=1, source_target_pairs={{3,0},{2,1},{5,6},{4,7},{11,8},{10,9},{13,14},{12,15},{19,16},{18,... | collective-permute-start | bytes 2261000 | tf_op jit(solution)/shard_map/ppermute | solution.py:697
  82.9 42.4 %collective-permute-start.5 = (f32[8,184,128]{2,1,0:T(8,128)}, f32[8,184,128]{2,1,0:T(8,128)}, u32[]{:S(2)}, u32[]{:S(2)}) collective-permute-start(f32[8,184,128]{2,1,0:T(8,128)} %get-tuple-element.126), channel_id=1, source_target_pairs={{68,0},{69,1},{66,6},{67,7},{76,8},{77,9},{74,14},{75,15},{84,16},... | collective-permute-start | bytes 2261000 | tf_op jit(solution)/shard_map/ppermute | solution.py:698

commit v6 on v5

--- a/solution.py
+++ b/solution.py
@@ -492,12 +492,31 @@
     )(place, own_u, own_v, own_h, west, east, uv, h_first, h_second)
 
 
-def filter_kernel(place, x, matrix, columns, table, out, spectra, waves):
+def filter_kernel(place, x, matrix, columns, table, result, out, spectra, waves, done):
+    at = lax.broadcasted_iota(jnp.int32, (16, ROWS), 0)
+    full = COLS // 16
+    empty = jnp.zeros((HALF - COLS, ROWS), jnp.float32)
+    ratio = table[0, 5:6, :]
+
     def column(rows, q):
         return columns[rows, q : q + 1]
 
-    def gather(start, blocks):
-        rows = pl.ds(pl.multiple_of(start, 16), 16)
+    def gather(item, c):
+        rows = slice(c * 16, c * 16 + 16)
+        if c < full:
+            blocks = [x[p, item, rows, :] for p in range(16)]
+        else:
+            tail = slice(c * 16, COLS)
+            blocks = [jnp.concatenate([x[p, item, tail, :], empty], 0) for p in range(16)]
+        for chunk, spot, source, distance in ((0, 0, COLS, -1), (full, COLS % 16 - 1, COLS + 1, 1)):
+            if c == chunk:
+                blocks = [
+                    block
+                    + jnp.where(
+                        at == spot, x[(p + distance) % 16, item, source : source + 1, :], 0.0
+                    )
+                    for p, block in enumerate(blocks)
+                ]
         pairs = forward16(blocks)
         parts = [(pairs[0][0], None)] + pairs[1:] + [(pairs[0][1], None)]
         for q, (re, im) in enumerate(parts):
@@ -508,30 +527,8 @@
                 re, im = (c * re, s * re) if im is None else times((re, im), c, s)
             for side, value in enumerate((re, im)):
                 high, low = split(value)
-                spectra[q, 0, rows, side * ROWS : (side + 1) * ROWS] = high
-                spectra[q, 1, rows, side * ROWS : (side + 1) * ROWS] = low
-
-    at = lax.broadcasted_iota(jnp.int32, (16, ROWS), 0)
-
-    def with_beside(blocks, spot, source, distance):
-        return [
-            block + jnp.where(at == spot, x[(p + distance) % 16, source : source + 1, :], 0.0)
-            for p, block in enumerate(blocks)
-        ]
-
-    gather(0, with_beside([x[p, 0:16, :] for p in range(16)], 0, COLS, -1))
-
-    def fill(c, carry):
-        start = pl.multiple_of(c * 16, 16)
-        gather(start, [x[p, pl.ds(start, 16), :] for p in range(16)])
-        return carry
-
-    full = COLS // 16
-    lax.fori_loop(1, full, fill, 0, unroll=full - 1)
-    empty = jnp.zeros((HALF - COLS, ROWS), jnp.float32)
-    tail = pl.ds(16 * full, COLS % 16)
-    blocks = [jnp.concatenate([x[p, tail, :], empty], 0) for p in range(16)]
-    gather(16 * full, with_beside(blocks, COLS % 16 - 1, COLS + 1, 1))
+                spectra[item, q, 0, rows, side * ROWS : (side + 1) * ROWS] = high
+                spectra[item, q, 1, rows, side * ROWS : (side + 1) * ROWS] = low
 
     def product(high, low):
         found = jnp.dot(matrix[: 2 * HALF], high, preferred_element_type=jnp.float32)
@@ -540,10 +537,9 @@
         cos, sin = found[:HALF], found[HALF:]
         return cos[:, :ROWS], cos[:, ROWS:], sin[:, :ROWS], sin[:, ROWS:]
 
-    ratio = table[0, 5:6, :]
-    rows = slice(0, HALF)
-    for q in range(9):
-        cos_re, cos_im, sin_re, sin_im = product(spectra[q, 0], spectra[q, 1])
+    def damp(item, q):
+        rows = slice(0, HALF)
+        cos_re, cos_im, sin_re, sin_im = product(spectra[item, q, 0], spectra[item, q, 1])
         damping = jnp.minimum(ratio * column(rows, 32 + q), scale_of(q))
         re, im = damping * (cos_re + sin_im), damping * (cos_im - sin_re)
         cos_re, cos_im, sin_re, sin_im = product(*split(jnp.concatenate([re, im], 1)))
@@ -552,45 +548,76 @@
             im = cos_im + sin_re
             c, s = column(rows, q), column(rows, 16 + q)
             if q < 8:
-                waves[q, 1] = c * im - s * re
+                waves[item, q, 1] = c * im - s * re
             re = c * re + s * im
-        waves[q, 0] = re
-
-    def give(c, carry):
-        rows = pl.ds(pl.multiple_of(c * 8, 8), 8)
-        pairs = [(waves[0, 0, rows, :], waves[8, 0, rows, :])]
-        pairs += [(waves[q, 0, rows, :], waves[q, 1, rows, :]) for q in range(1, 8)]
+        waves[item, q, 0] = re
+
+    def give(item, c):
+        rows = slice(c * 8, c * 8 + 8)
+        pairs = [(waves[item, 0, 0, rows, :], waves[item, 8, 0, rows, :])]
+        pairs += [(waves[item, q, 0, rows, :], waves[item, q, 1, rows, :]) for q in range(1, 8)]
         for p, value in enumerate(inverse16(pairs)):
-            out[p, rows, :] = value
-        return carry
-
-    lax.fori_loop(0, TALL // 8, give, 0, unroll=TALL // 8)
+            out[p, item, rows, :] = value
+
+    items = x.shape[1]
+    gathers, gives = HALF // 16, TALL // 8
+    copies = []
+
+    def send(item, first, count):
+        rows = pl.ds(first, count)
+        copies.append(
+            pltpu.make_async_copy(
+                out.at[:, item, rows, :], result.at[:, item, rows, :], done.at[len(copies)]
+            )
+        )
+        copies[-1].start()
+
+    for c in range(gathers):
+        gather(0, c)
+    for item in range(items):
+        for q in range(9):
+            damp(item, q)
+            if item + 1 < items:
+                for c in range(q * gathers // 9, (q + 1) * gathers // 9):
+                    gather(item + 1, c)
+            if item:
+                for c in range(q * gives // 9, (q + 1) * gives // 9):
+                    give(item - 1, c)
+        if item:
+            send(item - 1, 0, TALL)
+    for c in range(gives):
+        give(items - 1, c)
+        if c == 11:
+            send(items - 1, 0, 96)
+    send(items - 1, 96, TALL - 96)
+    for copy in copies:
+        copy.wait()
 
 
 def polar_filter(place, x, tables):
     matrix, columns = fourier_tables()
-    field = pl.BlockSpec((LEV, None, TALL, ROWS), lambda i, s: (0, i, 0, 0))
+    items = x.shape[1]
+    vmem = pl.BlockSpec(memory_space=pltpu.VMEM)
     return pl.pallas_call(
         filter_kernel,
         grid_spec=pltpu.PrefetchScalarGridSpec(
             num_scalar_prefetch=1,
-            grid=(x.shape[1],),
-            in_specs=[
-                field,
-                pl.BlockSpec(matrix.shape, lambda i, s: (0, 0)),
-                pl.BlockSpec(columns.shape, lambda i, s: (0, 0)),
-                pl.BlockSpec((1, 8, ROWS), lambda i, s: (s[0], 0, 0)),
-            ],
-            out_specs=field,
+            grid=(1,),
+            in_specs=[vmem] * 3 + [pl.BlockSpec((1, 8, ROWS), lambda i, s: (s[0], 0, 0))],
+            out_specs=pl.BlockSpec(memory_space=pl.ANY),
             scratch_shapes=[
-                pltpu.VMEM((9, 2, HALF, 2 * ROWS), jnp.bfloat16),
-                pltpu.VMEM((9, 2, HALF, ROWS), jnp.float32),
+                pltpu.VMEM(x.shape, jnp.float32),
+                pltpu.VMEM((items, 9, 2, HALF, 2 * ROWS), jnp.bfloat16),
+                pltpu.VMEM((items, 9, 2, HALF, ROWS), jnp.float32),
+                pltpu.SemaphoreType.DMA((items + 1,)),
             ],
         ),
         out_shape=jax.ShapeDtypeStruct(x.shape, jnp.float32),
         compiler_params=pltpu.CompilerParams(vmem_limit_bytes=28 * 1024 * 1024),
         cost_estimate=pl.CostEstimate(
-            flops=216 * HALF * HALF * ROWS * x.shape[1], bytes_accessed=3_500_000 * x.shape[1], transcendentals=0
+            flops=216 * HALF * HALF * ROWS * items,
+            bytes_accessed=3_500_000 * items,
+            transcendentals=0,
         ),
     )(place, x, jnp.asarray(matrix), jnp.asarray(columns), tables)
 

time: 131 us -> 130 us (level)
  no operation moved by 1% of the time
where the time goes in v6:
time: 130 us
  waiting for transfers between devices  42.2 us (32%)
  blocking collectives  41.1 us (32%)
  Pallas kernels  27.4 us (21%)
  starting transfers between devices  18.1 us (14%)
    all_to_all x1, blocking collectives, exchange(): return lax.all_to_all(value, 'lon', split_axis=0, concat_axis=0, tiled=True)  41.1 us
    all_to_all x1, waiting for transfers between devices, exchange(): return lax.all_to_all(value, 'lon', split_axis=0, concat_axis=0, tiled=True)  40.1 us
    pallas_call x1, Pallas kernels, polar_filter(): pl.pallas_call(filter_kernel, grid_spec=pltpu.PrefetchScalarGridSpec(num_...  9.99 us
    pallas_call x1, Pallas kernels, stencil(): pl.pallas_call(functools.partial(stencil_kernel, polar), grid_spec=pltpu....  7.95 us
    all_to_all x1, starting transfers between devices, exchange(): return lax.all_to_all(value, 'lon', split_axis=0, concat_axis=0, tiled=True)  7.43 us
    pallas_call x1, Pallas kernels, unpack(): pl.pallas_call(unpack_kernel, grid_spec=pltpu.PrefetchScalarGridSpec(num_...  4.97 us
    pallas_call x1, Pallas kernels, pack(): pl.pallas_call(pack_kernel, grid_spec=pltpu.PrefetchScalarGridSpec(num_sc...  4.44 us
  transfers between devices with their start and end apart: 7, of which 3 were waited for; matrix products, arithmetic and copies ran while one was open for 0% of the time, Pallas kernels for 8%

profile of v6, /device:TPU:1, one launch (start us, length us, event | category | flops | bytes accessed | tf_op | source)
XLA Modules:
  0.0 129.9 jit_solution(10725926164070142498)
XLA Ops:
  0.7 0.1 stack.35.place
  0.7 4.4 %shard_map.85 = (f32[4,2,16,128]{3,2,1,0:T(8,128)}, f32[4,2,16,128]{3,2,1,0:T(8,128)}) custom-call(s32[5]{0:T(128)S(1)} %stack.35.place, f32[2880,128]{1,0:T(8,128)} %bitcast.32, f32[2880,128]{1,0:T(8,128)} %bitcast.35, f32[2880,128]{1,0:T(8,128)} %bitcast.38), custom_call_target="tpu_custom_call" | custom-call | bytes 4700000 | tf_op jit(solution)/shard_map/pallas_call | solution.py:223
  5.2 2.5 %collective-permute-start = (f32[4,2,16,128]{3,2,1,0:T(8,128)}, f32[4,2,16,128]{3,2,1,0:T(8,128)S(1)}, u32[]{:S(2)}, u32[]{:S(2)}) collective-permute-start(f32[4,2,16,128]{3,2,1,0:T(8,128)} %get-tuple-element.111), channel_id=1, source_target_pairs={{0,1},{1,0},{2,3},{3,2},{4,5},{5,4},{6,7},{7,6},{8,9},{9,8},{10,11... | collective-permute-start | bytes 196616 | tf_op jit(solution)/shard_map/ppermute | solution.py:663
  7.7 1.3 collective-permute-start.1
  8.9 0.6 collective-permute-done
  9.5 1.5 %collective-permute-done.1 = f32[4,2,16,128]{3,2,1,0:T(8,128)S(1)} collective-permute-done((f32[4,2,16,128]{3,2,1,0:T(8,128)}, f32[4,2,16,128]{3,2,1,0:T(8,128)S(1)}, u32[]{:S(2)}, u32[]{:S(2)}) %collective-permute-start.1) | collective-permute-done | bytes 65568 | tf_op jit(solution)/shard_map/ppermute | solution.py:669
  11.0 0.0 copy-start.3
  11.0 8.0 %conditional.4 = ((f32[16,2,184,128]{3,2,1,0:T(8,128)}, f32[8,184,128]{2,1,0:T(8,128)}, f32[8,184,128]{2,1,0:T(8,128)})) conditional(s32[]{:T(128)} %convert_element_type.2, () %tuple.37, (s32[5]{0:T(128)S(1)}, f32[2880,128]{1,0:T(8,128)S(1)}, f32[2880,128]{1,0:T(8,128)S(1)}, f32[2880,128]{1,0:T(8,128)}, f32[4,2,16,128]{3,2,1,0:T(8,128)S(1)}, ...), branch_computations={%region_0.1_spmd, %region_1.2_spmd} | conditional | flops 60000000 | bytes 9000008 | solution.py:691
  11.0 8.0 %branch_1_fun.4 = (f32[16,2,184,128]{3,2,1,0:T(8,128)}, f32[8,184,128]{2,1,0:T(8,128)}, f32[8,184,128]{2,1,0:T(8,128)}) custom-call(s32[5]{0:T(128)S(1)} %get-tuple-element.54.place, f32[2880,128]{1,0:T(8,128)S(1)} %get-tuple-element.55.h.h_west.h_east, f32[2880,128]{1,0:T(8,128)S(1)} %get-tuple-element.56.u.u_west.u_east, ...), custom_call_target="tpu_custom_call" | custom-call | flops 60000000 | bytes 9000000 | tf_op jit(solution)/shard_map/cond/branch_1_fun/pallas_call | solution.py:415
  19.0 2.2 %collective-permute-start.2 = (f32[8,184,128]{2,1,0:T(8,128)}, f32[8,184,128]{2,1,0:T(8,128)}, u32[]{:S(2)}, u32[]{:S(2)}) collective-permute-start(f32[8,184,128]{2,1,0:T(8,128)} %get-tuple-element.119), channel_id=1, source_target_pairs={{0,3},{1,2},{6,5},{7,4},{8,11},{9,10},{14,13},{15,12},{16,19},{17,... | collective-permute-start | bytes 2261000 | tf_op jit(solution)/shard_map/ppermute | solution.py:698
  21.1 2.2 %collective-permute-start.3 = (f32[8,184,128]{2,1,0:T(8,128)}, f32[8,184,128]{2,1,0:T(8,128)}, u32[]{:S(2)}, u32[]{:S(2)}) collective-permute-start(f32[8,184,128]{2,1,0:T(8,128)} %get-tuple-element.120), channel_id=1, source_target_pairs={{0,68},{1,69},{6,66},{7,67},{8,76},{9,77},{14,74},{15,75},{16,84},... | collective-permute-start | bytes 2261000 | tf_op jit(solution)/shard_map/ppermute | solution.py:699
  23.3 57.8 %conditional.5 = (f32[16,2,184,128]{3,2,1,0:T(8,128)}, f32[2880,128]{1,0:T(8,128)}, f32[2880,128]{1,0:T(8,128)}, f32[2880,128]{1,0:T(8,128)}, f32[3,16,128]{2,1,0:T(8,128)S(1)}, /*index=5*/f32[3,16,128]{2,1,0:T(8,128)S(1)}) conditional(s32[]{:T(128)} %convert_element_type.2, (s32[5]{0:T(128)S(1)}, f32[2880,128]{1,0:T(8,128)S(1)}, ...), branch_computations={%region_2.3_spmd, %region_3.4_spmd} | conditional | flops 2038431744 | bytes 16044048 | solution.py:711
  23.3 7.4 %all-to-all-start = ((f32[16,2,184,128]{3,2,1,0:T(8,128)}), f32[16,2,184,128]{3,2,1,0:T(8,128)S(1)}, u32[]{:S(2)}, u32[]{:S(2)}) async-start(f32[16,2,184,128]{3,2,1,0:T(8,128)} %get-tuple-element.74), calls=%async_computation | async-start | bytes 6029312 | tf_op jit(solution)/shard_map/cond/branch_1_fun/all_to_all | solution.py:675
  30.8 40.1 %all-to-all-done.x = f32[16,2,184,128]{3,2,1,0:T(8,128)S(1)} async-done(((f32[16,2,184,128]{3,2,1,0:T(8,128)}), f32[16,2,184,128]{3,2,1,0:T(8,128)S(1)}, u32[]{:S(2)}, u32[]{:S(2)}) %all-to-all-start) | async-done | bytes 3014688 | tf_op jit(solution)/shard_map/cond/branch_1_fun/all_to_all | solution.py:675
  70.9 10.0 %branch_1_fun.5 = f32[16,2,184,128]{3,2,1,0:T(8,128)} custom-call(s32[5]{0:T(128)S(1)} %get-tuple-element.73.place, f32[16,2,184,128]{3,2,1,0:T(8,128)S(1)} %all-to-all-done.x, bf16[768,192]{1,0:T(8,128)(2,1)S(1)} %get-tuple-element.75.matrix, f32[192,128]{1,0:T(8,128)} %get-tuple-element.76.columns, f32[8,8,128]{2,1,0:T(8,128)S(1)} %get-tuple-element.77.table), custom_call_target="tpu_custom_call" | custom-call | flops 2038431744 | bytes 7000000 | tf_op jit(solution)/shard_map/cond/branch_1_fun/pallas_call | solution.py:601
  81.1 0.0 collective-permute-done.2
  81.1 0.0 collective-permute-done.3
  81.2 1.3 collective-permute-start.4
  82.5 1.3 collective-permute-start.5
  83.8 41.1 %conditional.6 = (f32[16,2,184,128]{3,2,1,0:T(8,128)S(1)}) conditional(s32[]{:T(128)} %convert_element_type.2, () %tuple.39, f32[16,2,184,128]{3,2,1,0:T(8,128)} %get-tuple-element.122), branch_computations={%region_4.5_spmd, %region_5.6_spmd} | conditional | bytes 6029320 | solution.py:726
  83.8 41.1 %all_to_all.20 = f32[16,2,184,128]{3,2,1,0:T(8,128)S(1)} all-to-all(f32[16,2,184,128]{3,2,1,0:T(8,128)} %param.5), channel_id=1, replica_groups=mesh['lon'=16,'lat'=8] {'lon'}, dimensions={0} | all-to-all | bytes 6029312 | tf_op jit(solution)/shard_map/cond/branch_1_fun/all_to_all | solution.py:675
  124.9 0.0 collective-permute-done.4.h_first
  124.9 0.0 collective-permute-done.5.h_second
  124.9 5.0 %shard_map.86 = (f32[2880,128]{1,0:T(8,128)}, f32[2880,128]{1,0:T(8,128)}, f32[2880,128]{1,0:T(8,128)}) custom-call(s32[5]{0:T(128)S(1)} %stack.35.place, f32[2880,128]{1,0:T(8,128)} %get-tuple-element.114.own_u, f32[2880,128]{1,0:T(8,128)} %get-tuple-element.115.own_v, f32[2880,128]{1,0:T(8,128)} %get-tuple-element.116.own_h, ...), custom_call_target="tpu_custom_call" | custom-call | bytes 8847360 | tf_op jit(solution)/shard_map/pallas_call | solution.py:476
  (10 shorter events, 0.0 us)
Async XLA Ops:
  0.7 10.2 %copy-start = (f32[16,180,128]{2,0,1:T(8,128)S(1)}, f32[16,180,128]{2,0,1:T(8,128)}, u32[]{:S(2)}) copy-start(f32[16,180,128]{2,0,1:T(8,128)} %param.16) | copy-start | bytes 4423684
  0.7 10.2 %copy-start.1 = (f32[16,180,128]{2,0,1:T(8,128)S(1)}, f32[16,180,128]{2,0,1:T(8,128)}, u32[]{:S(2)}) copy-start(f32[16,180,128]{2,0,1:T(8,128)} %param.14) | copy-start | bytes 4423684
  0.7 10.2 %copy-start.2 = (f32[8,8,128]{2,1,0:T(8,128)S(1)}, f32[8,8,128]{2,1,0:T(8,128)}, u32[]{:S(2)}) copy-start(f32[8,8,128]{2,1,0:T(8,128)} %constant.89.clone) | copy-start | bytes 98308
  5.2 4.3 %collective-permute-start = (f32[4,2,16,128]{3,2,1,0:T(8,128)}, f32[4,2,16,128]{3,2,1,0:T(8,128)S(1)}, u32[]{:S(2)}, u32[]{:S(2)}) collective-permute-start(f32[4,2,16,128]{3,2,1,0:T(8,128)} %get-tuple-element.111), channel_id=1, source_target_pairs={{0,1},{1,0},{2,3},{3,2},{4,5},{5,4},{6,7},{7,6},{8,9},{9,8},{10,11... | collective-permute-start | bytes 196616 | tf_op jit(solution)/shard_map/ppermute | solution.py:663
  7.7 3.3 %collective-permute-start.1 = (f32[4,2,16,128]{3,2,1,0:T(8,128)}, f32[4,2,16,128]{3,2,1,0:T(8,128)S(1)}, u32[]{:S(2)}, u32[]{:S(2)}) collective-permute-start(f32[4,2,16,128]{3,2,1,0:T(8,128)} %get-tuple-element.112), channel_id=1, source_target_pairs={{1,2},{3,4},{5,6},{9,10},{11,12},{13,14},{17,18},{19,20},{21,22},{... | collective-permute-start | bytes 196616 | tf_op jit(solution)/shard_map/ppermute | solution.py:669
  11.0 12.3 %copy-start.3 = (bf16[768,192]{1,0:T(8,128)(2,1)S(1)}, bf16[768,192]{1,0:T(8,128)(2,1)}, u32[]{:S(2)}) copy-start(bf16[768,192]{1,0:T(8,128)(2,1)} %constant.90.clone) | copy-start | bytes 884740
  19.0 62.1 %collective-permute-start.2 = (f32[8,184,128]{2,1,0:T(8,128)}, f32[8,184,128]{2,1,0:T(8,128)}, u32[]{:S(2)}, u32[]{:S(2)}) collective-permute-start(f32[8,184,128]{2,1,0:T(8,128)} %get-tuple-element.119), channel_id=1, source_target_pairs={{0,3},{1,2},{6,5},{7,4},{8,11},{9,10},{14,13},{15,12},{16,19},{17,... | collective-permute-start | bytes 2261000 | tf_op jit(solution)/shard_map/ppermute | solution.py:698
  21.1 60.0 %collective-permute-start.3 = (f32[8,184,128]{2,1,0:T(8,128)}, f32[8,184,128]{2,1,0:T(8,128)}, u32[]{:S(2)}, u32[]{:S(2)}) collective-permute-start(f32[8,184,128]{2,1,0:T(8,128)} %get-tuple-element.120), channel_id=1, source_target_pairs={{0,68},{1,69},{6,66},{7,67},{8,76},{9,77},{14,74},{15,75},{16,84},... | collective-permute-start | bytes 2261000 | tf_op jit(solution)/shard_map/ppermute | solution.py:699
  23.3 47.6 %all-to-all-start = ((f32[16,2,184,128]{3,2,1,0:T(8,128)}), f32[16,2,184,128]{3,2,1,0:T(8,128)S(1)}, u32[]{:S(2)}, u32[]{:S(2)}) async-start(f32[16,2,184,128]{3,2,1,0:T(8,128)} %get-tuple-element.74), calls=%async_computation | async-start | bytes 6029312 | tf_op jit(solution)/shard_map/cond/branch_1_fun/all_to_all | solution.py:675
  81.2 43.7 %collective-permute-start.4 = (f32[8,184,128]{2,1,0:T(8,128)}, f32[8,184,128]{2,1,0:T(8,128)}, u32[]{:S(2)}, u32[]{:S(2)}) collective-permute-start(f32[8,184,128]{2,1,0:T(8,128)} %get-tuple-element.125), channel_id=1, source_target_pairs={{3,0},{2,1},{5,6},{4,7},{11,8},{10,9},{13,14},{12,15},{19,16},{18,... | collective-permute-start | bytes 2261000 | tf_op jit(solution)/shard_map/ppermute | solution.py:724
  82.5 42.4 %collective-permute-start.5 = (f32[8,184,128]{2,1,0:T(8,128)}, f32[8,184,128]{2,1,0:T(8,128)}, u32[]{:S(2)}, u32[]{:S(2)}) collective-permute-start(f32[8,184,128]{2,1,0:T(8,128)} %get-tuple-element.126), channel_id=1, source_target_pairs={{68,0},{69,1},{66,6},{67,7},{76,8},{77,9},{74,14},{75,15},{84,16},... | collective-permute-start | bytes 2261000 | tf_op jit(solution)/shard_map/ppermute | solution.py:725
